TPU v7x, 512 devices: a whole 4x4x16 slice. The times are simulated.
512 devices in a mesh: pipe: 16 (over x_lo, y, core), expert: 32 (over z, x_hi).
Axes of the slice: x: 4 (x_hi: 2, x_lo: 2; x = x_hi * 2 + x_lo), y: 4, z: 16, core: 2. Of those that a mesh axis runs over, the one named last changes fastest.
Arguments:
- fwd_tokens: bfloat16 [16, 256, 3584], P('pipe', 'expert'), may hold values from -6 to 6
- saved_tokens: bfloat16 [2, 16, 256, 3584], P(None, 'pipe', 'expert'), may hold values from -6 to 6
- cotangent: bfloat16 [16, 256, 3584], P('pipe', 'expert'), may hold values from -6 to 6
- fwd_routes: int32 [2, 16, 256, 2], P(None, 'pipe', 'expert'), may hold values from 0 to 3, all different within a row; in each aligned block of 8 rows (0 to 7, 8 to 15, ..., all dimensions but the last counted through in order) at most 5 rows name the same one
- bwd_routes: int32 [2, 16, 256, 2], P(None, 'pipe', 'expert'), may hold values from 0 to 3, all different within a row; in each aligned block of 8 rows (0 to 7, 8 to 15, ..., all dimensions but the last counted through in order) at most 5 rows name the same one
- norm_gain: float32 [16, 3584], P('pipe'), may hold values from 0.1 to 1.9
- router: bfloat16 [16, 3584, 4], P('pipe'), may hold values from -0.09375 to 0.09375
- w_gate: bfloat16 [16, 3584, 4096], P('pipe', None, 'expert'), may hold values from -0.09375 to 0.09375
- w_up: bfloat16 [16, 3584, 4096], P('pipe', None, 'expert'), may hold values from -0.09375 to 0.09375
- w_down: bfloat16 [16, 4096, 3584], P('pipe', 'expert'), may hold values from -0.1875 to 0.1875
Outputs:
- fwd_out: bfloat16 [16, 256, 3584], P('pipe', 'expert')
- bwd_out: bfloat16 [16, 256, 3584], P('pipe', 'expert')
Inputs may be any that keep to these rules, and one draw needn't show every extreme that they name: `fwd_routes`: each row names 2 different experts. In every aligned block of 8 rows (one device's tokens of one step and section) no expert is named more than 5 times; in at least one block some expert is named exactly 5 times. `bwd_routes`: each row names 2 different experts. In every aligned block of 8 rows (one device's tokens of one step and section) no expert is named more than 5 times; in at least one block some expert is named exactly 5 times.
All inputs are finite; a program needn't handle non-finite values.
Results may differ from a plain program's by a relative error of at most 0.018.
Values may be sent and summed in bfloat16 or wider, within the bound.
No kernel may reach another device: no remote copies, remote signals or barrier semaphores. Data moves between devices by JAX's collectives and lax.ppermute only.
A program may use at most 64 MiB of HBM per device.

v0:
```python
import jax
import jax.numpy as jnp
from jax import lax
from jax.sharding import PartitionSpec as P


def from_behind(block, axis, distance):
    devices = range(lax.axis_size(axis))
    route = [((i - distance) % len(devices), i) for i in devices]
    return lax.ppermute(block, axis, route)


def norm_rows(values, norm_gain):
    wide = values.astype(jnp.float32)
    scale = lax.rsqrt(jnp.mean(wide * wide, axis=-1, keepdims=True) + 1e-06)
    return wide * scale * norm_gain


def gate_values(normed, router_w, routes, expert_count):
    logits = jnp.dot(normed, router_w, preferred_element_type=jnp.float32)
    sig_all = jax.nn.sigmoid(logits)
    route_pick = (routes[..., None] == jnp.arange(expert_count, dtype=jnp.int32)).astype(
        jnp.float32
    )
    chosen = jnp.sum(route_pick * sig_all[:, None, :], axis=-1)
    gate_total = jnp.sum(chosen, axis=-1, keepdims=True)
    gate_share = chosen / gate_total
    return (chosen, gate_total, gate_share, route_pick)


def slot_matrix(routes, expert_count, cap_rows):
    flat_routes = routes.reshape(-1)
    hit_table = (flat_routes[:, None] == jnp.arange(expert_count, dtype=jnp.int32)).astype(
        jnp.int32
    )
    before = jnp.cumsum(hit_table, axis=0) - hit_table
    slot_index = jnp.sum(before * hit_table, axis=1)
    position = flat_routes * cap_rows + slot_index
    placement = (position[:, None] == jnp.arange(expert_count * cap_rows, dtype=jnp.int32)).astype(
        jnp.float32
    )
    return placement.reshape(routes.shape[0], routes.shape[1], expert_count * cap_rows)


def expert_forward(row_block, gate_w, up_w, down_w):
    gate_pre = jnp.dot(row_block, gate_w, preferred_element_type=jnp.float32)
    up_pre = jnp.dot(row_block, up_w, preferred_element_type=jnp.float32)
    hidden = (jax.nn.silu(gate_pre) * up_pre).astype(jnp.bfloat16)
    return jnp.dot(hidden, down_w, preferred_element_type=jnp.float32).astype(jnp.bfloat16)


def expert_backward(row_block, cotan_rows, gate_w, up_w, down_w):
    gate_pre = jnp.dot(row_block, gate_w, preferred_element_type=jnp.float32)
    up_pre = jnp.dot(row_block, up_w, preferred_element_type=jnp.float32)
    gate_sig = jax.nn.sigmoid(gate_pre)
    gate_act = gate_pre * gate_sig
    hidden = (gate_act * up_pre).astype(jnp.bfloat16)
    expert_out = jnp.dot(hidden, down_w, preferred_element_type=jnp.float32).astype(jnp.bfloat16)
    hidden_grad = jnp.einsum("rd,fd->rf", cotan_rows, down_w, preferred_element_type=jnp.float32)
    gate_grad = (hidden_grad * up_pre * gate_sig * (1.0 + gate_pre * (1.0 - gate_sig))).astype(
        jnp.bfloat16
    )
    up_grad = (hidden_grad * gate_act).astype(jnp.bfloat16)
    row_grad = jnp.einsum("rf,df->rd", gate_grad, gate_w, preferred_element_type=jnp.float32)
    row_grad = row_grad + jnp.einsum("rf,df->rd", up_grad, up_w, preferred_element_type=jnp.float32)
    return (row_grad.astype(jnp.bfloat16), expert_out)


def token_grad(
    saved, cotan, norm_gain, router_w, chosen, gate_total, gate_share, route_pick, dgate, row_sum
):
    dchosen = (dgate - jnp.sum(gate_share * dgate, axis=-1, keepdims=True)) / gate_total
    logit_grad = dchosen * chosen * (1.0 - chosen)
    logit_full = jnp.einsum("tk,tke->te", logit_grad, route_pick, precision=lax.Precision.HIGHEST)
    router_back = jnp.dot(
        logit_full, router_w.astype(jnp.float32).T, precision=lax.Precision.HIGHEST
    )
    _, norm_pull = jax.vjp(lambda values: norm_rows(values, norm_gain), saved.astype(jnp.float32))
    return (cotan.astype(jnp.float32) + norm_pull(row_sum + router_back)[0]).astype(jnp.bfloat16)


def prepare_group(tokens_in, routes, norm_gain, router_w, expert_count, cap_rows):
    normed = norm_rows(tokens_in, norm_gain).astype(jnp.bfloat16)
    chosen, gate_total, gate_share, route_pick = gate_values(normed, router_w, routes, expert_count)
    gb_wide = gate_share.astype(jnp.bfloat16).astype(jnp.float32)
    placement = slot_matrix(routes, expert_count, cap_rows)
    spread = jnp.sum(placement, axis=1).astype(jnp.bfloat16)
    weighted = jnp.sum(placement * gb_wide[:, :, None], axis=1).astype(jnp.bfloat16)
    outgoing = jnp.einsum("tp,td->pd", spread, normed, preferred_element_type=jnp.float32).astype(
        jnp.bfloat16
    )
    outgoing = outgoing.reshape(expert_count, cap_rows, tokens_in.shape[-1])
    return (outgoing, (chosen, gate_total, gate_share, route_pick, placement, spread, weighted))


def local(
    fwd_tokens,
    saved_tokens,
    cotangent,
    fwd_routes,
    bwd_routes,
    norm_gain,
    router,
    w_gate,
    w_up,
    w_down,
):
    forward_in = fwd_tokens[0]
    cotan_in = cotangent[0]
    gain_row = norm_gain[0]
    router_w = router[0]
    gate_w = w_gate[0]
    up_w = w_up[0]
    down_w = w_down[0]
    tick_count = saved_tokens.shape[0]
    tok_rows = forward_in.shape[0]
    width = forward_in.shape[1]
    top_count = fwd_routes.shape[-1]
    expert_count = router_w.shape[1]
    cap_rows = 5 * tok_rows * top_count // (4 * expert_count)
    split_count = lax.axis_size("expert") // expert_count

    def fold_parts(received):
        return received.reshape(expert_count, split_count, cap_rows, width)

    for tick_index in range(tick_count):
        saved = saved_tokens[tick_index, 0]
        send_fwd, fwd_parts = prepare_group(
            forward_in, fwd_routes[tick_index, 0], gain_row, router_w, expert_count, cap_rows
        )
        send_saved, bwd_parts = prepare_group(
            saved, bwd_routes[tick_index, 0], gain_row, router_w, expert_count, cap_rows
        )
        chosen_b, total_b, share_b, pick_b, place_b, spread_b, weighted_b = bwd_parts
        send_cot = jnp.einsum(
            "tp,td->pd", weighted_b, cotan_in, preferred_element_type=jnp.float32
        ).astype(jnp.bfloat16)
        send_cot = send_cot.reshape(expert_count, cap_rows, width)
        send_fwd = jnp.repeat(send_fwd, split_count, axis=0)
        send_saved = jnp.repeat(send_saved, split_count, axis=0)
        send_cot = jnp.repeat(send_cot, split_count, axis=0)
        row_block = lax.all_to_all(send_fwd, "expert", split_axis=0, concat_axis=0, tiled=True)
        run_row_shape = row_block.shape
        result = expert_forward(row_block.reshape(-1, width), gate_w, up_w, down_w).reshape(
            run_row_shape
        )
        back_fwd = lax.all_to_all(result, "expert", split_axis=0, concat_axis=0, tiled=True)
        pieces = (
            lax.all_to_all(send_saved, "expert", split_axis=0, concat_axis=0, tiled=True),
            lax.all_to_all(send_cot, "expert", split_axis=0, concat_axis=0, tiled=True),
        )
        row_shape = pieces[0].shape
        grads, outs = expert_backward(
            pieces[0].reshape(-1, width), pieces[1].reshape(-1, width), gate_w, up_w, down_w
        )
        back_grad = lax.all_to_all(
            grads.reshape(row_shape), "expert", split_axis=0, concat_axis=0, tiled=True
        )
        back_out = lax.all_to_all(
            outs.reshape(row_shape), "expert", split_axis=0, concat_axis=0, tiled=True
        )
        weighted_f = fwd_parts[6].reshape(tok_rows, expert_count, cap_rows)
        mixture = jnp.einsum(
            "tec,ejcd->td", weighted_f, fold_parts(back_fwd), preferred_element_type=jnp.float32
        )
        fwd_result = (forward_in.astype(jnp.float32) + mixture).astype(jnp.bfloat16)
        spread_three = spread_b.reshape(tok_rows, expert_count, cap_rows)
        row_sum = jnp.einsum(
            "tec,ejcd->td", spread_three, fold_parts(back_grad), preferred_element_type=jnp.float32
        )
        place_four = place_b.astype(jnp.bfloat16).reshape(
            tok_rows, top_count, expert_count, cap_rows
        )
        out_route = jnp.einsum(
            "tkec,ejcd->tkd", place_four, fold_parts(back_out), preferred_element_type=jnp.float32
        )
        dgate = jnp.sum(out_route * cotan_in.astype(jnp.float32)[:, None, :], axis=-1)
        bwd_result = token_grad(
            saved, cotan_in, gain_row, router_w, chosen_b, total_b, share_b, pick_b, dgate, row_sum
        )
        if tick_index + 1 < tick_count:
            forward_in = from_behind(fwd_result, "pipe", 1)
            cotan_in = from_behind(bwd_result, "pipe", -1)
    return (fwd_result[None], bwd_result[None])


def solution(mesh):
    return jax.shard_map(
        local,
        mesh=mesh,
        in_specs=(
            P("pipe", "expert", None),
            P(None, "pipe", "expert", None),
            P("pipe", "expert", None),
            P(None, "pipe", "expert", None),
            P(None, "pipe", "expert", None),
            P("pipe", None),
            P("pipe", None, None),
            P("pipe", None, "expert"),
            P("pipe", None, "expert"),
            P("pipe", "expert", None),
        ),
        out_specs=(P("pipe", "expert", None), P("pipe", "expert", None)),
        check_vma=False,
    )
```

profile of v0, /device:TPU:56, one launch (start us, length us, event | category | flops | bytes accessed | tf_op | source)
XLA Modules:
  0.0 1155.2 jit_solution(18383151806400044760)
XLA Ops:
  9.4 17.9 %all-to-all-start.5 = ((bf16[32,5,3584]{2,1,0:T(8,128)(2,1)}), bf16[32,5,3584]{2,1,0:T(8,128)(2,1)S(1)}, u32[]{:S(2)}, u32[]{:S(2)}) async-start(bf16[32,5,3584]{2,1,0:T(8,128)(2,1)} %bitcast.254), calls=%async_computation.5 | async-start | bytes 3670016 | tf_op jit(solution)/shard_map/all_to_all | solution.py:149
  27.7 87.2 %all-to-all-done.5 = bf16[32,5,3584]{2,1,0:T(8,128)(2,1)S(1)} async-done(((bf16[32,5,3584]{2,1,0:T(8,128)(2,1)}), bf16[32,5,3584]{2,1,0:T(8,128)(2,1)S(1)}, u32[]{:S(2)}, u32[]{:S(2)}) %all-to-all-start.5) | async-done | bytes 1146912 | tf_op jit(solution)/shard_map/all_to_all | solution.py:149
  116.2 6.7 all-to-all-start.4
  126.8 82.8 %all-to-all-done.4 = bf16[32,5,3584]{2,1,0:T(8,128)(2,1)} async-done(((bf16[32,5,3584]{2,1,0:T(8,128)(2,1)}), bf16[32,5,3584]{2,1,0:T(8,128)(2,1)}, u32[]{:S(2)}, u32[]{:S(2)}) %all-to-all-start.4) | async-done | bytes 1146912 | tf_op jit(solution)/shard_map/all_to_all | solution.py:150
  211.0 7.0 all-to-all-start
  219.3 2.6 reshape.406
  222.0 1.9 fusion.49
  226.8 2.5 reshape.410
  229.3 75.5 %all-to-all-done = bf16[32,5,3584]{2,1,0:T(8,128)(2,1)} async-done(((bf16[32,5,3584]{2,1,0:T(8,128)(2,1)}), bf16[32,5,3584]{2,1,0:T(8,128)(2,1)}, u32[]{:S(2)}, u32[]{:S(2)}) %all-to-all-start) | async-done | bytes 1146912 | tf_op jit(solution)/shard_map/all_to_all | solution.py:142
  304.9 6.9 all-to-all-start.6
  313.3 2.6 reshape.411
  315.9 82.8 %all-to-all-done.6 = bf16[32,5,3584]{2,1,0:T(8,128)(2,1)} async-done(((bf16[32,5,3584]{2,1,0:T(8,128)(2,1)}), bf16[32,5,3584]{2,1,0:T(8,128)(2,1)}, u32[]{:S(2)}, u32[]{:S(2)}) %all-to-all-start.6) | async-done | bytes 1146912 | tf_op jit(solution)/shard_map/all_to_all | solution.py:156
  398.6 6.9 all-to-all-start.7
  405.6 2.5 reshape.398
  408.1 1.7 fusion.53
  409.8 3.1 convolution_convert_fusion.3
  412.9 2.5 reshape.399
  415.4 77.0 %all-to-all-done.7 = bf16[32,5,3584]{2,1,0:T(8,128)(2,1)} async-done(((bf16[32,5,3584]{2,1,0:T(8,128)(2,1)}), bf16[32,5,3584]{2,1,0:T(8,128)(2,1)}, u32[]{:S(2)}, u32[]{:S(2)}) %all-to-all-start.7) | async-done | bytes 1146912 | tf_op jit(solution)/shard_map/all_to_all | solution.py:159
  492.4 6.9 all-to-all-start.1
  499.4 1.9 convert_reduce_fusion.2
  501.8 1.9 convert_reduce_fusion.3
  507.0 79.2 %all-to-all-done.1 = bf16[32,5,3584]{2,1,0:T(8,128)(2,1)} async-done(((bf16[32,5,3584]{2,1,0:T(8,128)(2,1)}), bf16[32,5,3584]{2,1,0:T(8,128)(2,1)}, u32[]{:S(2)}, u32[]{:S(2)}) %all-to-all-start.1) | async-done | bytes 1146912 | tf_op jit(solution)/shard_map/all_to_all | solution.py:147
  587.6 7.1 all-to-all-start.9
  594.8 1.9 collective-permute-start.1
  596.7 1.8 collective-permute-done.1
  598.8 82.5 %all-to-all-done.9 = bf16[32,5,3584]{2,1,0:T(8,128)(2,1)} async-done(((bf16[32,5,3584]{2,1,0:T(8,128)(2,1)}), bf16[32,5,3584]{2,1,0:T(8,128)(2,1)}, u32[]{:S(2)}, u32[]{:S(2)}) %all-to-all-start.9) | async-done | bytes 1146912 | tf_op jit(solution)/shard_map/all_to_all | solution.py:149
  682.7 7.2 all-to-all-start.8
  690.0 1.9 convert_reduce_fusion.5
  692.2 1.9 collective-permute-start
  694.1 3.6 collective-permute-done
  698.5 78.3 %all-to-all-done.8 = bf16[32,5,3584]{2,1,0:T(8,128)(2,1)} async-done(((bf16[32,5,3584]{2,1,0:T(8,128)(2,1)}), bf16[32,5,3584]{2,1,0:T(8,128)(2,1)}, u32[]{:S(2)}, u32[]{:S(2)}) %all-to-all-start.8) | async-done | bytes 1146912 | tf_op jit(solution)/shard_map/all_to_all | solution.py:150
  778.2 6.9 all-to-all-start.2
  785.1 2.5 reshape.417
  787.7 1.8 fusion.34
  791.4 2.6 reshape.419
  794.0 78.0 %all-to-all-done.2 = bf16[32,5,3584]{2,1,0:T(8,128)(2,1)} async-done(((bf16[32,5,3584]{2,1,0:T(8,128)(2,1)}), bf16[32,5,3584]{2,1,0:T(8,128)(2,1)}, u32[]{:S(2)}, u32[]{:S(2)}) %all-to-all-start.2) | async-done | bytes 1146912 | tf_op jit(solution)/shard_map/all_to_all | solution.py:142
  872.0 6.9 all-to-all-start.11
  878.9 2.6 reshape.414
  885.2 2.6 reshape.418
  887.8 78.0 %all-to-all-done.11 = bf16[32,5,3584]{2,1,0:T(8,128)(2,1)} async-done(((bf16[32,5,3584]{2,1,0:T(8,128)(2,1)}), bf16[32,5,3584]{2,1,0:T(8,128)(2,1)}, u32[]{:S(2)}, u32[]{:S(2)}) %all-to-all-start.11) | async-done | bytes 1146912 | tf_op jit(solution)/shard_map/all_to_all | solution.py:159
  965.8 6.9 all-to-all-start.10
  972.7 2.5 reshape.402
  976.9 2.1 convolution_convert_fusion.2
  980.5 79.0 %all-to-all-done.10 = bf16[32,5,3584]{2,1,0:T(8,128)(2,1)} async-done(((bf16[32,5,3584]{2,1,0:T(8,128)(2,1)}), bf16[32,5,3584]{2,1,0:T(8,128)(2,1)}, u32[]{:S(2)}, u32[]{:S(2)}) %all-to-all-start.10) | async-done | bytes 1146912 | tf_op jit(solution)/shard_map/all_to_all | solution.py:156
  1059.5 6.9 all-to-all-start.3
  1066.6 1.9 convert_reduce_fusion
  1069.0 1.9 convert_reduce_fusion.1
  1071.6 81.6 %all-to-all-done.3 = bf16[32,5,3584]{2,1,0:T(8,128)(2,1)S(1)} async-done(((bf16[32,5,3584]{2,1,0:T(8,128)(2,1)}), bf16[32,5,3584]{2,1,0:T(8,128)(2,1)S(1)}, u32[]{:S(2)}, u32[]{:S(2)}) %all-to-all-start.3) | async-done | bytes 1146912 | tf_op jit(solution)/shard_map/all_to_all | solution.py:147
  (175 shorter events, 43.1 us)
Async XLA Ops:
  0.6 223.7 %copy-start = (bf16[1,128,3584]{2,1,0:T(8,128)(2,1)S(1)}, bf16[1,128,3584]{2,1,0:T(8,128)(2,1)}, u32[]{:S(2)}) copy-start(bf16[1,128,3584]{2,1,0:T(8,128)(2,1)} %param.19) | copy-start | bytes 2752516
  1.7 0.7 copy-start.26
  1.7 7.7 copy-start.20
  9.4 18.0 %copy-start.7 = (bf16[1,8,3584]{2,1,0:T(8,128)(2,1)S(1)}, bf16[1,8,3584]{2,1,0:T(8,128)(2,1)}, u32[]{:S(2)}) copy-start(bf16[1,8,3584]{2,1,0:T(8,128)(2,1)} %param.12) | copy-start | bytes 172036
  9.4 105.5 %all-to-all-start.5 = ((bf16[32,5,3584]{2,1,0:T(8,128)(2,1)}), bf16[32,5,3584]{2,1,0:T(8,128)(2,1)S(1)}, u32[]{:S(2)}, u32[]{:S(2)}) async-start(bf16[32,5,3584]{2,1,0:T(8,128)(2,1)} %bitcast.254), calls=%async_computation.5 | async-start | bytes 3670016 | tf_op jit(solution)/shard_map/all_to_all | solution.py:149
  116.2 6.8 copy-start.11
  116.2 8.6 copy-start.8
  116.2 8.8 copy-start.9
  116.2 93.4 %all-to-all-start.4 = ((bf16[32,5,3584]{2,1,0:T(8,128)(2,1)}), bf16[32,5,3584]{2,1,0:T(8,128)(2,1)}, u32[]{:S(2)}, u32[]{:S(2)}) async-start(bf16[32,5,3584]{2,1,0:T(8,128)(2,1)} %bitcast.249), calls=%async_computation.4 | async-start | bytes 3670016 | tf_op jit(solution)/shard_map/all_to_all | solution.py:150
  211.0 93.9 %all-to-all-start = ((bf16[32,5,3584]{2,1,0:T(8,128)(2,1)}), bf16[32,5,3584]{2,1,0:T(8,128)(2,1)}, u32[]{:S(2)}, u32[]{:S(2)}) async-start(bf16[32,5,3584]{2,1,0:T(8,128)(2,1)} %bitcast.252), calls=%async_computation | async-start | bytes 3670016 | tf_op jit(solution)/shard_map/all_to_all | solution.py:142
  219.3 2.6 copy-start.1
  219.3 4.5 copy-start.2
  222.0 1.9 copy-start.3
  222.0 2.4 copy-start.5
  304.9 93.8 %all-to-all-start.6 = ((bf16[32,5,3584]{2,1,0:T(8,128)(2,1)}), bf16[32,5,3584]{2,1,0:T(8,128)(2,1)}, u32[]{:S(2)}, u32[]{:S(2)}) async-start(bf16[32,5,3584]{2,1,0:T(8,128)(2,1)} %reshape.410), calls=%async_computation.6 | async-start | bytes 3670016 | tf_op jit(solution)/shard_map/all_to_all | solution.py:156
  398.6 93.8 %all-to-all-start.7 = ((bf16[32,5,3584]{2,1,0:T(8,128)(2,1)}), bf16[32,5,3584]{2,1,0:T(8,128)(2,1)}, u32[]{:S(2)}, u32[]{:S(2)}) async-start(bf16[32,5,3584]{2,1,0:T(8,128)(2,1)} %reshape.411), calls=%async_computation.7 | async-start | bytes 3670016 | tf_op jit(solution)/shard_map/all_to_all | solution.py:159
  492.4 93.8 %all-to-all-start.1 = ((bf16[32,5,3584]{2,1,0:T(8,128)(2,1)}), bf16[32,5,3584]{2,1,0:T(8,128)(2,1)}, u32[]{:S(2)}, u32[]{:S(2)}) async-start(bf16[32,5,3584]{2,1,0:T(8,128)(2,1)} %reshape.399), calls=%async_computation.1 | async-start | bytes 3670016 | tf_op jit(solution)/shard_map/all_to_all | solution.py:147
  499.4 4.3 copy-start.24
  501.3 2.7 copy-start.6
  501.3 4.7 copy-start.16
  504.9 0.6 copy-start.28
  504.9 1.8 copy-start.22
  505.5 0.5 copy-start.13
  587.5 7.1 copy-start.27
  587.5 7.1 copy-start.30
  587.5 7.1 copy-start.21
  587.6 11.0 copy-start.10
  587.6 93.7 %all-to-all-start.9 = ((bf16[32,5,3584]{2,1,0:T(8,128)(2,1)}), bf16[32,5,3584]{2,1,0:T(8,128)(2,1)}, u32[]{:S(2)}, u32[]{:S(2)}) async-start(bf16[32,5,3584]{2,1,0:T(8,128)(2,1)} %bitcast.251), calls=%async_computation.9 | async-start | bytes 3670016 | tf_op jit(solution)/shard_map/all_to_all | solution.py:149
  594.8 3.7 collective-permute-start.1
  682.7 7.3 copy-start.12
  682.7 94.1 %all-to-all-start.8 = ((bf16[32,5,3584]{2,1,0:T(8,128)(2,1)}), bf16[32,5,3584]{2,1,0:T(8,128)(2,1)}, u32[]{:S(2)}, u32[]{:S(2)}) async-start(bf16[32,5,3584]{2,1,0:T(8,128)(2,1)} %bitcast.250), calls=%async_computation.8 | async-start | bytes 3670016 | tf_op jit(solution)/shard_map/all_to_all | solution.py:150
  689.9 8.1 copy-start.18
  689.9 8.2 copy-start.19
  692.2 5.5 collective-permute-start
  778.2 93.8 %all-to-all-start.2 = ((bf16[32,5,3584]{2,1,0:T(8,128)(2,1)}), bf16[32,5,3584]{2,1,0:T(8,128)(2,1)}, u32[]{:S(2)}, u32[]{:S(2)}) async-start(bf16[32,5,3584]{2,1,0:T(8,128)(2,1)} %bitcast.253), calls=%async_computation.2 | async-start | bytes 3670016 | tf_op jit(solution)/shard_map/all_to_all | solution.py:142
  787.7 1.8 copy-start.4
  872.0 93.8 %all-to-all-start.11 = ((bf16[32,5,3584]{2,1,0:T(8,128)(2,1)}), bf16[32,5,3584]{2,1,0:T(8,128)(2,1)}, u32[]{:S(2)}, u32[]{:S(2)}) async-start(bf16[32,5,3584]{2,1,0:T(8,128)(2,1)} %reshape.419), calls=%async_computation.11 | async-start | bytes 3670016 | tf_op jit(solution)/shard_map/all_to_all | solution.py:159
  965.8 93.8 %all-to-all-start.10 = ((bf16[32,5,3584]{2,1,0:T(8,128)(2,1)}), bf16[32,5,3584]{2,1,0:T(8,128)(2,1)}, u32[]{:S(2)}, u32[]{:S(2)}) async-start(bf16[32,5,3584]{2,1,0:T(8,128)(2,1)} %reshape.418), calls=%async_computation.10 | async-start | bytes 3670016 | tf_op jit(solution)/shard_map/all_to_all | solution.py:156
  1059.5 93.7 %all-to-all-start.3 = ((bf16[32,5,3584]{2,1,0:T(8,128)(2,1)}), bf16[32,5,3584]{2,1,0:T(8,128)(2,1)S(1)}, u32[]{:S(2)}, u32[]{:S(2)}) async-start(bf16[32,5,3584]{2,1,0:T(8,128)(2,1)} %reshape.403), calls=%async_computation.3 | async-start | bytes 3670016 | tf_op jit(solution)/shard_map/all_to_all | solution.py:147
  1066.4 2.1 copy-start.17
  1066.4 2.1 copy-start.25
  1066.4 2.5 copy-start.15
  1066.4 2.6 copy-start.14
  1068.5 3.1 copy-start.29
  1070.9 82.7 %copy-start.23 = (f32[8]{0:T(128)S(1)}, f32[8]{0:T(128)}, u32[]{:S(2)}) copy-start(f32[8]{0:T(128)} %copy-done.22) | copy-start | bytes 100
where the time goes:
time: 1160 us
  waiting for transfers between devices  967 us (83%)
  starting transfers between devices  98.1 us (8%)
  local copies, waits for them, and re-layouts  40.6 us (4%)
  matrix products  30.1 us (3%)
  other arithmetic  17.8 us (2%)
    all_to_all x2, waiting for transfers between devices, local(): lax.all_to_all(send_saved, 'expert', split_axis=0, concat_axis=0, tiled=T...  170 us
    all_to_all x2, waiting for transfers between devices, local(): lax.all_to_all(grads.reshape(row_shape), 'expert', split_axis=0, concat_a...  162 us
    all_to_all x2, waiting for transfers between devices, local(): lax.all_to_all(send_cot, 'expert', split_axis=0, concat_axis=0, tiled=True)  161 us
    all_to_all x2, waiting for transfers between devices, local(): lax.all_to_all(result, 'expert', split_axis=0, concat_axis=0, tiled=True)  161 us
    all_to_all x2, waiting for transfers between devices, local(): lax.all_to_all(outs.reshape(row_shape), 'expert', split_axis=0, concat_ax...  155 us
    all_to_all x2, waiting for transfers between devices, local(): lax.all_to_all(send_fwd, 'expert', split_axis=0, concat_axis=0, tiled=True)  154 us
    all_to_all x2, starting transfers between devices, local(): lax.all_to_all(send_saved, 'expert', split_axis=0, concat_axis=0, tiled=T...  25 us
  transfers between devices with their start and end apart: 14, of which 14 were waited for; matrix products, arithmetic and copies ran while one was open for 6% of the time, Pallas kernels for 0%

commit v1 on v0

v1 whole, which is shorter than its diff:
```python
import jax
import jax.numpy as jnp
from jax import lax
from jax.sharding import PartitionSpec as P

BF16 = jnp.bfloat16
F32 = jnp.float32


def shift(block, axis, distance):
    size = lax.axis_size(axis)
    return lax.ppermute(block, axis, [((i - distance) % size, i) for i in range(size)])


def norm_rows(values, norm_gain):
    wide = values.astype(F32)
    scale = lax.rsqrt(jnp.mean(wide * wide, axis=-1, keepdims=True) + 1e-06)
    return wide * scale * norm_gain


def norm_pull(values, norm_gain, grad):
    wide = values.astype(F32)
    scale = lax.rsqrt(jnp.mean(wide * wide, axis=-1, keepdims=True) + 1e-06)
    scaled = grad * norm_gain
    inner = jnp.mean(scaled * wide, axis=-1, keepdims=True)
    return scale * (scaled - wide * (scale * scale) * inner)


def gate_values(normed, router_w, pick):
    logits = jnp.dot(normed, router_w, preferred_element_type=F32)
    sig_all = jax.nn.sigmoid(logits)
    chosen = jnp.sum(pick * sig_all[:, None, :], axis=-1)
    total = jnp.sum(chosen, axis=-1, keepdims=True)
    return chosen, total, chosen / total


def slot_places(routes, experts, cap):
    flat = routes.reshape(-1)
    hit = (flat[:, None] == jnp.arange(experts, dtype=jnp.int32)).astype(F32)
    count = flat.shape[0]
    earlier = (jnp.arange(count)[:, None] > jnp.arange(count)[None, :]).astype(F32)
    before = jnp.dot(earlier, hit, preferred_element_type=F32)
    slot = jnp.sum(before * hit, axis=1).astype(jnp.int32)
    place = hit[:, :, None] * (slot[:, None, None] == jnp.arange(cap, dtype=jnp.int32)).astype(F32)
    return place.reshape(routes.shape + (experts, cap))


def slab_sizes(width):
    return width // 2, width // 7


def pieces(rows, step):
    return jnp.concatenate([rows[:, i:i + step] for i in range(0, rows.shape[1], step)], axis=0)


def unpieces(stacked, count):
    tokens = stacked.shape[0] // count
    return jnp.concatenate([stacked[i * tokens:(i + 1) * tokens] for i in range(count)], axis=1)


def pack_rows(rows, spread, copies, scalars=None):
    tokens, width = rows.shape
    experts = spread.shape[1]
    half, piece = slab_sizes(width)
    eye2 = jnp.eye(2, dtype=F32)
    eye87 = jnp.eye(8, 7, dtype=F32)
    main = jnp.einsum("tes,hg->ehsgt", spread[:, :, :4], eye2).reshape(experts, 1, 8, 2 * tokens)
    tail = jnp.einsum("te,cd->ecdt", spread[:, :, 4], eye87).reshape(experts, 1, 8, 7 * tokens)
    main = jnp.broadcast_to(main, (experts, copies, 8, 2 * tokens)).reshape(-1, 2 * tokens)
    tail = jnp.broadcast_to(tail, (experts, copies, 8, 7 * tokens)).reshape(-1, 7 * tokens)
    out_main = jnp.dot(main.astype(BF16), pieces(rows, half), preferred_element_type=F32).astype(BF16)
    out_tail = jnp.dot(tail.astype(BF16), pieces(rows, piece), preferred_element_type=F32)
    if scalars is not None:
        extra = jnp.zeros((experts, 1, 8, piece), F32).at[:, 0, 7, :scalars.shape[1]].set(scalars)
        extra = jnp.broadcast_to(extra, (experts, copies, 8, piece)).reshape(-1, piece)
        out_tail = out_tail + extra
    slab = jnp.concatenate([out_main, out_tail.astype(BF16)], axis=1)
    return slab.reshape(experts * copies, 8, half + piece)


def combine_rows(slabs, weights):
    tokens, experts, cap = weights.shape
    copies = slabs.shape[0] // experts
    half = slabs.shape[2] * 7 // 9
    eye2 = jnp.eye(2, dtype=F32)
    eye78 = jnp.eye(7, 8, dtype=F32)
    flat = slabs.reshape(-1, slabs.shape[2])
    main = jnp.einsum("tes,gh->gtehs", weights[:, :, :4], eye2).reshape(2 * tokens, experts, 1, 8)
    tail = jnp.einsum("te,dc->dtec", weights[:, :, 4], eye78).reshape(7 * tokens, experts, 1, 8)
    main = jnp.broadcast_to(main, (2 * tokens, experts, copies, 8)).reshape(2 * tokens, -1)
    tail = jnp.broadcast_to(tail, (7 * tokens, experts, copies, 8)).reshape(7 * tokens, -1)
    sum_main = jnp.dot(main.astype(BF16), flat[:, :half], preferred_element_type=F32)
    sum_tail = jnp.dot(tail.astype(BF16), flat[:, half:], preferred_element_type=F32)
    return unpieces(sum_main, 2) + unpieces(sum_tail, 7)


def open_slabs(slabs):
    sources, _, full = slabs.shape
    half = full * 7 // 9
    first = jnp.concatenate([slabs[:, 0:4, :half], slabs[:, 4:8, :half]], axis=2)
    last = slabs[:, 0:7, half:].reshape(sources, -1)
    return jnp.concatenate([first.reshape(sources * 4, -1), last], axis=0)


def close_slabs(rows, sources, scalars=None):
    width = rows.shape[1]
    half, piece = slab_sizes(width)
    first = rows[:sources * 4].reshape(sources, 4, width)
    main = jnp.concatenate([first[:, :, :half], first[:, :, half:]], axis=1)
    last = rows[sources * 4:].reshape(sources, 7, piece)
    extra = jnp.zeros((sources, 1, piece), BF16)
    if scalars is not None:
        extra = extra.at[:, 0, :scalars.shape[1]].set(scalars.astype(BF16))
    tail = jnp.concatenate([last, extra], axis=1)
    return jnp.concatenate([main, tail], axis=2)


def slot_scalars(slabs, count, first=0):
    half = slabs.shape[2] * 7 // 9
    return slabs[:, 7, half + first:half + first + count].astype(F32)


def in_row_order(per_slot):
    sources = per_slot.shape[0]
    return jnp.concatenate([per_slot[:, :4].reshape(sources * 4), per_slot[:, 4]])


def in_slot_order(per_row, sources):
    return jnp.concatenate([per_row[:sources * 4].reshape(sources, 4), per_row[sources * 4:, None]], axis=1)


def expert_forward(slabs, gate_w, up_w, down_w):
    rows = open_slabs(slabs)
    gate_pre = jnp.dot(rows, gate_w, preferred_element_type=F32)
    up_pre = jnp.dot(rows, up_w, preferred_element_type=F32)
    hidden = (jax.nn.silu(gate_pre) * up_pre).astype(BF16)
    out = jnp.dot(hidden, down_w, preferred_element_type=F32).astype(BF16)
    return close_slabs(out, slabs.shape[0])


def expert_backward(saved_slabs, cot_slabs, gate_w, up_w, down_w):
    sources = saved_slabs.shape[0]
    rows = open_slabs(saved_slabs)
    cot = open_slabs(cot_slabs)
    gb = in_row_order(slot_scalars(cot_slabs, 5))
    gate_pre = jnp.dot(rows, gate_w, preferred_element_type=F32)
    up_pre = jnp.dot(rows, up_w, preferred_element_type=F32)
    gate_sig = jax.nn.sigmoid(gate_pre)
    gate_act = gate_pre * gate_sig
    hidden = (gate_act * up_pre).astype(BF16).astype(F32)
    cot_hidden = jnp.einsum("rd,fd->rf", cot, down_w, preferred_element_type=F32)
    dgate = jnp.sum(hidden * cot_hidden, axis=1)
    hidden_grad = cot_hidden * gb[:, None]
    gate_grad = (hidden_grad * up_pre * gate_sig * (1.0 + gate_pre * (1.0 - gate_sig))).astype(BF16)
    up_grad = (hidden_grad * gate_act).astype(BF16)
    row_grad = jnp.einsum("rf,df->rd", gate_grad, gate_w, preferred_element_type=F32)
    row_grad = row_grad + jnp.einsum("rf,df->rd", up_grad, up_w, preferred_element_type=F32)
    dgate = in_slot_order(dgate, sources)
    high = lax.reduce_precision(dgate, 8, 7)
    low = dgate - high
    return close_slabs(row_grad.astype(BF16), sources, jnp.concatenate([high, low], axis=1))


def local(
    fwd_tokens,
    saved_tokens,
    cotangent,
    fwd_routes,
    bwd_routes,
    norm_gain,
    router,
    w_gate,
    w_up,
    w_down,
):
    gain = norm_gain[0]
    router_w = router[0]
    ticks = saved_tokens.shape[0]
    tokens = fwd_tokens.shape[1]
    top = fwd_routes.shape[-1]
    experts = router_w.shape[1]
    cap = 5 * tokens * top // (4 * experts)
    ranks = lax.axis_size("expert")
    depth = ranks // 2
    copies = depth // experts
    columns = [[x + 2 * z for z in range(depth)] for x in range(2)]
    partner = [(i, i ^ 1) for i in range(ranks)]

    def exchange(slabs):
        return lax.all_to_all(
            slabs, "expert", split_axis=0, concat_axis=0, axis_index_groups=columns, tiled=True
        )

    gate_w = jnp.concatenate([w_gate[0], lax.ppermute(w_gate[0], "expert", partner)], axis=1)
    up_w = jnp.concatenate([w_up[0], lax.ppermute(w_up[0], "expert", partner)], axis=1)
    down_w = jnp.concatenate([w_down[0], lax.ppermute(w_down[0], "expert", partner)], axis=0)

    forward_in = fwd_tokens[0]
    cotan_in = cotangent[0]
    expert_ids = jnp.arange(experts, dtype=jnp.int32)
    saved_parts = []
    for t in range(ticks):
        saved = saved_tokens[t, 0]
        saved_norm = norm_rows(saved, gain).astype(BF16)
        pick = (bwd_routes[t, 0][..., None] == expert_ids).astype(F32)
        place = slot_places(bwd_routes[t, 0], experts, cap)
        chosen, total, share = gate_values(saved_norm, router_w, pick)
        gb = share.astype(BF16).astype(F32)
        spread = jnp.sum(place, axis=1)
        slot_gb = jnp.sum(place * gb[:, :, None, None], axis=(0, 1))
        saved_parts.append((saved, saved_norm, pick, place, chosen, total, share, spread, slot_gb))

    for t in range(ticks):
        saved, saved_norm, pick, place, chosen, total, share, spread, slot_gb = saved_parts[t]
        normed = norm_rows(forward_in, gain).astype(BF16)
        place_f = slot_places(fwd_routes[t, 0], experts, cap)
        pick_f = (fwd_routes[t, 0][..., None] == expert_ids).astype(F32)
        rows_f = exchange(pack_rows(normed, jnp.sum(place_f, axis=1), copies))
        rows_m = exchange(pack_rows(saved_norm, spread, copies))
        rows_c = exchange(pack_rows(cotan_in, spread, copies, slot_gb))
        _, _, share_f = gate_values(normed, router_w, pick_f)
        gb_f = share_f.astype(BF16).astype(F32)
        weights_f = jnp.sum(place_f * gb_f[:, :, None, None], axis=1)
        back_f = exchange(expert_forward(rows_f, gate_w, up_w, down_w))
        back_b = exchange(expert_backward(rows_m, rows_c, gate_w, up_w, down_w))

        fwd_result = (forward_in.astype(F32) + combine_rows(back_f, weights_f)).astype(BF16)

        row_sum = combine_rows(back_b, spread)
        slot_dgate = slot_scalars(back_b, cap) + slot_scalars(back_b, cap, cap)
        slot_dgate = jnp.sum(slot_dgate.reshape(experts, copies, cap), axis=1)
        dgate = jnp.sum(place * slot_dgate, axis=(2, 3))
        dchosen = (dgate - jnp.sum(share * dgate, axis=-1, keepdims=True)) / total
        logit_grad = dchosen * chosen * (1.0 - chosen)
        logit_full = jnp.sum(logit_grad[:, :, None] * pick, axis=1)
        router_back = jnp.dot(logit_full, router_w.astype(F32).T, precision=lax.Precision.HIGHEST)
        pulled = norm_pull(saved, gain, row_sum + router_back)
        bwd_result = (cotan_in.astype(F32) + pulled).astype(BF16)
        if t + 1 < ticks:
            forward_in = shift(fwd_result, "pipe", 1)
            cotan_in = shift(bwd_result, "pipe", -1)
    return (fwd_result[None], bwd_result[None])


def solution(mesh):
    return jax.shard_map(
        local,
        mesh=mesh,
        in_specs=(
            P("pipe", "expert", None),
            P(None, "pipe", "expert", None),
            P("pipe", "expert", None),
            P(None, "pipe", "expert", None),
            P(None, "pipe", "expert", None),
            P("pipe", None),
            P("pipe", None, None),
            P("pipe", None, "expert"),
            P("pipe", None, "expert"),
            P("pipe", "expert", None),
        ),
        out_specs=(P("pipe", "expert", None), P("pipe", "expert", None)),
        check_vma=False,
    )
```

time: 1160 us -> 476 us (0.41)
  the two profiles are of different devices: /device:TPU:56 before, /device:TPU:44 now
where the time goes in v1:
time: 476 us; the launch traced here: 474 us
  waiting for transfers between devices  258 us (54%)
  starting transfers between devices  86.6 us (18%)
  blocking collectives  40.5 us (9%)
  matrix products  32.7 us (7%)
  local copies, waits for them, and re-layouts  26.9 us (6%)
  other arithmetic  26.4 us (6%)
    all_to_all x9, waiting for transfers between devices, exchange(): lax.all_to_all(slabs, 'expert', split_axis=0, concat_axis=0, axis_index_g...  227 us
    all_to_all x9, starting transfers between devices, exchange(): lax.all_to_all(slabs, 'expert', split_axis=0, concat_axis=0, axis_index_g...  72.8 us
    all_to_all x1, blocking collectives, exchange(): lax.all_to_all(slabs, 'expert', split_axis=0, concat_axis=0, axis_index_g...  40.5 us
    ppermute x1, waiting for transfers between devices, local(): lax.ppermute(w_down[0], 'expert', partner)  17.7 us
    ppermute x1, waiting for transfers between devices, local(): lax.ppermute(w_gate[0], 'expert', partner)  10.6 us
  transfers between devices with their start and end apart: 14, of which 12 were waited for; matrix products, arithmetic and copies ran while one was open for 9% of the time, Pallas kernels for 0%

profile of v1, /device:TPU:44, one launch (start us, length us, event | category | flops | bytes accessed | tf_op | source)
XLA Modules:
  0.0 474.1 jit_solution(3011532190295318556)
XLA Ops:
  3.9 1.0 fusion.16
  5.0 1.0 fusion.22
  15.8 15.2 %all-to-all-start.5 = ((bf16[16,8,2304]{2,1,0:T(8,128)(2,1)}), bf16[16,8,2304]{2,1,0:T(8,128)(2,1)S(1)}, u32[]{:S(2)}, u32[]{:S(2)}) async-start(bf16[16,8,2304]{2,1,0:T(8,128)(2,1)} %maximum_bitcast_fusion.3), calls=%async_computation.5 | async-start | bytes 1179648 | tf_op jit(solution)/shard_map/all_to_all | solution.py:190
  32.5 29.9 %all-to-all-done.5 = bf16[16,8,2304]{2,1,0:T(8,128)(2,1)S(1)} async-done(((bf16[16,8,2304]{2,1,0:T(8,128)(2,1)}), bf16[16,8,2304]{2,1,0:T(8,128)(2,1)S(1)}, u32[]{:S(2)}, u32[]{:S(2)}) %all-to-all-start.5) | async-done | bytes 589856 | tf_op jit(solution)/shard_map/all_to_all | solution.py:190
  62.4 6.8 %all-to-all-start.4 = ((bf16[16,8,2304]{2,1,0:T(8,128)(2,1)}), bf16[16,8,2304]{2,1,0:T(8,128)(2,1)S(1)}, u32[]{:S(2)}, u32[]{:S(2)}) async-start(bf16[16,8,2304]{2,1,0:T(8,128)(2,1)} %maximum_bitcast_fusion.2), calls=%async_computation.4 | async-start | bytes 1179648 | tf_op jit(solution)/shard_map/all_to_all | solution.py:190
  69.2 2.4 collective-permute-start.1
  71.7 4.9 %collective-permute-start = (bf16[3584,128]{1,0:T(8,128)(2,1)S(1)}, bf16[3584,128]{1,0:T(8,128)(2,1)S(1)}, u32[]{:S(2)}, u32[]{:S(2)}) collective-permute-start(bf16[3584,128]{1,0:T(8,128)(2,1)S(1)} %bitcast.310), channel_id=1, source_target_pairs={{0,1},{1,0},{2,3},{3,2},{4,5},{5,4},{6,7},{7,6},{8,9},{9,8},{10,11... | collective-permute-start | bytes 2752520 | tf_op jit(solution)/shard_map/ppermute | solution.py:194
  76.6 2.4 collective-permute-start.2
  80.2 1.1 reshape.978
  82.2 18.6 %all-to-all-done.4 = bf16[16,8,2304]{2,1,0:T(8,128)(2,1)S(1)} async-done(((bf16[16,8,2304]{2,1,0:T(8,128)(2,1)}), bf16[16,8,2304]{2,1,0:T(8,128)(2,1)S(1)}, u32[]{:S(2)}, u32[]{:S(2)}) %all-to-all-start.4) | async-done | bytes 589856 | tf_op jit(solution)/shard_map/all_to_all | solution.py:190
  103.0 2.1 fusion.219
  105.1 10.6 %collective-permute-done = bf16[3584,128]{1,0:T(8,128)(2,1)S(1)} collective-permute-done((bf16[3584,128]{1,0:T(8,128)(2,1)S(1)}, bf16[3584,128]{1,0:T(8,128)(2,1)S(1)}, u32[]{:S(2)}, u32[]{:S(2)}) %collective-permute-start) | collective-permute-done | bytes 917536 | tf_op jit(solution)/shard_map/ppermute | solution.py:194
  116.2 17.7 %collective-permute-done.2 = bf16[128,3584]{1,0:T(8,128)(2,1)} collective-permute-done((bf16[128,3584]{1,0:T(8,128)(2,1)}, bf16[128,3584]{1,0:T(8,128)(2,1)}, u32[]{:S(2)}, u32[]{:S(2)}) %collective-permute-start.2) | collective-permute-done | bytes 917536 | tf_op jit(solution)/shard_map/ppermute | solution.py:196
  133.9 2.0 multiply_reduce_fusion.1
  135.9 2.2 fusion.144
  139.7 1.1 fusion.30
  140.8 12.2 %all-to-all-start.6 = ((bf16[16,8,2304]{2,1,0:T(8,128)(2,1)}), bf16[16,8,2304]{2,1,0:T(8,128)(2,1)S(1)}, u32[]{:S(2)}, u32[]{:S(2)}) async-start(bf16[16,8,2304]{2,1,0:T(8,128)(2,1)} %fusion.30), calls=%async_computation.6 | async-start | bytes 1179648 | tf_op jit(solution)/shard_map/all_to_all | solution.py:190
  154.9 28.1 %all-to-all-done.6 = bf16[16,8,2304]{2,1,0:T(8,128)(2,1)S(1)} async-done(((bf16[16,8,2304]{2,1,0:T(8,128)(2,1)}), bf16[16,8,2304]{2,1,0:T(8,128)(2,1)S(1)}, u32[]{:S(2)}, u32[]{:S(2)}) %all-to-all-start.6) | async-done | bytes 589856 | tf_op jit(solution)/shard_map/all_to_all | solution.py:190
  184.2 1.5 fusion.84
  190.1 40.5 %all_to_all.50 = bf16[16,8,2304]{2,1,0:T(8,128)(2,1)S(1)} all-to-all(bf16[16,8,2304]{2,1,0:T(8,128)(2,1)S(1)} %maximum_bitcast_fusion), channel_id=1, replica_groups={{0,2,4,6,8,10,12,14,16,18,20,22,24,26,28,30},{1,3,5,7,9,11,13,15,17,19,..., dimensions={0} | all-to-all | bytes 1179648 | tf_op jit(solution)/shard_map/all_to_all | solution.py:190
  232.5 3.4 convolution_convert_fusion.1
  236.4 1.1 fusion.33
  237.5 4.2 all-to-all-start.1
  243.2 29.2 %all-to-all-done.1 = bf16[16,8,2304]{2,1,0:T(8,128)(2,1)S(1)} async-done(((bf16[16,8,2304]{2,1,0:T(8,128)(2,1)}), bf16[16,8,2304]{2,1,0:T(8,128)(2,1)S(1)}, u32[]{:S(2)}, u32[]{:S(2)}) %all-to-all-start.1) | async-done | bytes 589856 | tf_op jit(solution)/shard_map/all_to_all | solution.py:190
  273.0 2.1 collective-permute-start.3
  276.1 2.4 collective-permute-done.3
  281.3 7.0 %all-to-all-start.2 = ((bf16[16,8,2304]{2,1,0:T(8,128)(2,1)}), bf16[16,8,2304]{2,1,0:T(8,128)(2,1)S(1)}, u32[]{:S(2)}, u32[]{:S(2)}) async-start(bf16[16,8,2304]{2,1,0:T(8,128)(2,1)} %maximum_bitcast_fusion.1), calls=%async_computation.2 | async-start | bytes 1179648 | tf_op jit(solution)/shard_map/all_to_all | solution.py:190
  288.5 1.9 collective-permute-start.4
  294.5 24.6 %all-to-all-done.2 = bf16[16,8,2304]{2,1,0:T(8,128)(2,1)S(1)} async-done(((bf16[16,8,2304]{2,1,0:T(8,128)(2,1)}), bf16[16,8,2304]{2,1,0:T(8,128)(2,1)S(1)}, u32[]{:S(2)}, u32[]{:S(2)}) %all-to-all-start.2) | async-done | bytes 589856 | tf_op jit(solution)/shard_map/all_to_all | solution.py:190
  319.1 6.9 %all-to-all-start.8 = ((bf16[16,8,2304]{2,1,0:T(8,128)(2,1)}), bf16[16,8,2304]{2,1,0:T(8,128)(2,1)S(1)}, u32[]{:S(2)}, u32[]{:S(2)}) async-start(bf16[16,8,2304]{2,1,0:T(8,128)(2,1)} %maximum_bitcast_fusion.5), calls=%async_computation.8 | async-start | bytes 1179648 | tf_op jit(solution)/shard_map/all_to_all | solution.py:190
  327.1 1.1 reshape.967
  329.7 3.4 convolution_convert_fusion
  333.7 1.1 reshape.970
  334.9 22.2 %all-to-all-done.8 = bf16[16,8,2304]{2,1,0:T(8,128)(2,1)S(1)} async-done(((bf16[16,8,2304]{2,1,0:T(8,128)(2,1)}), bf16[16,8,2304]{2,1,0:T(8,128)(2,1)S(1)}, u32[]{:S(2)}, u32[]{:S(2)}) %all-to-all-start.8) | async-done | bytes 589856 | tf_op jit(solution)/shard_map/all_to_all | solution.py:190
  357.9 6.8 %all-to-all-start.7 = ((bf16[16,8,2304]{2,1,0:T(8,128)(2,1)}), bf16[16,8,2304]{2,1,0:T(8,128)(2,1)S(1)}, u32[]{:S(2)}, u32[]{:S(2)}) async-start(bf16[16,8,2304]{2,1,0:T(8,128)(2,1)} %maximum_bitcast_fusion.4), calls=%async_computation.7 | async-start | bytes 1179648 | tf_op jit(solution)/shard_map/all_to_all | solution.py:190
  364.7 1.4 fusion.227
  367.0 1.1 reshape.989
  369.2 2.5 fusion.218
  371.7 1.1 fusion.222
  373.0 1.1 fusion.34
  374.0 21.8 %all-to-all-done.7 = bf16[16,8,2304]{2,1,0:T(8,128)(2,1)S(1)} async-done(((bf16[16,8,2304]{2,1,0:T(8,128)(2,1)}), bf16[16,8,2304]{2,1,0:T(8,128)(2,1)S(1)}, u32[]{:S(2)}, u32[]{:S(2)}) %all-to-all-start.7) | async-done | bytes 589856 | tf_op jit(solution)/shard_map/all_to_all | solution.py:190
  395.8 6.8 %all-to-all-start.3 = ((bf16[16,8,2304]{2,1,0:T(8,128)(2,1)}), bf16[16,8,2304]{2,1,0:T(8,128)(2,1)S(1)}, u32[]{:S(2)}, u32[]{:S(2)}) async-start(bf16[16,8,2304]{2,1,0:T(8,128)(2,1)} %fusion.34), calls=%async_computation.3 | async-start | bytes 1179648 | tf_op jit(solution)/shard_map/all_to_all | solution.py:190
  403.6 2.3 multiply_reduce_fusion
  405.9 2.2 fusion.145
  409.7 1.1 fusion.32
  410.7 23.0 %all-to-all-done.3 = bf16[16,8,2304]{2,1,0:T(8,128)(2,1)S(1)} async-done(((bf16[16,8,2304]{2,1,0:T(8,128)(2,1)}), bf16[16,8,2304]{2,1,0:T(8,128)(2,1)S(1)}, u32[]{:S(2)}, u32[]{:S(2)}) %all-to-all-start.3) | async-done | bytes 589856 | tf_op jit(solution)/shard_map/all_to_all | solution.py:190
  433.8 6.8 %all-to-all-start.9 = ((bf16[16,8,2304]{2,1,0:T(8,128)(2,1)}), bf16[16,8,2304]{2,1,0:T(8,128)(2,1)S(1)}, u32[]{:S(2)}, u32[]{:S(2)}) async-start(bf16[16,8,2304]{2,1,0:T(8,128)(2,1)} %fusion.32), calls=%async_computation.9 | async-start | bytes 1179648 | tf_op jit(solution)/shard_map/all_to_all | solution.py:190
  441.9 29.9 %all-to-all-done.9 = bf16[16,8,2304]{2,1,0:T(8,128)(2,1)S(1)} async-done(((bf16[16,8,2304]{2,1,0:T(8,128)(2,1)}), bf16[16,8,2304]{2,1,0:T(8,128)(2,1)S(1)}, u32[]{:S(2)}, u32[]{:S(2)}) %all-to-all-start.9) | async-done | bytes 589856 | tf_op jit(solution)/shard_map/all_to_all | solution.py:190
  (504 shorter events, 51.2 us)
Async XLA Ops:
  15.8 46.6 %all-to-all-start.5 = ((bf16[16,8,2304]{2,1,0:T(8,128)(2,1)}), bf16[16,8,2304]{2,1,0:T(8,128)(2,1)S(1)}, u32[]{:S(2)}, u32[]{:S(2)}) async-start(bf16[16,8,2304]{2,1,0:T(8,128)(2,1)} %maximum_bitcast_fusion.3), calls=%async_computation.5 | async-start | bytes 1179648 | tf_op jit(solution)/shard_map/all_to_all | solution.py:190
  31.7 40.0 %copy-start.1 = (bf16[1,3584,128]{2,1,0:T(8,128)(2,1)S(1)}, bf16[1,3584,128]{2,1,0:T(8,128)(2,1)}, u32[]{:S(2)}) copy-start(bf16[1,3584,128]{2,1,0:T(8,128)(2,1)} %param.25) | copy-start | bytes 2752516
  62.4 38.4 %all-to-all-start.4 = ((bf16[16,8,2304]{2,1,0:T(8,128)(2,1)}), bf16[16,8,2304]{2,1,0:T(8,128)(2,1)S(1)}, u32[]{:S(2)}, u32[]{:S(2)}) async-start(bf16[16,8,2304]{2,1,0:T(8,128)(2,1)} %maximum_bitcast_fusion.2), calls=%async_computation.4 | async-start | bytes 1179648 | tf_op jit(solution)/shard_map/all_to_all | solution.py:190
  69.2 33.8 %collective-permute-start.1 = (bf16[3584,128]{1,0:T(8,128)(2,1)}, bf16[3584,128]{1,0:T(8,128)(2,1)}, u32[]{:S(2)}, u32[]{:S(2)}) collective-permute-start(bf16[3584,128]{1,0:T(8,128)(2,1)} %bitcast.14), channel_id=1, source_target_pairs={{0,1},{1,0},{2,3},{3,2},{4,5},{5,4},{6,7},{7,6},{8,9},{9,8},{10,11... | collective-permute-start | bytes 2752520 | tf_op jit(solution)/shard_map/ppermute | solution.py:195
  71.7 44.1 %collective-permute-start = (bf16[3584,128]{1,0:T(8,128)(2,1)S(1)}, bf16[3584,128]{1,0:T(8,128)(2,1)S(1)}, u32[]{:S(2)}, u32[]{:S(2)}) collective-permute-start(bf16[3584,128]{1,0:T(8,128)(2,1)S(1)} %bitcast.310), channel_id=1, source_target_pairs={{0,1},{1,0},{2,3},{3,2},{4,5},{5,4},{6,7},{7,6},{8,9},{9,8},{10,11... | collective-permute-start | bytes 2752520 | tf_op jit(solution)/shard_map/ppermute | solution.py:194
  76.6 57.3 %collective-permute-start.2 = (bf16[128,3584]{1,0:T(8,128)(2,1)}, bf16[128,3584]{1,0:T(8,128)(2,1)}, u32[]{:S(2)}, u32[]{:S(2)}) collective-permute-start(bf16[128,3584]{1,0:T(8,128)(2,1)} %bitcast.371), channel_id=1, source_target_pairs={{0,1},{1,0},{2,3},{3,2},{4,5},{5,4},{6,7},{7,6},{8,9},{9,8},{10,11... | collective-permute-start | bytes 2752520 | tf_op jit(solution)/shard_map/ppermute | solution.py:196
  140.8 42.7 %copy-start.25 = (f32[8,2,5]{0,2,1:T(8,128)S(1)}, f32[8,2,5]{0,2,1:T(8,128)}, u32[]{:S(2)}) copy-start(f32[8,2,5]{0,2,1:T(8,128)} %copy-done.24) | copy-start | bytes 964
  140.8 42.7 %copy-start.39 = (f32[8,2,4]{0,2,1:T(4,128)S(1)}, f32[8,2,4]{0,2,1:T(4,128)}, u32[]{:S(2)}) copy-start(f32[8,2,4]{0,2,1:T(4,128)} %copy-done.38) | copy-start | bytes 772
  140.8 42.8 %copy-start.66 = (f32[8,2]{0,1:T(2,128)S(1)}, f32[8,2]{0,1:T(2,128)}, u32[]{:S(2)}) copy-start(f32[8,2]{0,1:T(2,128)} %get-tuple-element.71) | copy-start | bytes 196
  140.8 42.8 %copy-start.60 = (f32[8,2]{0,1:T(2,128)S(1)}, f32[8,2]{0,1:T(2,128)}, u32[]{:S(2)}) copy-start(f32[8,2]{0,1:T(2,128)} %copy-done.59) | copy-start | bytes 196
  140.8 42.8 %copy-start.64 = (f32[8]{0:T(128)S(1)}, f32[8]{0:T(128)}, u32[]{:S(2)}) copy-start(f32[8]{0:T(128)} %copy-done.63) | copy-start | bytes 100
  140.8 42.9 %copy-start.51 = (s32[8,2]{0,1:T(2,128)S(1)}, s32[8,2]{0,1:T(2,128)}, u32[]{:S(2)}) copy-start(s32[8,2]{0,1:T(2,128)} %copy-done.50) | copy-start | bytes 196
  140.8 42.2 %all-to-all-start.6 = ((bf16[16,8,2304]{2,1,0:T(8,128)(2,1)}), bf16[16,8,2304]{2,1,0:T(8,128)(2,1)S(1)}, u32[]{:S(2)}, u32[]{:S(2)}) async-start(bf16[16,8,2304]{2,1,0:T(8,128)(2,1)} %fusion.30), calls=%async_computation.6 | async-start | bytes 1179648 | tf_op jit(solution)/shard_map/all_to_all | solution.py:190
  153.5 30.7 %copy-start.3 = (bf16[2,1,8,3584]{3,2,1,0:T(8,128)(2,1)S(1)}, bf16[2,1,8,3584]{3,2,1,0:T(8,128)(2,1)}, u32[]{:S(2)}) copy-start(bf16[2,1,8,3584]{3,2,1,0:T(8,128)(2,1)} %param.19) | copy-start | bytes 344068
  154.8 32.2 %copy-start.48 = (s32[8,2]{0,1:T(2,128)S(1)}, s32[8,2]{0,1:T(2,128)}, u32[]{:S(2)}) copy-start(s32[8,2]{0,1:T(2,128)} %copy-done.47) | copy-start | bytes 196
  154.8 32.9 %copy-start.36 = (f32[8,2,4]{0,2,1:T(4,128)S(1)}, f32[8,2,4]{0,2,1:T(4,128)}, u32[]{:S(2)}) copy-start(f32[8,2,4]{0,2,1:T(4,128)} %get-tuple-element.160) | copy-start | bytes 772
  154.9 34.2 %copy-start.53 = (f32[2,2]{1,0:T(2,128)S(1)}, f32[2,2]{1,0:T(2,128)}, u32[]{:S(2)}) copy-start(f32[2,2]{1,0:T(2,128)} %copy-done.52) | copy-start | bytes 52
  237.5 35.4 %copy-start.11 = (bf16[1,8,3584]{2,1,0:T(8,128)(2,1)S(1)}, bf16[1,8,3584]{2,1,0:T(8,128)(2,1)}, u32[]{:S(2)}) copy-start(bf16[1,8,3584]{2,1,0:T(8,128)(2,1)} %param.18) | copy-start | bytes 172036
  237.5 34.9 %all-to-all-start.1 = ((bf16[16,8,2304]{2,1,0:T(8,128)(2,1)}), bf16[16,8,2304]{2,1,0:T(8,128)(2,1)S(1)}, u32[]{:S(2)}, u32[]{:S(2)}) async-start(bf16[16,8,2304]{2,1,0:T(8,128)(2,1)} %fusion.33), calls=%async_computation.1 | async-start | bytes 1179648 | tf_op jit(solution)/shard_map/all_to_all | solution.py:190
  241.7 33.4 %copy-start.76 = (f32[8]{0:T(128)S(1)}, f32[8]{0:T(128)}, u32[]{:S(2)}) copy-start(f32[8]{0:T(128)} %get-tuple-element.50) | copy-start | bytes 100
  241.7 33.5 %copy-start.28 = (bf16[4,2,4,2,8]{4,3,2,1,0:T(2,128)(2,1)S(1)}, bf16[4,2,4,2,8]{4,3,2,1,0:T(2,128)(2,1)}, u32[]{:S(2)}) copy-start(bf16[4,2,4,2,8]{4,3,2,1,0:T(2,128)(2,1)} %get-tuple-element.122) | copy-start | bytes 3076
  241.7 33.5 %copy-start.46 = (f32[4,5]{0,1:T(8,128)S(1)}, f32[4,5]{0,1:T(8,128)}, u32[]{:S(2)}) copy-start(f32[4,5]{0,1:T(8,128)} %get-tuple-element.55) | copy-start | bytes 244
  241.7 33.6 %copy-start.27 = (bf16[2,8,4,2,4]{1,3,4,0,2:T(2,128)(2,1)S(1)}, bf16[2,8,4,2,4]{1,3,4,0,2:T(2,128)(2,1)}, u32[]{:S(2)}) copy-start(bf16[2,8,4,2,4]{1,3,4,0,2:T(2,128)(2,1)} %get-tuple-element.121) | copy-start | bytes 3076
  241.8 36.9 %copy-start.6 = (bf16[1,8,3584]{2,1,0:T(8,128)(2,1)S(1)}, bf16[1,8,3584]{2,1,0:T(8,128)(2,1)}, u32[]{:S(2)}) copy-start(bf16[1,8,3584]{2,1,0:T(8,128)(2,1)} %param.20) | copy-start | bytes 172036
  241.8 36.9 %copy-start.12 = (f32[8,3584]{1,0:T(8,128)S(1)}, f32[8,3584]{1,0:T(8,128)}, u32[]{:S(2)}) copy-start(f32[8,3584]{1,0:T(8,128)} %get-tuple-element.155) | copy-start | bytes 344068
  241.8 36.9 %copy-start.69 = (f32[8]{0:T(128)S(1)}, f32[8]{0:T(128)}, u32[]{:S(2)}) copy-start(f32[8]{0:T(128)} %copy-done.68) | copy-start | bytes 100
  241.8 36.9 %copy-start.72 = (f32[8]{0:T(128)S(1)}, f32[8]{0:T(128)}, u32[]{:S(2)}) copy-start(f32[8]{0:T(128)} %copy-done.71) | copy-start | bytes 100
  241.8 36.9 %copy-start.75 = (f32[8]{0:T(128)S(1)}, f32[8]{0:T(128)}, u32[]{:S(2)}) copy-start(f32[8]{0:T(128)} %get-tuple-element.151) | copy-start | bytes 100
  273.0 5.5 %collective-permute-start.3 = (bf16[8,3584]{1,0:T(8,128)(2,1)S(1)}, bf16[8,3584]{1,0:T(8,128)(2,1)S(1)}, u32[]{:S(2)}, u32[]{:S(2)}) collective-permute-start(bf16[8,3584]{1,0:T(8,128)(2,1)S(1)} %fusion.73), channel_id=1, source_target_pairs={{480,0},{0,32},{32,64},{64,96},{96,128},{128,160},{160,192},{192,2... | collective-permute-start | bytes 172040 | tf_op jit(solution)/shard_map/ppermute | solution.py:12
  281.3 37.8 %all-to-all-start.2 = ((bf16[16,8,2304]{2,1,0:T(8,128)(2,1)}), bf16[16,8,2304]{2,1,0:T(8,128)(2,1)S(1)}, u32[]{:S(2)}, u32[]{:S(2)}) async-start(bf16[16,8,2304]{2,1,0:T(8,128)(2,1)} %maximum_bitcast_fusion.1), calls=%async_computation.2 | async-start | bytes 1179648 | tf_op jit(solution)/shard_map/all_to_all | solution.py:190
  288.5 4.6 collective-permute-start.4
  319.1 38.0 %all-to-all-start.8 = ((bf16[16,8,2304]{2,1,0:T(8,128)(2,1)}), bf16[16,8,2304]{2,1,0:T(8,128)(2,1)S(1)}, u32[]{:S(2)}, u32[]{:S(2)}) async-start(bf16[16,8,2304]{2,1,0:T(8,128)(2,1)} %maximum_bitcast_fusion.5), calls=%async_computation.8 | async-start | bytes 1179648 | tf_op jit(solution)/shard_map/all_to_all | solution.py:190
  357.9 37.9 %all-to-all-start.7 = ((bf16[16,8,2304]{2,1,0:T(8,128)(2,1)}), bf16[16,8,2304]{2,1,0:T(8,128)(2,1)S(1)}, u32[]{:S(2)}, u32[]{:S(2)}) async-start(bf16[16,8,2304]{2,1,0:T(8,128)(2,1)} %maximum_bitcast_fusion.4), calls=%async_computation.7 | async-start | bytes 1179648 | tf_op jit(solution)/shard_map/all_to_all | solution.py:190
  395.8 38.0 %all-to-all-start.3 = ((bf16[16,8,2304]{2,1,0:T(8,128)(2,1)}), bf16[16,8,2304]{2,1,0:T(8,128)(2,1)S(1)}, u32[]{:S(2)}, u32[]{:S(2)}) async-start(bf16[16,8,2304]{2,1,0:T(8,128)(2,1)} %fusion.34), calls=%async_computation.3 | async-start | bytes 1179648 | tf_op jit(solution)/shard_map/all_to_all | solution.py:190
  410.7 30.2 %copy-start.44 = (bf16[16,4,8]{0,2,1:T(8,128)(2,1)S(1)}, bf16[16,4,8]{0,2,1:T(8,128)(2,1)}, u32[]{:S(2)}) copy-start(bf16[16,4,8]{0,2,1:T(8,128)(2,1)} %convert_element_type.658) | copy-start | bytes 3076
  410.7 30.4 %copy-start.8 = (bf16[8,3584]{1,0:T(8,128)(2,1)S(1)}, bf16[8,3584]{1,0:T(8,128)(2,1)}, u32[]{:S(2)}) copy-start(bf16[8,3584]{1,0:T(8,128)(2,1)} %copy-done.7) | copy-start | bytes 172036
  433.8 38.0 %all-to-all-start.9 = ((bf16[16,8,2304]{2,1,0:T(8,128)(2,1)}), bf16[16,8,2304]{2,1,0:T(8,128)(2,1)S(1)}, u32[]{:S(2)}, u32[]{:S(2)}) async-start(bf16[16,8,2304]{2,1,0:T(8,128)(2,1)} %fusion.32), calls=%async_computation.9 | async-start | bytes 1179648 | tf_op jit(solution)/shard_map/all_to_all | solution.py:190
  440.6 31.7 %copy-start.37 = (f32[8,2,4]{0,2,1:T(4,128)S(1)}, f32[8,2,4]{0,2,1:T(4,128)}, u32[]{:S(2)}) copy-start(f32[8,2,4]{0,2,1:T(4,128)} %get-tuple-element.160) | copy-start | bytes 772
  440.6 31.7 %copy-start.65 = (f32[8,2]{0,1:T(2,128)S(1)}, f32[8,2]{0,1:T(2,128)}, u32[]{:S(2)}) copy-start(f32[8,2]{0,1:T(2,128)} %get-tuple-element.69) | copy-start | bytes 196
  440.6 31.8 %copy-start.56 = (f32[8,2]{0,1:T(2,128)S(1)}, f32[8,2]{0,1:T(2,128)}, u32[]{:S(2)}) copy-start(f32[8,2]{0,1:T(2,128)} %copy-done.55) | copy-start | bytes 196
  440.6 31.8 %copy-start.62 = (f32[8]{0:T(128)S(1)}, f32[8]{0:T(128)}, u32[]{:S(2)}) copy-start(f32[8]{0:T(128)} %copy-done.61) | copy-start | bytes 100
  440.6 31.8 %copy-start.49 = (s32[8,2]{0,1:T(2,128)S(1)}, s32[8,2]{0,1:T(2,128)}, u32[]{:S(2)}) copy-start(s32[8,2]{0,1:T(2,128)} %copy-done.47) | copy-start | bytes 196
  440.6 31.8 %copy-start.43 = (bf16[56,4,8]{0,2,1:T(8,128)(2,1)S(1)}, bf16[56,4,8]{0,2,1:T(8,128)(2,1)}, u32[]{:S(2)}) copy-start(bf16[56,4,8]{0,2,1:T(8,128)(2,1)} %convert_element_type.756) | copy-start | bytes 10756
  440.6 32.0 %copy-start.42 = (bf16[16,4,8]{0,2,1:T(8,128)(2,1)S(1)}, bf16[16,4,8]{0,2,1:T(8,128)(2,1)}, u32[]{:S(2)}) copy-start(bf16[16,4,8]{0,2,1:T(8,128)(2,1)} %convert_element_type.728) | copy-start | bytes 3076
  441.1 31.8 %copy-start.4 = (bf16[2,1,8,3584]{3,2,1,0:T(8,128)(2,1)S(1)}, bf16[2,1,8,3584]{3,2,1,0:T(8,128)(2,1)}, u32[]{:S(2)}) copy-start(bf16[2,1,8,3584]{3,2,1,0:T(8,128)(2,1)} %param.19) | copy-start | bytes 344068
  441.2 32.2 %copy-start.10 = (bf16[8,3584]{1,0:T(8,128)(2,1)S(1)}, bf16[8,3584]{1,0:T(8,128)(2,1)}, u32[]{:S(2)}) copy-start(bf16[8,3584]{1,0:T(8,128)(2,1)} %copy-done.9) | copy-start | bytes 172036
  441.2 32.2 %copy-start.70 = (f32[8]{0:T(128)S(1)}, f32[8]{0:T(128)}, u32[]{:S(2)}) copy-start(f32[8]{0:T(128)} %copy-done.68) | copy-start | bytes 100
  441.2 32.2 %copy-start.74 = (f32[8]{0:T(128)S(1)}, f32[8]{0:T(128)}, u32[]{:S(2)}) copy-start(f32[8]{0:T(128)} %get-tuple-element.149) | copy-start | bytes 100
  (44 other events, 289.4 us)

commit v2 on v1

--- a/solution.py
+++ b/solution.py
@@ -138,11 +138,11 @@
     return close_slabs(out, slabs.shape[0])
 
 
-def expert_backward(saved_slabs, cot_slabs, gate_w, up_w, down_w):
+def expert_backward(saved_slabs, cot_slabs, part, parts, gate_w, up_w, down_w):
     sources = saved_slabs.shape[0]
     rows = open_slabs(saved_slabs)
     cot = open_slabs(cot_slabs)
-    gb = in_row_order(slot_scalars(cot_slabs, 5))
+    gb = in_row_order(slot_scalars(saved_slabs, 5))
     gate_pre = jnp.dot(rows, gate_w, preferred_element_type=F32)
     up_pre = jnp.dot(rows, up_w, preferred_element_type=F32)
     gate_sig = jax.nn.sigmoid(gate_pre)
@@ -157,8 +157,10 @@
     row_grad = row_grad + jnp.einsum("rf,df->rd", up_grad, up_w, preferred_element_type=F32)
     dgate = in_slot_order(dgate, sources)
     high = lax.reduce_precision(dgate, 8, 7)
-    low = dgate - high
-    return close_slabs(row_grad.astype(BF16), sources, jnp.concatenate([high, low], axis=1))
+    both = jnp.concatenate([high, dgate - high], axis=1)
+    mine = (jnp.arange(parts) == part).astype(F32)
+    scalars = (mine[None, :, None] * both[:, None, :]).reshape(sources, -1)
+    return close_slabs(row_grad.astype(BF16), sources, scalars)
 
 
 def local(
@@ -183,62 +185,98 @@
     ranks = lax.axis_size("expert")
     depth = ranks // 2
     copies = depth // experts
-    columns = [[x + 2 * z for z in range(depth)] for x in range(2)]
     partner = [(i, i ^ 1) for i in range(ranks)]
-
-    def exchange(slabs):
+    far = [[x + 2 * (p + copies * e) for e in range(experts)] for p in range(copies) for x in range(2)]
+    near = [[x + 2 * (p + copies * e) for p in range(copies)] for e in range(experts) for x in range(2)]
+    part = lax.axis_index("expert") // 2 % copies
+
+    def swap(slabs, groups):
         return lax.all_to_all(
-            slabs, "expert", split_axis=0, concat_axis=0, axis_index_groups=columns, tiled=True
+            slabs, "expert", split_axis=0, concat_axis=0, axis_index_groups=groups, tiled=True
         )
 
-    gate_w = jnp.concatenate([w_gate[0], lax.ppermute(w_gate[0], "expert", partner)], axis=1)
-    up_w = jnp.concatenate([w_up[0], lax.ppermute(w_up[0], "expert", partner)], axis=1)
-    down_w = jnp.concatenate([w_down[0], lax.ppermute(w_down[0], "expert", partner)], axis=0)
-
-    forward_in = fwd_tokens[0]
-    cotan_in = cotangent[0]
+    def dispatch(*slabs):
+        held = swap(jnp.concatenate(slabs, axis=1), far)
+        spread = swap(jnp.broadcast_to(held[None], (copies,) + held.shape), near)
+        spread = spread.reshape((depth,) + held.shape[1:])
+        return [spread[:, 8 * i:8 * i + 8] for i in range(len(slabs))]
+
+    def gather_back(*slabs):
+        parts = jnp.concatenate(slabs, axis=1)
+        parts = swap(parts.reshape((copies, experts) + parts.shape[1:]), near)
+        held = swap(jnp.sum(parts.astype(F32), axis=0).astype(BF16), far)
+        return [held[:, 8 * i:8 * i + 8] for i in range(len(slabs))]
+
+    def after(value, *earlier):
+        return lax.optimization_barrier((value,) + earlier)[0]
+
+    gate_r = lax.ppermute(w_gate[0], "expert", partner)
+    up_r = lax.ppermute(w_up[0], "expert", partner)
+    down_r = lax.ppermute(w_down[0], "expert", partner)
+
     expert_ids = jnp.arange(experts, dtype=jnp.int32)
-    saved_parts = []
-    for t in range(ticks):
+    fwd_places = [slot_places(fwd_routes[t, 0], experts, cap) for t in range(ticks)]
+    bwd_places = [slot_places(bwd_routes[t, 0], experts, cap) for t in range(ticks)]
+    fwd_spreads = [jnp.sum(place, axis=1) for place in fwd_places]
+    bwd_spreads = [jnp.sum(place, axis=1) for place in bwd_places]
+
+    def pack_saved(t):
         saved = saved_tokens[t, 0]
         saved_norm = norm_rows(saved, gain).astype(BF16)
         pick = (bwd_routes[t, 0][..., None] == expert_ids).astype(F32)
-        place = slot_places(bwd_routes[t, 0], experts, cap)
         chosen, total, share = gate_values(saved_norm, router_w, pick)
         gb = share.astype(BF16).astype(F32)
-        spread = jnp.sum(place, axis=1)
-        slot_gb = jnp.sum(place * gb[:, :, None, None], axis=(0, 1))
-        saved_parts.append((saved, saved_norm, pick, place, chosen, total, share, spread, slot_gb))
-
-    for t in range(ticks):
-        saved, saved_norm, pick, place, chosen, total, share, spread, slot_gb = saved_parts[t]
-        normed = norm_rows(forward_in, gain).astype(BF16)
-        place_f = slot_places(fwd_routes[t, 0], experts, cap)
-        pick_f = (fwd_routes[t, 0][..., None] == expert_ids).astype(F32)
-        rows_f = exchange(pack_rows(normed, jnp.sum(place_f, axis=1), copies))
-        rows_m = exchange(pack_rows(saved_norm, spread, copies))
-        rows_c = exchange(pack_rows(cotan_in, spread, copies, slot_gb))
-        _, _, share_f = gate_values(normed, router_w, pick_f)
-        gb_f = share_f.astype(BF16).astype(F32)
-        weights_f = jnp.sum(place_f * gb_f[:, :, None, None], axis=1)
-        back_f = exchange(expert_forward(rows_f, gate_w, up_w, down_w))
-        back_b = exchange(expert_backward(rows_m, rows_c, gate_w, up_w, down_w))
-
-        fwd_result = (forward_in.astype(F32) + combine_rows(back_f, weights_f)).astype(BF16)
-
-        row_sum = combine_rows(back_b, spread)
-        slot_dgate = slot_scalars(back_b, cap) + slot_scalars(back_b, cap, cap)
-        slot_dgate = jnp.sum(slot_dgate.reshape(experts, copies, cap), axis=1)
-        dgate = jnp.sum(place * slot_dgate, axis=(2, 3))
+        slot_gb = jnp.sum(bwd_places[t] * gb[:, :, None, None], axis=(0, 1))
+        slabs = pack_rows(saved_norm, bwd_spreads[t], 1, slot_gb)
+        return slabs, (saved, pick, chosen, total, share)
+
+    def finish_forward(t, tokens_in, normed, back):
+        pick = (fwd_routes[t, 0][..., None] == expert_ids).astype(F32)
+        _, _, share = gate_values(normed, router_w, pick)
+        gb = share.astype(BF16).astype(F32)
+        weights = jnp.sum(fwd_places[t] * gb[:, :, None, None], axis=1)
+        return (tokens_in.astype(F32) + combine_rows(back, weights)).astype(BF16)
+
+    def finish_backward(t, cot, parts, back):
+        saved, pick, chosen, total, share = parts
+        row_sum = combine_rows(back, bwd_spreads[t])
+        slot_dgate = slot_scalars(back, copies * 2 * cap).reshape(experts, copies * 2, cap).sum(axis=1)
+        dgate = jnp.sum(bwd_places[t] * slot_dgate, axis=(2, 3))
         dchosen = (dgate - jnp.sum(share * dgate, axis=-1, keepdims=True)) / total
         logit_grad = dchosen * chosen * (1.0 - chosen)
         logit_full = jnp.sum(logit_grad[:, :, None] * pick, axis=1)
         router_back = jnp.dot(logit_full, router_w.astype(F32).T, precision=lax.Precision.HIGHEST)
-        pulled = norm_pull(saved, gain, row_sum + router_back)
-        bwd_result = (cotan_in.astype(F32) + pulled).astype(BF16)
+        return (cot.astype(F32) + norm_pull(saved, gain, row_sum + router_back)).astype(BF16)
+
+    forward_in = fwd_tokens[0]
+    cotan_in = cotangent[0]
+    normed = norm_rows(forward_in, gain).astype(BF16)
+    packed = [pack_saved(t) for t in range(ticks)]
+    rows_f, rows_c, *rows_m = dispatch(
+        pack_rows(normed, fwd_spreads[0], 1),
+        pack_rows(cotan_in, bwd_spreads[0], 1),
+        *[slabs for slabs, _ in packed],
+    )
+    weights = (
+        jnp.concatenate([w_gate[0], gate_r], axis=1),
+        jnp.concatenate([w_up[0], up_r], axis=1),
+        jnp.concatenate([w_down[0], down_r], axis=0),
+    )
+    for t in range(ticks):
+        back_f, back_b = gather_back(
+            expert_forward(rows_f, *weights),
+            expert_backward(rows_m[t], rows_c, part, copies, *weights),
+        )
+        fwd_result = finish_forward(t, forward_in, normed, back_f)
+        bwd_result = finish_backward(t, cotan_in, packed[t][1], back_b)
         if t + 1 < ticks:
             forward_in = shift(fwd_result, "pipe", 1)
             cotan_in = shift(bwd_result, "pipe", -1)
+            normed = norm_rows(forward_in, gain).astype(BF16)
+            rows_f, rows_c = dispatch(
+                pack_rows(normed, fwd_spreads[t + 1], 1),
+                pack_rows(cotan_in, bwd_spreads[t + 1], 1),
+            )
     return (fwd_result[None], bwd_result[None])
 
 

time: 476 us -> 370 us (0.78)
  the two profiles are of different devices: /device:TPU:44 before, /device:TPU:62 now
where the time goes in v2:
time: 370 us; the launch traced here: 368 us
  blocking collectives  140 us (38%)
  waiting for transfers between devices  103 us (28%)
  matrix products  37.8 us (10%)
  starting transfers between devices  32.7 us (9%)
  local copies, waits for them, and re-layouts  32.6 us (9%)
  other arithmetic  18.8 us (5%)
    all_to_all x4, blocking collectives, swap(): lax.all_to_all(slabs, 'expert', split_axis=0, concat_axis=0, axis_index_g...  140 us
    all_to_all x4, waiting for transfers between devices, swap(): lax.all_to_all(slabs, 'expert', split_axis=0, concat_axis=0, axis_index_g...  98.6 us
    all_to_all x4, starting transfers between devices, swap(): lax.all_to_all(slabs, 'expert', split_axis=0, concat_axis=0, axis_index_g...  18.2 us
    unnamed x236, local copies, waits for them, and re-layouts  10.2 us
  transfers between devices with their start and end apart: 9, of which 6 were waited for; matrix products, arithmetic and copies ran while one was open for 8% of the time, Pallas kernels for 0%

profile of v2, /device:TPU:62, one launch (start us, length us, event | category | flops | bytes accessed | tf_op | source)
XLA Modules:
  0.0 368.0 jit_solution(17262864773408854669)
XLA Ops:
  0.7 1.0 fusion.65
  4.0 1.0 fusion.32
  5.0 1.0 fusion.29
  7.1 1.0 fusion.35
  11.8 1.2 slice_bitcast_fusion.17
  17.7 49.6 %all_to_all.40 = bf16[4,32,2304]{2,1,0:T(8,128)(2,1)S(1)} all-to-all(bf16[4,32,2304]{2,1,0:T(8,128)(2,1)S(1)} %pad_maximum_fusion.3), channel_id=1, replica_groups={{0,8,16,24},{1,9,17,25},{2,10,18,26},{3,11,19,27},{4,12,20,28},{5,13,21..., dimensions={0} | all-to-all | bytes 1179648 | tf_op jit(solution)/shard_map/all_to_all | solution.py:194
  67.3 1.7 broadcast_in_dim.12
  69.0 3.9 %all-to-all-start.1 = ((bf16[4,4,32,2304]{3,2,1,0:T(8,128)(2,1)}), bf16[4,4,32,2304]{3,2,1,0:T(8,128)(2,1)S(1)}, u32[]{:S(2)}, u32[]{:S(2)}) async-start(bf16[4,4,32,2304]{3,2,1,0:T(8,128)(2,1)} %broadcast_in_dim.12), calls=%async_computation.1 | async-start | bytes 4718592 | tf_op jit(solution)/shard_map/all_to_all | solution.py:194
  72.9 3.3 collective-permute-start.1
  76.2 4.0 %collective-permute-start = (bf16[3584,128]{1,0:T(8,128)(2,1)S(1)}, bf16[3584,128]{1,0:T(8,128)(2,1)}, u32[]{:S(2)}, u32[]{:S(2)}) collective-permute-start(bf16[3584,128]{1,0:T(8,128)(2,1)S(1)} %bitcast.295), channel_id=1, source_target_pairs={{0,1},{1,0},{2,3},{3,2},{4,5},{5,4},{6,7},{7,6},{8,9},{9,8},{10,11... | collective-permute-start | bytes 2752520 | tf_op jit(solution)/shard_map/ppermute | solution.py:213
  80.2 3.3 collective-permute-start.2
  84.3 38.1 %all-to-all-done.1 = bf16[4,4,32,2304]{3,2,1,0:T(8,128)(2,1)S(1)} async-done(((bf16[4,4,32,2304]{3,2,1,0:T(8,128)(2,1)}), bf16[4,4,32,2304]{3,2,1,0:T(8,128)(2,1)S(1)}, u32[]{:S(2)}, u32[]{:S(2)}) %all-to-all-start.1) | async-done | bytes 2359328 | tf_op jit(solution)/shard_map/all_to_all | solution.py:194
  122.4 1.5 fusion.231
  125.7 1.9 reshape.894
  127.7 2.0 pad_maximum_fusion.6
  129.7 1.9 reshape.897
  131.6 1.8 constant_dynamic-update-slice_fusion.31
  133.4 1.6 copy.217
  135.0 1.6 copy.216
  138.3 1.6 constant_dynamic-update-slice_fusion.30
  139.9 2.1 fusion.223
  142.0 1.8 fusion.227
  143.9 2.0 multiply_reduce_fusion.1
  145.9 1.9 fusion.141
  147.8 2.0 fusion
  150.9 1.7 fusion.228
  152.6 3.3 convolution_convert_fusion.1
  159.0 32.0 %all_to_all.41 = bf16[4,4,16,2304]{3,2,1,0:T(8,128)(2,1)S(1)} all-to-all(bf16[4,4,16,2304]{3,2,1,0:T(8,128)(2,1)S(1)} %bitcast.293), channel_id=1, replica_groups={{0,2,4,6},{1,3,5,7},{8,10,12,14},{9,11,13,15},{16,18,20,22},{17,19,21,2..., dimensions={0} | all-to-all | bytes 2359296 | tf_op jit(solution)/shard_map/all_to_all | solution.py:194
  192.0 3.5 all-to-all-start.3
  197.0 17.7 %all-to-all-done.3 = bf16[4,16,2304]{2,1,0:T(8,128)(2,1)S(1)} async-done(((bf16[4,16,2304]{2,1,0:T(8,128)(2,1)}), bf16[4,16,2304]{2,1,0:T(8,128)(2,1)S(1)}, u32[]{:S(2)}, u32[]{:S(2)}) %all-to-all-start.3) | async-done | bytes 294944 | tf_op jit(solution)/shard_map/all_to_all | solution.py:194
  215.3 1.9 collective-permute-start.3
  217.9 2.9 collective-permute-done.3
  224.1 1.9 collective-permute-start.4
  226.4 1.5 collective-permute-done.4
  228.5 25.7 %all_to_all.42 = bf16[4,16,2304]{2,1,0:T(8,128)(2,1)S(1)} all-to-all(bf16[4,16,2304]{2,1,0:T(8,128)(2,1)S(1)} %pad_maximum_fusion.10), channel_id=1, replica_groups={{0,8,16,24},{1,9,17,25},{2,10,18,26},{3,11,19,27},{4,12,20,28},{5,13,21..., dimensions={0} | all-to-all | bytes 589824 | tf_op jit(solution)/shard_map/all_to_all | solution.py:194
  254.2 1.1 broadcast_in_dim.14
  255.4 7.2 %all-to-all-start.5 = ((bf16[4,4,16,2304]{3,2,1,0:T(8,128)(2,1)}), bf16[4,4,16,2304]{3,2,1,0:T(8,128)(2,1)S(1)}, u32[]{:S(2)}, u32[]{:S(2)}) async-start(bf16[4,4,16,2304]{3,2,1,0:T(8,128)(2,1)} %broadcast_in_dim.14), calls=%async_computation.5 | async-start | bytes 2359296 | tf_op jit(solution)/shard_map/all_to_all | solution.py:194
  263.4 1.9 fusion.221
  265.4 2.3 fusion.225
  267.7 21.5 %all-to-all-done.5 = bf16[4,4,16,2304]{3,2,1,0:T(8,128)(2,1)S(1)} async-done(((bf16[4,4,16,2304]{3,2,1,0:T(8,128)(2,1)}), bf16[4,4,16,2304]{3,2,1,0:T(8,128)(2,1)S(1)}, u32[]{:S(2)}, u32[]{:S(2)}) %all-to-all-start.5) | async-done | bytes 1179680 | tf_op jit(solution)/shard_map/all_to_all | solution.py:194
  289.9 2.3 multiply_reduce_fusion
  292.3 1.9 fusion.142
  294.2 1.9 fusion.1
  297.8 1.7 fusion.226
  299.5 3.4 convolution_convert_fusion
  305.7 32.8 %all_to_all.43 = bf16[4,4,16,2304]{3,2,1,0:T(8,128)(2,1)S(1)} all-to-all(bf16[4,4,16,2304]{3,2,1,0:T(8,128)(2,1)S(1)} %bitcast.294), channel_id=1, replica_groups={{0,2,4,6},{1,3,5,7},{8,10,12,14},{9,11,13,15},{16,18,20,22},{17,19,21,2..., dimensions={0} | all-to-all | bytes 2359296 | tf_op jit(solution)/shard_map/all_to_all | solution.py:194
  339.5 3.6 all-to-all-start.7
  343.5 21.4 %all-to-all-done.7 = bf16[4,16,2304]{2,1,0:T(8,128)(2,1)S(1)} async-done(((bf16[4,16,2304]{2,1,0:T(8,128)(2,1)}), bf16[4,16,2304]{2,1,0:T(8,128)(2,1)S(1)}, u32[]{:S(2)}, u32[]{:S(2)}) %all-to-all-start.7) | async-done | bytes 294944 | tf_op jit(solution)/shard_map/all_to_all | solution.py:194
  (485 shorter events, 36.9 us)
Async XLA Ops:
  0.6 13.7 %copy-start.11 = (bf16[1,8,3584]{2,1,0:T(8,128)(2,1)S(1)}, bf16[1,8,3584]{2,1,0:T(8,128)(2,1)}, u32[]{:S(2)}) copy-start(bf16[1,8,3584]{2,1,0:T(8,128)(2,1)} %param.20) | copy-start | bytes 172036
  8.1 9.2 %copy-start.40 = (f32[8,7]{1,0:T(8,128)}, f32[8,7]{1,0:T(8,128)S(1)}, u32[]{:S(2)}) copy-start(f32[8,7]{1,0:T(8,128)S(1)} %fusion.191) | copy-start | bytes 676
  16.1 51.2 %copy-start.27 = (bf16[32,56]{1,0:T(8,128)(2,1)}, bf16[32,56]{1,0:T(8,128)(2,1)S(1)}, u32[]{:S(2)}) copy-start(bf16[32,56]{1,0:T(8,128)(2,1)S(1)} %convert_element_type.611) | copy-start | bytes 10756
  16.3 51.0 %copy-start.29 = (bf16[32,16]{1,0:T(8,128)(2,1)}, bf16[32,16]{1,0:T(8,128)(2,1)S(1)}, u32[]{:S(2)}) copy-start(bf16[32,16]{1,0:T(8,128)(2,1)S(1)} %convert_element_type.604) | copy-start | bytes 3076
  69.0 53.4 %all-to-all-start.1 = ((bf16[4,4,32,2304]{3,2,1,0:T(8,128)(2,1)}), bf16[4,4,32,2304]{3,2,1,0:T(8,128)(2,1)S(1)}, u32[]{:S(2)}, u32[]{:S(2)}) async-start(bf16[4,4,32,2304]{3,2,1,0:T(8,128)(2,1)} %broadcast_in_dim.12), calls=%async_computation.1 | async-start | bytes 4718592 | tf_op jit(solution)/shard_map/all_to_all | solution.py:194
  72.9 67.0 %collective-permute-start.1 = (bf16[3584,128]{1,0:T(8,128)(2,1)}, bf16[3584,128]{1,0:T(8,128)(2,1)}, u32[]{:S(2)}, u32[]{:S(2)}) collective-permute-start(bf16[3584,128]{1,0:T(8,128)(2,1)} %bitcast.330), channel_id=1, source_target_pairs={{0,1},{1,0},{2,3},{3,2},{4,5},{5,4},{6,7},{7,6},{8,9},{9,8},{10,11... | collective-permute-start | bytes 2752520 | tf_op jit(solution)/shard_map/ppermute | solution.py:214
  76.2 65.8 %collective-permute-start = (bf16[3584,128]{1,0:T(8,128)(2,1)S(1)}, bf16[3584,128]{1,0:T(8,128)(2,1)}, u32[]{:S(2)}, u32[]{:S(2)}) collective-permute-start(bf16[3584,128]{1,0:T(8,128)(2,1)S(1)} %bitcast.295), channel_id=1, source_target_pairs={{0,1},{1,0},{2,3},{3,2},{4,5},{5,4},{6,7},{7,6},{8,9},{9,8},{10,11... | collective-permute-start | bytes 2752520 | tf_op jit(solution)/shard_map/ppermute | solution.py:213
  80.2 63.6 %collective-permute-start.2 = (bf16[128,3584]{1,0:T(8,128)(2,1)}, bf16[128,3584]{1,0:T(8,128)(2,1)}, u32[]{:S(2)}, u32[]{:S(2)}) collective-permute-start(bf16[128,3584]{1,0:T(8,128)(2,1)} %bitcast.337), channel_id=1, source_target_pairs={{0,1},{1,0},{2,3},{3,2},{4,5},{5,4},{6,7},{7,6},{8,9},{9,8},{10,11... | collective-permute-start | bytes 2752520 | tf_op jit(solution)/shard_map/ppermute | solution.py:215
  158.9 37.4 %copy-start.38 = (bf16[2,8,4,2,4]{1,0,4,3,2:T(2,128)(2,1)S(1)}, bf16[2,8,4,2,4]{1,0,4,3,2:T(2,128)(2,1)}, u32[]{:S(2)}) copy-start(bf16[2,8,4,2,4]{1,0,4,3,2:T(2,128)(2,1)} %get-tuple-element.152) | copy-start | bytes 3076
  158.9 37.5 %copy-start.74 = (s32[1,1,8,2]{2,3,1,0:T(2,128)S(1)}, s32[1,1,8,2]{2,3,1,0:T(2,128)}, u32[]{:S(2)}) copy-start(s32[1,1,8,2]{2,3,1,0:T(2,128)} %get-tuple-element.147) | copy-start | bytes 196
  159.0 38.0 %copy-start.37 = (bf16[2,8,4,2,4]{1,0,4,3,2:T(2,128)(2,1)S(1)}, bf16[2,8,4,2,4]{1,0,4,3,2:T(2,128)(2,1)}, u32[]{:S(2)}) copy-start(bf16[2,8,4,2,4]{1,0,4,3,2:T(2,128)(2,1)} %get-tuple-element.151) | copy-start | bytes 3076
  191.0 24.3 %copy-start.15 = (bf16[1,8,3584]{2,1,0:T(8,128)(2,1)S(1)}, bf16[1,8,3584]{2,1,0:T(8,128)(2,1)}, u32[]{:S(2)}) copy-start(bf16[1,8,3584]{2,1,0:T(8,128)(2,1)} %param.18) | copy-start | bytes 172036
  191.0 26.5 %copy-start.34 = (f32[8,2,5]{0,2,1:T(8,128)S(1)}, f32[8,2,5]{0,2,1:T(8,128)}, u32[]{:S(2)}) copy-start(f32[8,2,5]{0,2,1:T(8,128)} %copy-done.33) | copy-start | bytes 964
  191.0 26.5 %copy-start.43 = (f32[8,2,4]{0,2,1:T(4,128)S(1)}, f32[8,2,4]{0,2,1:T(4,128)}, u32[]{:S(2)}) copy-start(f32[8,2,4]{0,2,1:T(4,128)} %copy-done.42) | copy-start | bytes 772
  191.0 26.6 %copy-start.73 = (f32[8,2]{0,1:T(2,128)S(1)}, f32[8,2]{0,1:T(2,128)}, u32[]{:S(2)}) copy-start(f32[8,2]{0,1:T(2,128)} %get-tuple-element.69) | copy-start | bytes 196
  191.0 26.6 %copy-start.57 = (f32[8,2]{0,1:T(2,128)S(1)}, f32[8,2]{0,1:T(2,128)}, u32[]{:S(2)}) copy-start(f32[8,2]{0,1:T(2,128)} %copy-done.56) | copy-start | bytes 196
  191.0 26.6 %copy-start.69 = (f32[8]{0:T(128)S(1)}, f32[8]{0:T(128)}, u32[]{:S(2)}) copy-start(f32[8]{0:T(128)} %copy-done.68) | copy-start | bytes 100
  192.0 25.9 %copy-start.53 = (s32[8,2]{0,1:T(2,128)S(1)}, s32[8,2]{0,1:T(2,128)}, u32[]{:S(2)}) copy-start(s32[8,2]{0,1:T(2,128)} %copy-done.52) | copy-start | bytes 196
  192.0 29.3 %copy-start.59 = (s32[8,2]{0,1:T(2,128)S(1)}, s32[8,2]{0,1:T(2,128)}, u32[]{:S(2)}) copy-start(s32[8,2]{0,1:T(2,128)} %copy-done.58) | copy-start | bytes 196
  192.0 29.3 %copy-start.49 = (f32[8,2,4]{0,2,1:T(4,128)S(1)}, f32[8,2,4]{0,2,1:T(4,128)}, u32[]{:S(2)}) copy-start(f32[8,2,4]{0,2,1:T(4,128)} %get-tuple-element.171) | copy-start | bytes 772
  192.0 29.4 %copy-start.71 = (f32[2,2]{0,1:T(2,128)S(1)}, f32[2,2]{0,1:T(2,128)}, u32[]{:S(2)}) copy-start(f32[2,2]{0,1:T(2,128)} %copy-done.70) | copy-start | bytes 52
  192.0 30.3 %copy-start.41 = (f32[8,7]{1,0:T(8,128)S(1)}, f32[8,7]{1,0:T(8,128)}, u32[]{:S(2)}) copy-start(f32[8,7]{1,0:T(8,128)} %copy-done.40) | copy-start | bytes 676
  192.0 22.8 %all-to-all-start.3 = ((bf16[4,16,2304]{2,1,0:T(8,128)(2,1)}), bf16[4,16,2304]{2,1,0:T(8,128)(2,1)S(1)}, u32[]{:S(2)}, u32[]{:S(2)}) async-start(bf16[4,16,2304]{2,1,0:T(8,128)(2,1)} %reduce_sum.375), calls=%async_computation.3 | async-start | bytes 589824 | tf_op jit(solution)/shard_map/all_to_all | solution.py:194
  195.5 27.0 %copy-start.46 = (f32[8,4]{0,1:T(4,128)S(1)}, f32[8,4]{0,1:T(4,128)}, u32[]{:S(2)}) copy-start(f32[8,4]{0,1:T(4,128)} %copy-done.45) | copy-start | bytes 388
  195.5 27.0 %copy-start.48 = (f32[8,4]{0,1:T(4,128)S(1)}, f32[8,4]{0,1:T(4,128)}, u32[]{:S(2)}) copy-start(f32[8,4]{0,1:T(4,128)} %copy-done.47) | copy-start | bytes 388
  197.0 26.6 %copy-start.4 = (bf16[2,1,8,3584]{3,2,1,0:T(8,128)(2,1)S(1)}, bf16[2,1,8,3584]{3,2,1,0:T(8,128)(2,1)}, u32[]{:S(2)}) copy-start(bf16[2,1,8,3584]{3,2,1,0:T(8,128)(2,1)} %param.19) | copy-start | bytes 344068
  215.0 9.0 %copy-start.12 = (bf16[1,8,3584]{2,1,0:T(8,128)(2,1)S(1)}, bf16[1,8,3584]{2,1,0:T(8,128)(2,1)}, u32[]{:S(2)}) copy-start(bf16[1,8,3584]{2,1,0:T(8,128)(2,1)} %param.20) | copy-start | bytes 172036
  215.0 9.0 %copy-start.63 = (f32[8]{0:T(128)S(1)}, f32[8]{0:T(128)}, u32[]{:S(2)}) copy-start(f32[8]{0:T(128)} %copy-done.62) | copy-start | bytes 100
  215.3 12.6 %copy-start.28 = (bf16[32,56]{1,0:T(8,128)(2,1)S(1)}, bf16[32,56]{1,0:T(8,128)(2,1)}, u32[]{:S(2)}) copy-start(bf16[32,56]{1,0:T(8,128)(2,1)} %copy-done.27) | copy-start | bytes 10756
  215.3 5.5 %collective-permute-start.3 = (bf16[8,3584]{1,0:T(8,128)(2,1)S(1)}, bf16[8,3584]{1,0:T(8,128)(2,1)S(1)}, u32[]{:S(2)}, u32[]{:S(2)}) collective-permute-start(bf16[8,3584]{1,0:T(8,128)(2,1)S(1)} %fusion.62), channel_id=1, source_target_pairs={{480,0},{0,32},{32,64},{64,96},{96,128},{128,160},{160,192},{192,2... | collective-permute-start | bytes 172040 | tf_op jit(solution)/shard_map/ppermute | solution.py:12
  217.7 10.4 %copy-start.30 = (bf16[32,16]{1,0:T(8,128)(2,1)S(1)}, bf16[32,16]{1,0:T(8,128)(2,1)}, u32[]{:S(2)}) copy-start(bf16[32,16]{1,0:T(8,128)(2,1)} %copy-done.29) | copy-start | bytes 3076
  224.1 3.7 %collective-permute-start.4 = (bf16[8,3584]{1,0:T(8,128)(2,1)S(1)}, bf16[8,3584]{1,0:T(8,128)(2,1)S(1)}, u32[]{:S(2)}, u32[]{:S(2)}) collective-permute-start(bf16[8,3584]{1,0:T(8,128)(2,1)S(1)} %fusion.72), channel_id=1, source_target_pairs={{32,0},{64,32},{96,64},{128,96},{160,128},{192,160},{224,192},{256... | collective-permute-start | bytes 172040 | tf_op jit(solution)/shard_map/ppermute | solution.py:12
  255.4 33.8 %all-to-all-start.5 = ((bf16[4,4,16,2304]{3,2,1,0:T(8,128)(2,1)}), bf16[4,4,16,2304]{3,2,1,0:T(8,128)(2,1)S(1)}, u32[]{:S(2)}, u32[]{:S(2)}) async-start(bf16[4,4,16,2304]{3,2,1,0:T(8,128)(2,1)} %broadcast_in_dim.14), calls=%async_computation.5 | async-start | bytes 2359296 | tf_op jit(solution)/shard_map/all_to_all | solution.py:194
  265.4 24.5 %copy-start.24 = (f32[80,256]{1,0:T(8,128)}, f32[80,256]{1,0:T(8,128)S(1)}, u32[]{:S(2)}) copy-start(f32[80,256]{1,0:T(8,128)S(1)} %fusion.221) | copy-start | bytes 245764
  305.7 37.5 %copy-start.36 = (bf16[2,8,4,2,4]{1,0,4,3,2:T(2,128)(2,1)S(1)}, bf16[2,8,4,2,4]{1,0,4,3,2:T(2,128)(2,1)}, u32[]{:S(2)}) copy-start(bf16[2,8,4,2,4]{1,0,4,3,2:T(2,128)(2,1)} %get-tuple-element.131) | copy-start | bytes 3076
  305.7 37.5 %copy-start.22 = (bf16[7,8,4,8]{1,0,3,2:T(8,128)(2,1)S(1)}, bf16[7,8,4,8]{1,0,3,2:T(8,128)(2,1)}, u32[]{:S(2)}) copy-start(bf16[7,8,4,8]{1,0,3,2:T(8,128)(2,1)} %get-tuple-element.135) | copy-start | bytes 10756
  305.7 37.6 %copy-start.35 = (bf16[2,8,4,2,4]{1,0,4,3,2:T(2,128)(2,1)S(1)}, bf16[2,8,4,2,4]{1,0,4,3,2:T(2,128)(2,1)}, u32[]{:S(2)}) copy-start(bf16[2,8,4,2,4]{1,0,4,3,2:T(2,128)(2,1)} %get-tuple-element.153) | copy-start | bytes 3076
  305.7 37.7 %copy-start.21 = (bf16[7,8,4,8]{1,0,3,2:T(8,128)(2,1)S(1)}, bf16[7,8,4,8]{1,0,3,2:T(8,128)(2,1)}, u32[]{:S(2)}) copy-start(bf16[7,8,4,8]{1,0,3,2:T(8,128)(2,1)} %get-tuple-element.137) | copy-start | bytes 10756
  338.5 26.9 %copy-start.32 = (f32[8,2,5]{0,2,1:T(8,128)S(1)}, f32[8,2,5]{0,2,1:T(8,128)}, u32[]{:S(2)}) copy-start(f32[8,2,5]{0,2,1:T(8,128)} %copy-done.31) | copy-start | bytes 964
  338.5 26.9 %copy-start.72 = (f32[8,2]{0,1:T(2,128)S(1)}, f32[8,2]{0,1:T(2,128)}, u32[]{:S(2)}) copy-start(f32[8,2]{0,1:T(2,128)} %get-tuple-element.71) | copy-start | bytes 196
  338.5 27.0 %copy-start.55 = (f32[8,2]{0,1:T(2,128)S(1)}, f32[8,2]{0,1:T(2,128)}, u32[]{:S(2)}) copy-start(f32[8,2]{0,1:T(2,128)} %copy-done.54) | copy-start | bytes 196
  338.5 27.0 %copy-start.67 = (f32[8]{0:T(128)S(1)}, f32[8]{0:T(128)}, u32[]{:S(2)}) copy-start(f32[8]{0:T(128)} %copy-done.66) | copy-start | bytes 100
  338.5 27.0 %copy-start.51 = (s32[8,2]{0,1:T(2,128)S(1)}, s32[8,2]{0,1:T(2,128)}, u32[]{:S(2)}) copy-start(s32[8,2]{0,1:T(2,128)} %copy-done.50) | copy-start | bytes 196
  339.5 27.1 %copy-start.14 = (bf16[8,3584]{1,0:T(8,128)(2,1)S(1)}, bf16[8,3584]{1,0:T(8,128)(2,1)}, u32[]{:S(2)}) copy-start(bf16[8,3584]{1,0:T(8,128)(2,1)} %copy-done.13) | copy-start | bytes 172036
  339.5 27.1 %copy-start.61 = (f32[8]{0:T(128)S(1)}, f32[8]{0:T(128)}, u32[]{:S(2)}) copy-start(f32[8]{0:T(128)} %copy-done.60) | copy-start | bytes 100
  339.5 27.1 %copy-start.75 = (f32[8]{0:T(128)S(1)}, f32[8]{0:T(128)}, u32[]{:S(2)}) copy-start(f32[8]{0:T(128)} %get-tuple-element.168) | copy-start | bytes 100
  339.5 27.9 %copy-start.17 = (bf16[8,3584]{1,0:T(8,128)(2,1)S(1)}, bf16[8,3584]{1,0:T(8,128)(2,1)}, u32[]{:S(2)}) copy-start(bf16[8,3584]{1,0:T(8,128)(2,1)} %copy-done.16) | copy-start | bytes 172036
  339.5 25.4 %all-to-all-start.7 = ((bf16[4,16,2304]{2,1,0:T(8,128)(2,1)}), bf16[4,16,2304]{2,1,0:T(8,128)(2,1)S(1)}, u32[]{:S(2)}, u32[]{:S(2)}) async-start(bf16[4,16,2304]{2,1,0:T(8,128)(2,1)} %reduce_sum.388), calls=%async_computation.7 | async-start | bytes 589824 | tf_op jit(solution)/shard_map/all_to_all | solution.py:194
  (46 other events, 141.3 us)

commit v3 on v2

--- a/solution.py
+++ b/solution.py
@@ -1,6 +1,10 @@
+import functools
+
 import jax
 import jax.numpy as jnp
 from jax import lax
+from jax.experimental import pallas as pl
+from jax.experimental.pallas import tpu as pltpu
 from jax.sharding import PartitionSpec as P
 
 BF16 = jnp.bfloat16
@@ -94,73 +98,148 @@
     return unpieces(sum_main, 2) + unpieces(sum_tail, 7)
 
 
-def open_slabs(slabs):
-    sources, _, full = slabs.shape
-    half = full * 7 // 9
-    first = jnp.concatenate([slabs[:, 0:4, :half], slabs[:, 4:8, :half]], axis=2)
-    last = slabs[:, 0:7, half:].reshape(sources, -1)
-    return jnp.concatenate([first.reshape(sources * 4, -1), last], axis=0)
-
-
-def close_slabs(rows, sources, scalars=None):
-    width = rows.shape[1]
-    half, piece = slab_sizes(width)
-    first = rows[:sources * 4].reshape(sources, 4, width)
-    main = jnp.concatenate([first[:, :, :half], first[:, :, half:]], axis=1)
-    last = rows[sources * 4:].reshape(sources, 7, piece)
-    extra = jnp.zeros((sources, 1, piece), BF16)
+def slot_scalars(slabs, count):
+    half = slabs.shape[2] * 7 // 9
+    return slabs[:, 7, half:half + count].astype(F32)
+
+
+SOURCES = 16
+
+
+def iota(shape, dim):
+    return lax.broadcasted_iota(jnp.int32, shape, dim)
+
+
+def one_hot(wanted, held):
+    return jnp.where(wanted == held, 1.0, 0.0).astype(BF16)
+
+
+def main_place(r):
+    return (((r >> 2) & (SOURCES - 1)) << 3) | ((r >> 6) << 2) | (r & 3)
+
+
+def tail_place(r):
+    return ((r & (SOURCES - 1)) << 3) | (r >> 4)
+
+
+def row_source(r):
+    return jnp.where(r < 4 * SOURCES, r >> 2, r - 4 * SOURCES)
+
+
+def row_slot(r):
+    return jnp.where(r < 4 * SOURCES, r & 3, 4)
+
+
+def dot(left, right, left_dim=1, right_dim=0):
+    return lax.dot_general(
+        left, right, (((left_dim,), (right_dim,)), ((), ())), preferred_element_type=F32
+    )
+
+
+def unpack(slabs, rows_ref):
+    half, piece = slab_sizes(rows_ref.shape[1])
+    count = 4 * SOURCES
+    pick = one_hot(main_place(iota((2 * count, 8 * SOURCES), 0)), iota((2 * count, 8 * SOURCES), 1))
+    main = dot(pick, slabs[:, :half]).astype(BF16)
+    rows_ref[:count, :half] = main[:count]
+    rows_ref[:count, half:] = main[count:]
+    pick = one_hot(tail_place(iota((7 * SOURCES, 8 * SOURCES), 0)), iota((7 * SOURCES, 8 * SOURCES), 1))
+    tail = dot(pick, slabs[:, half:]).astype(BF16)
+    for i in range(7):
+        rows_ref[count:, i * piece:(i + 1) * piece] = tail[i * SOURCES:(i + 1) * SOURCES]
+
+
+def pack(rows, keep_ref, send_ref, scalars=None):
+    half, piece = slab_sizes(rows.shape[1])
+    count = 4 * SOURCES
+    stacked = jnp.concatenate([rows[:count, :half], rows[:count, half:]], axis=0)
+    pick = one_hot(main_place(iota((8 * SOURCES, 2 * count), 1)), iota((8 * SOURCES, 2 * count), 0))
+    main = dot(pick, stacked).astype(BF16)
+    stacked = jnp.concatenate([rows[count:, i * piece:(i + 1) * piece] for i in range(7)], axis=0)
+    pick = one_hot(tail_place(iota((8 * SOURCES, 7 * SOURCES), 1)), iota((8 * SOURCES, 7 * SOURCES), 0))
+    tail = dot(pick, stacked)
+    mid = keep_ref.shape[0]
+    keep_ref[:, :half] = main[:mid]
+    send_ref[:, :half] = main[mid:]
+    lanes = 0
     if scalars is not None:
-        extra = extra.at[:, 0, :scalars.shape[1]].set(scalars.astype(BF16))
-    tail = jnp.concatenate([last, extra], axis=1)
-    return jnp.concatenate([main, tail], axis=2)
-
-
-def slot_scalars(slabs, count, first=0):
-    half = slabs.shape[2] * 7 // 9
-    return slabs[:, 7, half + first:half + first + count].astype(F32)
-
-
-def in_row_order(per_slot):
-    sources = per_slot.shape[0]
-    return jnp.concatenate([per_slot[:, :4].reshape(sources * 4), per_slot[:, 4]])
-
-
-def in_slot_order(per_row, sources):
-    return jnp.concatenate([per_row[:sources * 4].reshape(sources, 4), per_row[sources * 4:, None]], axis=1)
-
-
-def expert_forward(slabs, gate_w, up_w, down_w):
-    rows = open_slabs(slabs)
-    gate_pre = jnp.dot(rows, gate_w, preferred_element_type=F32)
-    up_pre = jnp.dot(rows, up_w, preferred_element_type=F32)
-    hidden = (jax.nn.silu(gate_pre) * up_pre).astype(BF16)
-    out = jnp.dot(hidden, down_w, preferred_element_type=F32).astype(BF16)
-    return close_slabs(out, slabs.shape[0])
-
-
-def expert_backward(saved_slabs, cot_slabs, part, parts, gate_w, up_w, down_w):
-    sources = saved_slabs.shape[0]
-    rows = open_slabs(saved_slabs)
-    cot = open_slabs(cot_slabs)
-    gb = in_row_order(slot_scalars(saved_slabs, 5))
-    gate_pre = jnp.dot(rows, gate_w, preferred_element_type=F32)
-    up_pre = jnp.dot(rows, up_w, preferred_element_type=F32)
+        lanes = scalars.shape[1]
+        first = (tail[:, :lanes] + scalars).astype(BF16)
+        keep_ref[:, half:half + lanes] = first[:mid]
+        send_ref[:, half:half + lanes] = first[mid:]
+    tail = tail[:, lanes:].astype(BF16)
+    keep_ref[:, half + lanes:] = tail[:mid]
+    send_ref[:, half + lanes:] = tail[mid:]
+
+
+def forward_kernel(near_ref, other_ref, gate_ref, up_ref, down_ref, keep_ref, send_ref, rows_ref):
+    unpack(jnp.concatenate([near_ref[...], other_ref[...]], axis=0), rows_ref)
+    rows = rows_ref[...]
+    gate_pre = dot(rows, gate_ref[...])
+    up_pre = dot(rows, up_ref[...])
+    hidden = (gate_pre * jax.nn.sigmoid(gate_pre) * up_pre).astype(BF16)
+    pack(dot(hidden, down_ref[...]).astype(BF16), keep_ref, send_ref)
+
+
+def backward_kernel(
+    tick, tokens, ticks, part_ref, saved_ref, near_ref, other_ref, gate_ref, up_ref, down_ref,
+    keep_ref, send_ref, rows_ref,
+):
+    part = part_ref[0]
+    slabs = jnp.concatenate([near_ref[...], other_ref[...]], axis=0)
+    count = 5 * SOURCES
+    half = slab_sizes(rows_ref.shape[1])[0]
+    lanes = 128
+    pick = one_hot((row_source(iota((count, 8 * SOURCES), 0)) << 3) | 7, iota((count, 8 * SOURCES), 1))
+    scalars = dot(pick, slabs[:, half:half + lanes])
+    slot = row_slot(iota((count, lanes), 0))
+    lane = iota((count, lanes), 1)
+    gb = jnp.sum(jnp.where(lane == slot, scalars, 0.0), axis=1, keepdims=True)
+    token = jnp.sum(jnp.where(lane == slot + 5, scalars, 0.0), axis=1, keepdims=True).astype(jnp.int32)
+    source = row_source(iota((count, 1), 0))
+    away = (((source >> 2) & 1) << 1) | (source >> 3)
+    depth_place = (away ^ part) + ((source & 3) << 2)
+    first = depth_place * (ticks * tokens) + tick * tokens
+    wanted = jnp.where(token < 0, -1, first + token)
+    pick = one_hot(wanted, iota((count, saved_ref.shape[0]), 1))
+    rows = dot(pick, saved_ref[...]).astype(BF16)
+    unpack(slabs, rows_ref)
+    cot_hidden = dot(rows_ref[...], down_ref[...], 1, 1)
+    gate_pre = dot(rows, gate_ref[...])
+    up_pre = dot(rows, up_ref[...])
     gate_sig = jax.nn.sigmoid(gate_pre)
     gate_act = gate_pre * gate_sig
     hidden = (gate_act * up_pre).astype(BF16).astype(F32)
-    cot_hidden = jnp.einsum("rd,fd->rf", cot, down_w, preferred_element_type=F32)
-    dgate = jnp.sum(hidden * cot_hidden, axis=1)
-    hidden_grad = cot_hidden * gb[:, None]
+    dgate = jnp.sum(hidden * cot_hidden, axis=1, keepdims=True)
+    hidden_grad = cot_hidden * gb
     gate_grad = (hidden_grad * up_pre * gate_sig * (1.0 + gate_pre * (1.0 - gate_sig))).astype(BF16)
     up_grad = (hidden_grad * gate_act).astype(BF16)
-    row_grad = jnp.einsum("rf,df->rd", gate_grad, gate_w, preferred_element_type=F32)
-    row_grad = row_grad + jnp.einsum("rf,df->rd", up_grad, up_w, preferred_element_type=F32)
-    dgate = in_slot_order(dgate, sources)
-    high = lax.reduce_precision(dgate, 8, 7)
-    both = jnp.concatenate([high, dgate - high], axis=1)
-    mine = (jnp.arange(parts) == part).astype(F32)
-    scalars = (mine[None, :, None] * both[:, None, :]).reshape(sources, -1)
-    return close_slabs(row_grad.astype(BF16), sources, scalars)
+    grad = dot(gate_grad, gate_ref[...], 1, 1) + dot(up_grad, up_ref[...], 1, 1)
+    high = dgate.astype(BF16).astype(F32)
+    own = lane - part * 10
+    both = jnp.where(own == slot, high, jnp.where(own == slot + 5, dgate - high, 0.0)).astype(BF16)
+    place = one_hot((row_source(iota((8 * SOURCES, count), 1)) << 3) | 7, iota((8 * SOURCES, count), 0))
+    pack(grad.astype(BF16), keep_ref, send_ref, dot(place, both))
+
+
+def run_kernel(kernel, slabs, operands, width, products, scalars=()):
+    near, other = [slab.reshape(-1, slab.shape[2]) for slab in slabs]
+    vmem = pl.BlockSpec(memory_space=pltpu.VMEM)
+    inputs = [*operands[:-3], near, other, *operands[-3:]]
+    moved = sum(value.size * value.dtype.itemsize for value in inputs) + 2 * near.size * 2
+    units = operands[-1].shape[0]
+    out = pl.pallas_call(
+        kernel,
+        out_shape=[jax.ShapeDtypeStruct(near.shape, BF16)] * 2,
+        in_specs=[pl.BlockSpec(memory_space=pltpu.SMEM)] * len(scalars) + [vmem] * len(inputs),
+        out_specs=[vmem] * 2,
+        scratch_shapes=[pltpu.VMEM((5 * SOURCES, width), BF16)],
+        compiler_params=pltpu.CompilerParams(vmem_limit_bytes=16 << 20),
+        cost_estimate=pl.CostEstimate(
+            flops=2 * products * 5 * SOURCES * width * units, bytes_accessed=moved, transcendentals=0
+        ),
+    )(*scalars, *inputs)
+    return [value.reshape(slabs[0].shape) for value in out]
 
 
 def local(
@@ -178,7 +257,7 @@
     gain = norm_gain[0]
     router_w = router[0]
     ticks = saved_tokens.shape[0]
-    tokens = fwd_tokens.shape[1]
+    tokens, width = fwd_tokens.shape[1:]
     top = fwd_routes.shape[-1]
     experts = router_w.shape[1]
     cap = 5 * tokens * top // (4 * experts)
@@ -187,7 +266,7 @@
     copies = depth // experts
     partner = [(i, i ^ 1) for i in range(ranks)]
     far = [[x + 2 * (p + copies * e) for e in range(experts)] for p in range(copies) for x in range(2)]
-    near = [[x + 2 * (p + copies * e) for p in range(copies)] for e in range(experts) for x in range(2)]
+    column = [[x + 2 * z for z in range(depth)] for x in range(2)]
     part = lax.axis_index("expert") // 2 % copies
 
     def swap(slabs, groups):
@@ -195,24 +274,38 @@
             slabs, "expert", split_axis=0, concat_axis=0, axis_index_groups=groups, tiled=True
         )
 
-    def dispatch(*slabs):
-        held = swap(jnp.concatenate(slabs, axis=1), far)
-        spread = swap(jnp.broadcast_to(held[None], (copies,) + held.shape), near)
-        spread = spread.reshape((depth,) + held.shape[1:])
-        return [spread[:, 8 * i:8 * i + 8] for i in range(len(slabs))]
-
-    def gather_back(*slabs):
-        parts = jnp.concatenate(slabs, axis=1)
-        parts = swap(parts.reshape((copies, experts) + parts.shape[1:]), near)
-        held = swap(jnp.sum(parts.astype(F32), axis=0).astype(BF16), far)
-        return [held[:, 8 * i:8 * i + 8] for i in range(len(slabs))]
-
     def after(value, *earlier):
         return lax.optimization_barrier((value,) + earlier)[0]
 
-    gate_r = lax.ppermute(w_gate[0], "expert", partner)
-    up_r = lax.ppermute(w_up[0], "expert", partner)
-    down_r = lax.ppermute(w_down[0], "expert", partner)
+    def across(value, bit):
+        return lax.ppermute(value, "expert", [(i, i ^ (2 * bit)) for i in range(ranks)])
+
+    def spread_near(held, then=()):
+        near = after(jnp.concatenate([held, across(held, 2)], axis=0), *then)
+        return near, across(near, 1)
+
+    def add(left, right):
+        return (left.astype(F32) + right.astype(F32)).astype(BF16)
+
+    def gather_near(keep, send):
+        parts = add(keep, across(send, 1))
+        count = parts.shape[0] // 2
+        return add(parts[:count], across(parts[count:], 2))
+
+    def dispatch(*slabs, first=(), then=((), ())):
+        held = swap(after(jnp.concatenate(slabs, axis=1), *first), far)
+        return [spread_near(held[:, 8 * i:8 * i + 8], then[i]) for i in range(len(slabs))]
+
+    def gather_back(*slabs):
+        held = swap(jnp.concatenate([gather_near(*slab) for slab in slabs], axis=1), far)
+        return [held[:, 8 * i:8 * i + 8] for i in range(len(slabs))]
+
+    half = w_gate.shape[1] // 2
+    gate_r0 = lax.ppermute(w_gate[0, :half], "expert", partner)
+    gate_r1 = lax.ppermute(after(w_gate[0, half:], gate_r0), "expert", partner)
+    up_r = lax.ppermute(after(w_up[0], gate_r0), "expert", partner)
+    down_r = lax.ppermute(after(w_down[0], gate_r1, up_r), "expert", partner)
+    gate_r = jnp.concatenate([gate_r0, gate_r1], axis=0)
 
     expert_ids = jnp.arange(experts, dtype=jnp.int32)
     fwd_places = [slot_places(fwd_routes[t, 0], experts, cap) for t in range(ticks)]
@@ -220,15 +313,17 @@
     fwd_spreads = [jnp.sum(place, axis=1) for place in fwd_places]
     bwd_spreads = [jnp.sum(place, axis=1) for place in bwd_places]
 
-    def pack_saved(t):
+    def saved_parts(t):
         saved = saved_tokens[t, 0]
         saved_norm = norm_rows(saved, gain).astype(BF16)
         pick = (bwd_routes[t, 0][..., None] == expert_ids).astype(F32)
         chosen, total, share = gate_values(saved_norm, router_w, pick)
         gb = share.astype(BF16).astype(F32)
         slot_gb = jnp.sum(bwd_places[t] * gb[:, :, None, None], axis=(0, 1))
-        slabs = pack_rows(saved_norm, bwd_spreads[t], 1, slot_gb)
-        return slabs, (saved, pick, chosen, total, share)
+        ids = jnp.arange(1, tokens + 1, dtype=F32)
+        slot_token = jnp.sum(bwd_spreads[t] * ids[:, None, None], axis=0) - 1.0
+        scalars = jnp.concatenate([slot_gb, slot_token], axis=1)
+        return saved_norm, scalars, (saved, pick, chosen, total, share)
 
     def finish_forward(t, tokens_in, normed, back):
         pick = (fwd_routes[t, 0][..., None] == expert_ids).astype(F32)
@@ -250,12 +345,16 @@
 
     forward_in = fwd_tokens[0]
     cotan_in = cotangent[0]
+    saved = [saved_parts(t) for t in range(ticks)]
+    saved_rows = lax.all_gather(
+        jnp.concatenate([one[0] for one in saved], axis=0), "expert", axis_index_groups=column, tiled=True
+    )
     normed = norm_rows(forward_in, gain).astype(BF16)
-    packed = [pack_saved(t) for t in range(ticks)]
-    rows_f, rows_c, *rows_m = dispatch(
+    rows_f, rows_c = dispatch(
         pack_rows(normed, fwd_spreads[0], 1),
-        pack_rows(cotan_in, bwd_spreads[0], 1),
-        *[slabs for slabs, _ in packed],
+        pack_rows(cotan_in, bwd_spreads[0], 1, saved[0][1]),
+        first=(gate_r0,),
+        then=((gate_r1, up_r), (saved_rows,)),
     )
     weights = (
         jnp.concatenate([w_gate[0], gate_r], axis=1),
@@ -264,18 +363,21 @@
     )
     for t in range(ticks):
         back_f, back_b = gather_back(
-            expert_forward(rows_f, *weights),
-            expert_backward(rows_m[t], rows_c, part, copies, *weights),
+            run_kernel(forward_kernel, rows_f, weights, width, 3),
+            run_kernel(
+                functools.partial(backward_kernel, t, tokens, ticks),
+                rows_c, (saved_rows,) + weights, width, 5, (part.reshape(1),),
+            ),
         )
         fwd_result = finish_forward(t, forward_in, normed, back_f)
-        bwd_result = finish_backward(t, cotan_in, packed[t][1], back_b)
+        bwd_result = finish_backward(t, cotan_in, saved[t][2], back_b)
         if t + 1 < ticks:
             forward_in = shift(fwd_result, "pipe", 1)
             cotan_in = shift(bwd_result, "pipe", -1)
             normed = norm_rows(forward_in, gain).astype(BF16)
             rows_f, rows_c = dispatch(
                 pack_rows(normed, fwd_spreads[t + 1], 1),
-                pack_rows(cotan_in, bwd_spreads[t + 1], 1),
+                pack_rows(cotan_in, bwd_spreads[t + 1], 1, saved[t + 1][1]),
             )
     return (fwd_result[None], bwd_result[None])
 

time: 370 us -> 301 us (0.81)
  the two profiles are of different devices: /device:TPU:62 before, /device:TPU:18 now
where the time goes in v3:
time: 301 us; the launch traced here: 300 us
  waiting for transfers between devices  123 us (41%)
  starting transfers between devices  88 us (29%)
  blocking collectives  25.3 us (8%)
  other arithmetic  18 us (6%)
  between operations  15.9 us (5%)
  local copies, waits for them, and re-layouts  14.9 us (5%)
  Pallas kernels  10.3 us (3%)
  matrix products  4.64 us (2%)
    all_to_all x3, waiting for transfers between devices, swap(): lax.all_to_all(slabs, 'expert', split_axis=0, concat_axis=0, axis_index_g...  51.2 us
    ppermute x16, waiting for transfers between devices, across(): lax.ppermute(value, 'expert', [(i, i ^ 2 * bit) for i in range(ranks)])  50.4 us
    ppermute x16, starting transfers between devices, across(): lax.ppermute(value, 'expert', [(i, i ^ 2 * bit) for i in range(ranks)])  47.5 us
    all_to_all x1, blocking collectives, swap(): lax.all_to_all(slabs, 'expert', split_axis=0, concat_axis=0, axis_index_g...  25.3 us
    all_to_all x3, starting transfers between devices, swap(): lax.all_to_all(slabs, 'expert', split_axis=0, concat_axis=0, axis_index_g...  22.1 us
    all_gather x1, waiting for transfers between devices, local(): lax.all_gather(jnp.concatenate([one[0] for one in saved], axis=0), 'exper...  16.2 us
    pallas_call x4, Pallas kernels, run_kernel(): pl.pallas_call(kernel, out_shape=[jax.ShapeDtypeStruct(near.shape, BF16)]...  10.3 us
  transfers between devices with their start and end apart: 26, of which 19 were waited for; matrix products, arithmetic and copies ran while one was open for 8% of the time, Pallas kernels for 3%

profile of v3, /device:TPU:18, one launch (start us, length us, event | category | flops | bytes accessed | tf_op | source)
XLA Modules:
  0.0 299.8 jit_solution(15576464318541891222)
XLA Ops:
  8.6 4.0 %collective-permute-start = (bf16[1792,128]{1,0:T(8,128)(2,1)S(1)}, bf16[1792,128]{1,0:T(8,128)(2,1)S(1)}, u32[]{:S(2)}, u32[]{:S(2)}) collective-permute-start(bf16[1792,128]{1,0:T(8,128)(2,1)S(1)} %get-tuple-element.79), channel_id=1, source_target_pairs={{0,1},{1,0},{2,3},{3,2},{4,5},{5,4},{6,7},{7,6},{8,9},{9,8},{10,11... | collective-permute-start | bytes 1376264 | tf_op jit(solution)/shard_map/ppermute | solution.py:304
  24.2 4.0 %collective-permute-start.2 = (bf16[1792,128]{1,0:T(8,128)(2,1)S(1)}, bf16[1792,128]{1,0:T(8,128)(2,1)}, u32[]{:S(2)}, u32[]{:S(2)}) collective-permute-start(bf16[1792,128]{1,0:T(8,128)(2,1)S(1)} %get-tuple-element.41), channel_id=1, source_target_pairs={{0,1},{1,0},{2,3},{3,2},{4,5},{5,4},{6,7},{7,6},{8,9},{9,8},{10,11... | collective-permute-start | bytes 1376264 | tf_op jit(solution)/shard_map/ppermute | solution.py:305
  29.0 15.1 %all-to-all-start = ((bf16[4,16,2304]{2,1,0:T(8,128)(2,1)}), bf16[4,16,2304]{2,1,0:T(8,128)(2,1)S(1)}, u32[]{:S(2)}, u32[]{:S(2)}) async-start(bf16[4,16,2304]{2,1,0:T(8,128)(2,1)} %pad_maximum_fusion.2), calls=%async_computation | async-start | bytes 589824 | tf_op jit(solution)/shard_map/all_to_all | solution.py:273
  45.3 3.3 %collective-permute-start.3 = (bf16[3584,128]{1,0:T(8,128)(2,1)}, bf16[3584,128]{1,0:T(8,128)(2,1)}, u32[]{:S(2)}, u32[]{:S(2)}) collective-permute-start(bf16[3584,128]{1,0:T(8,128)(2,1)} %bitcast.21), channel_id=1, source_target_pairs={{0,1},{1,0},{2,3},{3,2},{4,5},{5,4},{6,7},{7,6},{8,9},{9,8},{10,11... | collective-permute-start | bytes 2752520 | tf_op jit(solution)/shard_map/ppermute | solution.py:306
  48.6 1.5 maximum_maximum_fusion.gate_ref
  50.2 18.1 %all-to-all-done = bf16[4,16,2304]{2,1,0:T(8,128)(2,1)S(1)} async-done(((bf16[4,16,2304]{2,1,0:T(8,128)(2,1)}), bf16[4,16,2304]{2,1,0:T(8,128)(2,1)S(1)}, u32[]{:S(2)}, u32[]{:S(2)}) %all-to-all-start) | async-done | bytes 294944 | tf_op jit(solution)/shard_map/all_to_all | solution.py:273
  68.3 3.4 %collective-permute-start.1 = (bf16[4,8,2304]{2,1,0:T(8,128)(2,1)S(1)}, bf16[4,8,2304]{2,1,0:T(8,128)(2,1)S(1)}, u32[]{:S(2)}, u32[]{:S(2)}) collective-permute-start(bf16[4,8,2304]{2,1,0:T(8,128)(2,1)S(1)} %get-tuple-element.86), channel_id=1, source_target_pairs={{0,4},{1,5},{2,6},{3,7},{4,0},{5,1},{6,2},{7,3},{8,12},{9,13},{10,... | collective-permute-start | bytes 442376 | tf_op jit(solution)/shard_map/ppermute | solution.py:281
  71.7 3.4 %collective-permute-start.8 = (bf16[4,8,2304]{2,1,0:T(8,128)(2,1)S(1)}, bf16[4,8,2304]{2,1,0:T(8,128)(2,1)S(1)}, u32[]{:S(2)}, u32[]{:S(2)}) collective-permute-start(bf16[4,8,2304]{2,1,0:T(8,128)(2,1)S(1)} %get-tuple-element.87), channel_id=1, source_target_pairs={{0,4},{1,5},{2,6},{3,7},{4,0},{5,1},{6,2},{7,3},{8,12},{9,13},{10,... | collective-permute-start | bytes 442376 | tf_op jit(solution)/shard_map/ppermute | solution.py:281
  75.1 3.0 %collective-permute-start.5 = (bf16[128,3584]{1,0:T(8,128)(2,1)}, bf16[128,3584]{1,0:T(8,128)(2,1)}, u32[]{:S(2)}, u32[]{:S(2)}) collective-permute-start(bf16[128,3584]{1,0:T(8,128)(2,1)} %bitcast.279), channel_id=1, source_target_pairs={{0,1},{1,0},{2,3},{3,2},{4,5},{5,4},{6,7},{7,6},{8,9},{9,8},{10,11... | collective-permute-start | bytes 2752520 | tf_op jit(solution)/shard_map/ppermute | solution.py:307
  78.1 2.9 pad_maximum_fusion.up_ref
  81.0 5.1 %collective-permute-done.1 = bf16[4,8,2304]{2,1,0:T(8,128)(2,1)S(1)} collective-permute-done((bf16[4,8,2304]{2,1,0:T(8,128)(2,1)S(1)}, bf16[4,8,2304]{2,1,0:T(8,128)(2,1)S(1)}, u32[]{:S(2)}, u32[]{:S(2)}) %collective-permute-start.1) | collective-permute-done | bytes 147488 | tf_op jit(solution)/shard_map/ppermute | solution.py:281
  86.1 1.9 collective-permute-start.4
  88.2 16.2 %all-gather.2.cloned.1.call-done.saved_ref = bf16[256,3584]{1,0:T(8,128)(2,1)} async-done(((bf16[16,3584]{1,0:T(8,128)(2,1)}), bf16[256,3584]{1,0:T(8,128)(2,1)}) %all-gather.2.cloned.1.call-update) | async-done | bytes 1835024 | tf_op jit(solution)/shard_map/all_gather | solution.py:349
  104.4 3.5 %collective-permute-start.9 = (bf16[8,8,2304]{2,1,0:T(8,128)(2,1)S(1)}, bf16[8,8,2304]{2,1,0:T(8,128)(2,1)S(1)}, u32[]{:S(2)}, u32[]{:S(2)}) collective-permute-start(bf16[8,8,2304]{2,1,0:T(8,128)(2,1)S(1)} %pad_maximum_fusion.4), channel_id=1, source_target_pairs={{0,2},{1,3},{2,0},{3,1},{4,6},{5,7},{6,4},{7,5},{8,10},{9,11},{10,... | collective-permute-start | bytes 884744 | tf_op jit(solution)/shard_map/ppermute | solution.py:281
  107.9 1.6 pad_maximum_fusion.1.down_ref
  109.5 2.3 shard_map.113
  111.8 2.5 collective-permute-start.6
  122.3 3.2 %shard_map.114 = (bf16[64,2304]{1,0:T(8,128)(2,1)S(1)}, bf16[64,2304]{1,0:T(8,128)(2,1)S(1)}) custom-call(s32[1]{0:T(128)} %bitcast.28.part_ref, bf16[256,3584]{1,0:T(8,128)(2,1)S(1)} %copy-done.7, bf16[64,2304]{1,0:T(8,128)(2,1)S(1)} %bitcast.267, bf16[64,2304]{1,0:T(8,128)(2,1)S(1)} %bitcast.271, bf16[3584,256]{1,0:T(8,128)(2,1)S(1)} %maximum_maximum_fusion.gate_ref, ...), custom_call_target="tpu_custom_call" | custom-call | flops 734003200 | bytes 8519680 | tf_op jit(solution)/shard_map/pallas_call | solution.py:231
  125.6 3.4 %collective-permute-start.10 = (bf16[8,8,2304]{2,1,0:T(8,128)(2,1)S(1)}, bf16[8,8,2304]{2,1,0:T(8,128)(2,1)S(1)}, u32[]{:S(2)}, u32[]{:S(2)}) collective-permute-start(bf16[8,8,2304]{2,1,0:T(8,128)(2,1)S(1)} %bitcast.277), channel_id=1, source_target_pairs={{0,2},{1,3},{2,0},{3,1},{4,6},{5,7},{6,4},{7,5},{8,10},{9,11},{10,... | collective-permute-start | bytes 884744 | tf_op jit(solution)/shard_map/ppermute | solution.py:281
  129.1 4.2 %collective-permute-start.7 = (bf16[4,8,2304]{2,1,0:T(8,128)(2,1)S(1)}, bf16[4,8,2304]{2,1,0:T(8,128)(2,1)S(1)}, u32[]{:S(2)}, u32[]{:S(2)}) collective-permute-start(bf16[4,8,2304]{2,1,0:T(8,128)(2,1)S(1)} %slice.569), channel_id=1, source_target_pairs={{0,4},{1,5},{2,6},{3,7},{4,0},{5,1},{6,2},{7,3},{8,12},{9,13},{10,... | collective-permute-start | bytes 442376 | tf_op jit(solution)/shard_map/ppermute | solution.py:281
  133.3 3.7 %collective-permute-done.10 = bf16[8,8,2304]{2,1,0:T(8,128)(2,1)S(1)} collective-permute-done((bf16[8,8,2304]{2,1,0:T(8,128)(2,1)S(1)}, bf16[8,8,2304]{2,1,0:T(8,128)(2,1)S(1)}, u32[]{:S(2)}, u32[]{:S(2)}) %collective-permute-start.10) | collective-permute-done | bytes 294944 | tf_op jit(solution)/shard_map/ppermute | solution.py:281
  137.1 3.2 %collective-permute-start.11 = (bf16[4,8,2304]{2,1,0:T(8,128)(2,1)S(1)}, bf16[4,8,2304]{2,1,0:T(8,128)(2,1)S(1)}, u32[]{:S(2)}, u32[]{:S(2)}) collective-permute-start(bf16[4,8,2304]{2,1,0:T(8,128)(2,1)S(1)} %slice.572), channel_id=1, source_target_pairs={{0,4},{1,5},{2,6},{3,7},{4,0},{5,1},{6,2},{7,3},{8,12},{9,13},{10,... | collective-permute-start | bytes 442376 | tf_op jit(solution)/shard_map/ppermute | solution.py:281
  140.4 11.2 %collective-permute-done.11 = bf16[4,8,2304]{2,1,0:T(8,128)(2,1)S(1)} collective-permute-done((bf16[4,8,2304]{2,1,0:T(8,128)(2,1)S(1)}, bf16[4,8,2304]{2,1,0:T(8,128)(2,1)S(1)}, u32[]{:S(2)}, u32[]{:S(2)}) %collective-permute-start.11) | collective-permute-done | bytes 147488 | tf_op jit(solution)/shard_map/ppermute | solution.py:281
  152.4 3.5 %all-to-all-start.1 = ((bf16[4,16,2304]{2,1,0:T(8,128)(2,1)}), bf16[4,16,2304]{2,1,0:T(8,128)(2,1)S(1)}, u32[]{:S(2)}, u32[]{:S(2)}) async-start(bf16[4,16,2304]{2,1,0:T(8,128)(2,1)} %pad_maximum_fusion.5), calls=%async_computation.1 | async-start | bytes 589824 | tf_op jit(solution)/shard_map/all_to_all | solution.py:273
  156.7 13.6 %all-to-all-done.1 = bf16[4,16,2304]{2,1,0:T(8,128)(2,1)S(1)} async-done(((bf16[4,16,2304]{2,1,0:T(8,128)(2,1)}), bf16[4,16,2304]{2,1,0:T(8,128)(2,1)S(1)}, u32[]{:S(2)}, u32[]{:S(2)}) %all-to-all-start.1) | async-done | bytes 294944 | tf_op jit(solution)/shard_map/all_to_all | solution.py:273
  170.9 1.9 collective-permute-start.12
  173.4 3.0 collective-permute-done.12
  178.4 1.9 collective-permute-start.13
  182.6 25.3 %all_to_all.20 = bf16[4,16,2304]{2,1,0:T(8,128)(2,1)S(1)} all-to-all(bf16[4,16,2304]{2,1,0:T(8,128)(2,1)S(1)} %pad_maximum_fusion.6), channel_id=1, replica_groups={{0,8,16,24},{1,9,17,25},{2,10,18,26},{3,11,19,27},{4,12,20,28},{5,13,21..., dimensions={0} | all-to-all | bytes 589824 | tf_op jit(solution)/shard_map/all_to_all | solution.py:273
  207.9 5.4 %collective-permute-start.14 = (bf16[4,8,2304]{2,1,0:T(8,128)(2,1)S(1)}, bf16[4,8,2304]{2,1,0:T(8,128)(2,1)S(1)}, u32[]{:S(2)}, u32[]{:S(2)}) collective-permute-start(bf16[4,8,2304]{2,1,0:T(8,128)(2,1)S(1)} %get-tuple-element.82), channel_id=1, source_target_pairs={{0,4},{1,5},{2,6},{3,7},{4,0},{5,1},{6,2},{7,3},{8,12},{9,13},{10,... | collective-permute-start | bytes 442376 | tf_op jit(solution)/shard_map/ppermute | solution.py:281
  213.3 1.9 collective-permute-start.18
  215.2 9.1 %collective-permute-done.14 = bf16[4,8,2304]{2,1,0:T(8,128)(2,1)S(1)} collective-permute-done((bf16[4,8,2304]{2,1,0:T(8,128)(2,1)S(1)}, bf16[4,8,2304]{2,1,0:T(8,128)(2,1)S(1)}, u32[]{:S(2)}, u32[]{:S(2)}) %collective-permute-start.14) | collective-permute-done | bytes 147488 | tf_op jit(solution)/shard_map/ppermute | solution.py:281
  224.3 1.9 collective-permute-start.15
  226.4 3.8 %collective-permute-start.19 = (bf16[8,8,2304]{2,1,0:T(8,128)(2,1)S(1)}, bf16[8,8,2304]{2,1,0:T(8,128)(2,1)S(1)}, u32[]{:S(2)}, u32[]{:S(2)}) collective-permute-start(bf16[8,8,2304]{2,1,0:T(8,128)(2,1)S(1)} %pad_maximum_fusion.8), channel_id=1, source_target_pairs={{0,2},{1,3},{2,0},{3,1},{4,6},{5,7},{6,4},{7,5},{8,10},{9,11},{10,... | collective-permute-start | bytes 884744 | tf_op jit(solution)/shard_map/ppermute | solution.py:281
  230.2 5.9 %collective-permute-done.15 = bf16[8,8,2304]{2,1,0:T(8,128)(2,1)S(1)} collective-permute-done((bf16[8,8,2304]{2,1,0:T(8,128)(2,1)S(1)}, bf16[8,8,2304]{2,1,0:T(8,128)(2,1)S(1)}, u32[]{:S(2)}, u32[]{:S(2)}) %collective-permute-start.15) | collective-permute-done | bytes 294944 | tf_op jit(solution)/shard_map/ppermute | solution.py:281
  236.2 1.5 shard_map.115
  237.7 2.1 collective-permute-start.16
  239.8 2.7 collective-permute-done.19
  242.5 3.2 %shard_map.116 = (bf16[64,2304]{1,0:T(8,128)(2,1)S(1)}, bf16[64,2304]{1,0:T(8,128)(2,1)S(1)}) custom-call(s32[1]{0:T(128)} %bitcast.28.part_ref, bf16[256,3584]{1,0:T(8,128)(2,1)S(1)} %copy-done.8, bf16[64,2304]{1,0:T(8,128)(2,1)S(1)} %bitcast.269, bf16[64,2304]{1,0:T(8,128)(2,1)S(1)} %bitcast.273, bf16[3584,256]{1,0:T(8,128)(2,1)S(1)} %maximum_maximum_fusion.gate_ref, ...), custom_call_target="tpu_custom_call" | custom-call | flops 734003200 | bytes 8519680 | tf_op jit(solution)/shard_map/pallas_call | solution.py:231
  245.7 1.9 collective-permute-start.20
  247.7 2.2 collective-permute-done.16
  250.0 2.9 collective-permute-start.17
  252.9 1.6 collective-permute-done.20
  254.6 2.3 collective-permute-start.21
  256.9 7.1 %collective-permute-done.17 = bf16[4,8,2304]{2,1,0:T(8,128)(2,1)S(1)} collective-permute-done((bf16[4,8,2304]{2,1,0:T(8,128)(2,1)S(1)}, bf16[4,8,2304]{2,1,0:T(8,128)(2,1)S(1)}, u32[]{:S(2)}, u32[]{:S(2)}) %collective-permute-start.17) | collective-permute-done | bytes 147488 | tf_op jit(solution)/shard_map/ppermute | solution.py:281
  264.1 1.5 collective-permute-done.21
  266.4 3.6 %all-to-all-start.3 = ((bf16[4,16,2304]{2,1,0:T(8,128)(2,1)}), bf16[4,16,2304]{2,1,0:T(8,128)(2,1)S(1)}, u32[]{:S(2)}, u32[]{:S(2)}) async-start(bf16[4,16,2304]{2,1,0:T(8,128)(2,1)} %pad_maximum_fusion.9), calls=%async_computation.3 | async-start | bytes 589824 | tf_op jit(solution)/shard_map/all_to_all | solution.py:273
  270.4 19.5 %all-to-all-done.3 = bf16[4,16,2304]{2,1,0:T(8,128)(2,1)S(1)} async-done(((bf16[4,16,2304]{2,1,0:T(8,128)(2,1)}), bf16[4,16,2304]{2,1,0:T(8,128)(2,1)S(1)}, u32[]{:S(2)}, u32[]{:S(2)}) %all-to-all-start.3) | async-done | bytes 294944 | tf_op jit(solution)/shard_map/all_to_all | solution.py:273
  (385 shorter events, 34.0 us)
Async XLA Ops:
  7.2 97.2 %all-gather.2.cloned.1.call-start = ((), (), s32[]{:S(2)}) async-start(), calls=%async_computation.4 | async-start | bytes 1949696 | tf_op jit(solution)/shard_map/all_gather | solution.py:349
  8.6 15.7 %collective-permute-start = (bf16[1792,128]{1,0:T(8,128)(2,1)S(1)}, bf16[1792,128]{1,0:T(8,128)(2,1)S(1)}, u32[]{:S(2)}, u32[]{:S(2)}) collective-permute-start(bf16[1792,128]{1,0:T(8,128)(2,1)S(1)} %get-tuple-element.79), channel_id=1, source_target_pairs={{0,1},{1,0},{2,3},{3,2},{4,5},{5,4},{6,7},{7,6},{8,9},{9,8},{10,11... | collective-permute-start | bytes 1376264 | tf_op jit(solution)/shard_map/ppermute | solution.py:304
  18.6 30.0 %copy-start.9 = (bf16[1,3584,128]{2,1,0:T(8,128)(2,1)S(1)}, bf16[1,3584,128]{2,1,0:T(8,128)(2,1)}, u32[]{:S(2)}) copy-start(bf16[1,3584,128]{2,1,0:T(8,128)(2,1)} %param.21) | copy-start | bytes 2752516
  24.2 24.4 %collective-permute-start.2 = (bf16[1792,128]{1,0:T(8,128)(2,1)S(1)}, bf16[1792,128]{1,0:T(8,128)(2,1)}, u32[]{:S(2)}, u32[]{:S(2)}) collective-permute-start(bf16[1792,128]{1,0:T(8,128)(2,1)S(1)} %get-tuple-element.41), channel_id=1, source_target_pairs={{0,1},{1,0},{2,3},{3,2},{4,5},{5,4},{6,7},{7,6},{8,9},{9,8},{10,11... | collective-permute-start | bytes 1376264 | tf_op jit(solution)/shard_map/ppermute | solution.py:305
  29.0 39.2 %all-to-all-start = ((bf16[4,16,2304]{2,1,0:T(8,128)(2,1)}), bf16[4,16,2304]{2,1,0:T(8,128)(2,1)S(1)}, u32[]{:S(2)}, u32[]{:S(2)}) async-start(bf16[4,16,2304]{2,1,0:T(8,128)(2,1)} %pad_maximum_fusion.2), calls=%async_computation | async-start | bytes 589824 | tf_op jit(solution)/shard_map/all_to_all | solution.py:273
  45.3 29.7 %collective-permute-start.3 = (bf16[3584,128]{1,0:T(8,128)(2,1)}, bf16[3584,128]{1,0:T(8,128)(2,1)}, u32[]{:S(2)}, u32[]{:S(2)}) collective-permute-start(bf16[3584,128]{1,0:T(8,128)(2,1)} %bitcast.21), channel_id=1, source_target_pairs={{0,1},{1,0},{2,3},{3,2},{4,5},{5,4},{6,7},{7,6},{8,9},{9,8},{10,11... | collective-permute-start | bytes 2752520 | tf_op jit(solution)/shard_map/ppermute | solution.py:306
  68.3 17.8 %collective-permute-start.1 = (bf16[4,8,2304]{2,1,0:T(8,128)(2,1)S(1)}, bf16[4,8,2304]{2,1,0:T(8,128)(2,1)S(1)}, u32[]{:S(2)}, u32[]{:S(2)}) collective-permute-start(bf16[4,8,2304]{2,1,0:T(8,128)(2,1)S(1)} %get-tuple-element.86), channel_id=1, source_target_pairs={{0,4},{1,5},{2,6},{3,7},{4,0},{5,1},{6,2},{7,3},{8,12},{9,13},{10,... | collective-permute-start | bytes 442376 | tf_op jit(solution)/shard_map/ppermute | solution.py:281
  71.7 16.5 %collective-permute-start.8 = (bf16[4,8,2304]{2,1,0:T(8,128)(2,1)S(1)}, bf16[4,8,2304]{2,1,0:T(8,128)(2,1)S(1)}, u32[]{:S(2)}, u32[]{:S(2)}) collective-permute-start(bf16[4,8,2304]{2,1,0:T(8,128)(2,1)S(1)} %get-tuple-element.87), channel_id=1, source_target_pairs={{0,4},{1,5},{2,6},{3,7},{4,0},{5,1},{6,2},{7,3},{8,12},{9,13},{10,... | collective-permute-start | bytes 442376 | tf_op jit(solution)/shard_map/ppermute | solution.py:281
  75.1 32.8 %collective-permute-start.5 = (bf16[128,3584]{1,0:T(8,128)(2,1)}, bf16[128,3584]{1,0:T(8,128)(2,1)}, u32[]{:S(2)}, u32[]{:S(2)}) collective-permute-start(bf16[128,3584]{1,0:T(8,128)(2,1)} %bitcast.279), channel_id=1, source_target_pairs={{0,1},{1,0},{2,3},{3,2},{4,5},{5,4},{6,7},{7,6},{8,9},{9,8},{10,11... | collective-permute-start | bytes 2752520 | tf_op jit(solution)/shard_map/ppermute | solution.py:307
  86.1 23.4 %collective-permute-start.4 = (bf16[8,8,2304]{2,1,0:T(8,128)(2,1)S(1)}, bf16[8,8,2304]{2,1,0:T(8,128)(2,1)S(1)}, u32[]{:S(2)}, u32[]{:S(2)}) collective-permute-start(bf16[8,8,2304]{2,1,0:T(8,128)(2,1)S(1)} %pad_maximum_fusion.3), channel_id=1, source_target_pairs={{0,2},{1,3},{2,0},{3,1},{4,6},{5,7},{6,4},{7,5},{8,10},{9,11},{10,... | collective-permute-start | bytes 884744 | tf_op jit(solution)/shard_map/ppermute | solution.py:281
  104.4 13.4 %collective-permute-start.9 = (bf16[8,8,2304]{2,1,0:T(8,128)(2,1)S(1)}, bf16[8,8,2304]{2,1,0:T(8,128)(2,1)S(1)}, u32[]{:S(2)}, u32[]{:S(2)}) collective-permute-start(bf16[8,8,2304]{2,1,0:T(8,128)(2,1)S(1)} %pad_maximum_fusion.4), channel_id=1, source_target_pairs={{0,2},{1,3},{2,0},{3,1},{4,6},{5,7},{6,4},{7,5},{8,10},{9,11},{10,... | collective-permute-start | bytes 884744 | tf_op jit(solution)/shard_map/ppermute | solution.py:281
  111.8 17.2 %collective-permute-start.6 = (bf16[8,8,2304]{2,1,0:T(8,128)(2,1)}, bf16[8,8,2304]{2,1,0:T(8,128)(2,1)S(1)}, u32[]{:S(2)}, u32[]{:S(2)}) collective-permute-start(bf16[8,8,2304]{2,1,0:T(8,128)(2,1)} %bitcast.27), channel_id=1, source_target_pairs={{0,2},{1,3},{2,0},{3,1},{4,6},{5,7},{6,4},{7,5},{8,10},{9,11},{10,... | collective-permute-start | bytes 884744 | tf_op jit(solution)/shard_map/ppermute | solution.py:281
  125.6 11.4 %collective-permute-start.10 = (bf16[8,8,2304]{2,1,0:T(8,128)(2,1)S(1)}, bf16[8,8,2304]{2,1,0:T(8,128)(2,1)S(1)}, u32[]{:S(2)}, u32[]{:S(2)}) collective-permute-start(bf16[8,8,2304]{2,1,0:T(8,128)(2,1)S(1)} %bitcast.277), channel_id=1, source_target_pairs={{0,2},{1,3},{2,0},{3,1},{4,6},{5,7},{6,4},{7,5},{8,10},{9,11},{10,... | collective-permute-start | bytes 884744 | tf_op jit(solution)/shard_map/ppermute | solution.py:281
  129.1 26.8 %copy-start.61 = (s32[16]{0:T(128)S(1)}, s32[16]{0:T(128)}, u32[]{:S(2)}) copy-start(s32[16]{0:T(128)} %eq.283) | copy-start | bytes 196
  129.1 27.1 %copy-start.17 = (bf16[2,8,4,2,4]{1,0,4,3,2:T(2,128)(2,1)S(1)}, bf16[2,8,4,2,4]{1,0,4,3,2:T(2,128)(2,1)}, u32[]{:S(2)}) copy-start(bf16[2,8,4,2,4]{1,0,4,3,2:T(2,128)(2,1)} %get-tuple-element.128) | copy-start | bytes 3076
  129.1 27.2 %copy-start.16 = (bf16[4,2,4,2,8]{4,1,2,3,0:T(2,128)(2,1)S(1)}, bf16[4,2,4,2,8]{4,1,2,3,0:T(2,128)(2,1)}, u32[]{:S(2)}) copy-start(bf16[4,2,4,2,8]{4,1,2,3,0:T(2,128)(2,1)} %get-tuple-element.108) | copy-start | bytes 3076
  129.1 27.3 %copy-start.32 = (f32[4,5]{0,1:T(8,128)S(1)}, f32[4,5]{0,1:T(8,128)}, u32[]{:S(2)}) copy-start(f32[4,5]{0,1:T(8,128)} %get-tuple-element.72) | copy-start | bytes 244
  129.1 27.4 %copy-start.31 = (f32[4,5]{0,1:T(8,128)S(1)}, f32[4,5]{0,1:T(8,128)}, u32[]{:S(2)}) copy-start(f32[4,5]{0,1:T(8,128)} %get-tuple-element.58) | copy-start | bytes 244
  129.1 11.2 %collective-permute-start.7 = (bf16[4,8,2304]{2,1,0:T(8,128)(2,1)S(1)}, bf16[4,8,2304]{2,1,0:T(8,128)(2,1)S(1)}, u32[]{:S(2)}, u32[]{:S(2)}) collective-permute-start(bf16[4,8,2304]{2,1,0:T(8,128)(2,1)S(1)} %slice.569), channel_id=1, source_target_pairs={{0,4},{1,5},{2,6},{3,7},{4,0},{5,1},{6,2},{7,3},{8,12},{9,13},{10,... | collective-permute-start | bytes 442376 | tf_op jit(solution)/shard_map/ppermute | solution.py:281
  137.0 33.3 %copy-start.26 = (bf16[56,32]{0,1:T(8,128)(2,1)S(1)}, bf16[56,32]{0,1:T(8,128)(2,1)}, u32[]{:S(2)}) copy-start(bf16[56,32]{0,1:T(8,128)(2,1)} %convert_element_type.597) | copy-start | bytes 10756
  137.1 33.5 %copy-start.27 = (bf16[16,32]{0,1:T(8,128)(2,1)S(1)}, bf16[16,32]{0,1:T(8,128)(2,1)}, u32[]{:S(2)}) copy-start(bf16[16,32]{0,1:T(8,128)(2,1)} %convert_element_type.548) | copy-start | bytes 3076
  137.1 33.7 %copy-start.13 = (bf16[1,8,3584]{2,1,0:T(8,128)(2,1)S(1)}, bf16[1,8,3584]{2,1,0:T(8,128)(2,1)}, u32[]{:S(2)}) copy-start(bf16[1,8,3584]{2,1,0:T(8,128)(2,1)} %param.14) | copy-start | bytes 172036
  137.1 14.4 %collective-permute-start.11 = (bf16[4,8,2304]{2,1,0:T(8,128)(2,1)S(1)}, bf16[4,8,2304]{2,1,0:T(8,128)(2,1)S(1)}, u32[]{:S(2)}, u32[]{:S(2)}) collective-permute-start(bf16[4,8,2304]{2,1,0:T(8,128)(2,1)S(1)} %slice.572), channel_id=1, source_target_pairs={{0,4},{1,5},{2,6},{3,7},{4,0},{5,1},{6,2},{7,3},{8,12},{9,13},{10,... | collective-permute-start | bytes 442376 | tf_op jit(solution)/shard_map/ppermute | solution.py:281
  140.4 32.7 %copy-start.23 = (f32[8,2,4]{0,2,1:T(4,128)S(1)}, f32[8,2,4]{0,2,1:T(4,128)}, u32[]{:S(2)}) copy-start(f32[8,2,4]{0,2,1:T(4,128)} %copy-done.22) | copy-start | bytes 772
  140.4 32.7 %copy-start.56 = (f32[8,2]{0,1:T(2,128)S(1)}, f32[8,2]{0,1:T(2,128)}, u32[]{:S(2)}) copy-start(f32[8,2]{0,1:T(2,128)} %get-tuple-element.77) | copy-start | bytes 196
  140.4 32.8 %copy-start.41 = (f32[8,2]{0,1:T(2,128)S(1)}, f32[8,2]{0,1:T(2,128)}, u32[]{:S(2)}) copy-start(f32[8,2]{0,1:T(2,128)} %copy-done.40) | copy-start | bytes 196
  140.4 32.8 %copy-start.52 = (f32[8]{0:T(128)S(1)}, f32[8]{0:T(128)}, u32[]{:S(2)}) copy-start(f32[8]{0:T(128)} %copy-done.51) | copy-start | bytes 100
  152.4 17.9 %all-to-all-start.1 = ((bf16[4,16,2304]{2,1,0:T(8,128)(2,1)}), bf16[4,16,2304]{2,1,0:T(8,128)(2,1)S(1)}, u32[]{:S(2)}, u32[]{:S(2)}) async-start(bf16[4,16,2304]{2,1,0:T(8,128)(2,1)} %pad_maximum_fusion.5), calls=%async_computation.1 | async-start | bytes 589824 | tf_op jit(solution)/shard_map/all_to_all | solution.py:273
  170.9 5.5 %collective-permute-start.12 = (bf16[8,3584]{1,0:T(8,128)(2,1)S(1)}, bf16[8,3584]{1,0:T(8,128)(2,1)S(1)}, u32[]{:S(2)}, u32[]{:S(2)}) collective-permute-start(bf16[8,3584]{1,0:T(8,128)(2,1)S(1)} %fusion.49), channel_id=1, source_target_pairs={{480,0},{0,32},{32,64},{64,96},{96,128},{128,160},{160,192},{192,2... | collective-permute-start | bytes 172040 | tf_op jit(solution)/shard_map/ppermute | solution.py:16
  178.4 3.7 %collective-permute-start.13 = (bf16[8,3584]{1,0:T(8,128)(2,1)S(1)}, bf16[8,3584]{1,0:T(8,128)(2,1)S(1)}, u32[]{:S(2)}, u32[]{:S(2)}) collective-permute-start(bf16[8,3584]{1,0:T(8,128)(2,1)S(1)} %fusion.42), channel_id=1, source_target_pairs={{32,0},{64,32},{96,64},{128,96},{160,128},{192,160},{224,192},{256... | collective-permute-start | bytes 172040 | tf_op jit(solution)/shard_map/ppermute | solution.py:16
  182.2 54.0 %copy-start.6 = (bf16[256,3584]{1,0:T(8,128)(2,1)S(1)}, bf16[256,3584]{1,0:T(8,128)(2,1)}, u32[]{:S(2)}) copy-start(bf16[256,3584]{1,0:T(8,128)(2,1)} %copy-done.4) | copy-start | bytes 5505028
  182.2 54.0 %copy-start.3 = (bf16[3584,256]{1,0:T(8,128)(2,1)S(1)}, bf16[3584,256]{1,0:T(8,128)(2,1)}, u32[]{:S(2)}) copy-start(bf16[3584,256]{1,0:T(8,128)(2,1)} %pad_maximum_fusion.up_ref) | copy-start | bytes 5505028
  207.9 16.4 %collective-permute-start.14 = (bf16[4,8,2304]{2,1,0:T(8,128)(2,1)S(1)}, bf16[4,8,2304]{2,1,0:T(8,128)(2,1)S(1)}, u32[]{:S(2)}, u32[]{:S(2)}) collective-permute-start(bf16[4,8,2304]{2,1,0:T(8,128)(2,1)S(1)} %get-tuple-element.82), channel_id=1, source_target_pairs={{0,4},{1,5},{2,6},{3,7},{4,0},{5,1},{6,2},{7,3},{8,12},{9,13},{10,... | collective-permute-start | bytes 442376 | tf_op jit(solution)/shard_map/ppermute | solution.py:281
  213.3 13.1 %collective-permute-start.18 = (bf16[4,8,2304]{2,1,0:T(8,128)(2,1)S(1)}, bf16[4,8,2304]{2,1,0:T(8,128)(2,1)S(1)}, u32[]{:S(2)}, u32[]{:S(2)}) collective-permute-start(bf16[4,8,2304]{2,1,0:T(8,128)(2,1)S(1)} %get-tuple-element.83), channel_id=1, source_target_pairs={{0,4},{1,5},{2,6},{3,7},{4,0},{5,1},{6,2},{7,3},{8,12},{9,13},{10,... | collective-permute-start | bytes 442376 | tf_op jit(solution)/shard_map/ppermute | solution.py:281
  224.3 11.8 %collective-permute-start.15 = (bf16[8,8,2304]{2,1,0:T(8,128)(2,1)S(1)}, bf16[8,8,2304]{2,1,0:T(8,128)(2,1)S(1)}, u32[]{:S(2)}, u32[]{:S(2)}) collective-permute-start(bf16[8,8,2304]{2,1,0:T(8,128)(2,1)S(1)} %pad_maximum_fusion.7), channel_id=1, source_target_pairs={{0,2},{1,3},{2,0},{3,1},{4,6},{5,7},{6,4},{7,5},{8,10},{9,11},{10,... | collective-permute-start | bytes 884744 | tf_op jit(solution)/shard_map/ppermute | solution.py:281
  226.4 16.1 %collective-permute-start.19 = (bf16[8,8,2304]{2,1,0:T(8,128)(2,1)S(1)}, bf16[8,8,2304]{2,1,0:T(8,128)(2,1)S(1)}, u32[]{:S(2)}, u32[]{:S(2)}) collective-permute-start(bf16[8,8,2304]{2,1,0:T(8,128)(2,1)S(1)} %pad_maximum_fusion.8), channel_id=1, source_target_pairs={{0,2},{1,3},{2,0},{3,1},{4,6},{5,7},{6,4},{7,5},{8,10},{9,11},{10,... | collective-permute-start | bytes 884744 | tf_op jit(solution)/shard_map/ppermute | solution.py:281
  237.7 12.2 %collective-permute-start.16 = (bf16[8,8,2304]{2,1,0:T(8,128)(2,1)S(1)}, bf16[8,8,2304]{2,1,0:T(8,128)(2,1)S(1)}, u32[]{:S(2)}, u32[]{:S(2)}) collective-permute-start(bf16[8,8,2304]{2,1,0:T(8,128)(2,1)S(1)} %bitcast.276), channel_id=1, source_target_pairs={{0,2},{1,3},{2,0},{3,1},{4,6},{5,7},{6,4},{7,5},{8,10},{9,11},{10,... | collective-permute-start | bytes 884744 | tf_op jit(solution)/shard_map/ppermute | solution.py:281
  245.7 8.7 %collective-permute-start.20 = (bf16[8,8,2304]{2,1,0:T(8,128)(2,1)S(1)}, bf16[8,8,2304]{2,1,0:T(8,128)(2,1)S(1)}, u32[]{:S(2)}, u32[]{:S(2)}) collective-permute-start(bf16[8,8,2304]{2,1,0:T(8,128)(2,1)S(1)} %bitcast.275), channel_id=1, source_target_pairs={{0,2},{1,3},{2,0},{3,1},{4,6},{5,7},{6,4},{7,5},{8,10},{9,11},{10,... | collective-permute-start | bytes 884744 | tf_op jit(solution)/shard_map/ppermute | solution.py:281
  250.0 14.0 %collective-permute-start.17 = (bf16[4,8,2304]{2,1,0:T(8,128)(2,1)S(1)}, bf16[4,8,2304]{2,1,0:T(8,128)(2,1)S(1)}, u32[]{:S(2)}, u32[]{:S(2)}) collective-permute-start(bf16[4,8,2304]{2,1,0:T(8,128)(2,1)S(1)} %slice.624), channel_id=1, source_target_pairs={{0,4},{1,5},{2,6},{3,7},{4,0},{5,1},{6,2},{7,3},{8,12},{9,13},{10,... | collective-permute-start | bytes 442376 | tf_op jit(solution)/shard_map/ppermute | solution.py:281
  254.5 35.8 %copy-start.19 = (f32[8,2,4]{0,2,1:T(4,128)S(1)}, f32[8,2,4]{0,2,1:T(4,128)}, u32[]{:S(2)}) copy-start(f32[8,2,4]{0,2,1:T(4,128)} %copy-done.18) | copy-start | bytes 772
  254.5 35.9 %copy-start.55 = (f32[8,2]{0,1:T(2,128)S(1)}, f32[8,2]{0,1:T(2,128)}, u32[]{:S(2)}) copy-start(f32[8,2]{0,1:T(2,128)} %get-tuple-element.75) | copy-start | bytes 196
  254.5 35.9 %copy-start.39 = (f32[8,2]{0,1:T(2,128)S(1)}, f32[8,2]{0,1:T(2,128)}, u32[]{:S(2)}) copy-start(f32[8,2]{0,1:T(2,128)} %copy-done.38) | copy-start | bytes 196
  254.6 35.9 %copy-start.50 = (f32[8]{0:T(128)S(1)}, f32[8]{0:T(128)}, u32[]{:S(2)}) copy-start(f32[8]{0:T(128)} %copy-done.49) | copy-start | bytes 100
  254.6 35.9 %copy-start.34 = (s32[8,2]{0,1:T(2,128)S(1)}, s32[8,2]{0,1:T(2,128)}, u32[]{:S(2)}) copy-start(s32[8,2]{0,1:T(2,128)} %copy-done.33) | copy-start | bytes 196
  254.6 11.0 %collective-permute-start.21 = (bf16[4,8,2304]{2,1,0:T(8,128)(2,1)S(1)}, bf16[4,8,2304]{2,1,0:T(8,128)(2,1)S(1)}, u32[]{:S(2)}, u32[]{:S(2)}) collective-permute-start(bf16[4,8,2304]{2,1,0:T(8,128)(2,1)S(1)} %slice.627), channel_id=1, source_target_pairs={{0,4},{1,5},{2,6},{3,7},{4,0},{5,1},{6,2},{7,3},{8,12},{9,13},{10,... | collective-permute-start | bytes 442376 | tf_op jit(solution)/shard_map/ppermute | solution.py:281
  266.4 25.2 %copy-start.46 = (f32[8]{0:T(128)S(1)}, f32[8]{0:T(128)}, u32[]{:S(2)}) copy-start(f32[8]{0:T(128)} %copy-done.45) | copy-start | bytes 100
  266.4 25.2 %copy-start.57 = (f32[8]{0:T(128)S(1)}, f32[8]{0:T(128)}, u32[]{:S(2)}) copy-start(f32[8]{0:T(128)} %get-tuple-element.141) | copy-start | bytes 100
  266.4 23.4 %all-to-all-start.3 = ((bf16[4,16,2304]{2,1,0:T(8,128)(2,1)}), bf16[4,16,2304]{2,1,0:T(8,128)(2,1)S(1)}, u32[]{:S(2)}, u32[]{:S(2)}) async-start(bf16[4,16,2304]{2,1,0:T(8,128)(2,1)} %pad_maximum_fusion.9), calls=%async_computation.3 | async-start | bytes 589824 | tf_op jit(solution)/shard_map/all_to_all | solution.py:273
  (40 other events, 381.1 us)
Sparse Core Ops, SparseCore 0:
  14.5 89.8 all-gather.1

commit v4 on v3

--- a/solution.py
+++ b/solution.py
@@ -198,7 +198,7 @@
     token = jnp.sum(jnp.where(lane == slot + 5, scalars, 0.0), axis=1, keepdims=True).astype(jnp.int32)
     source = row_source(iota((count, 1), 0))
     away = (((source >> 2) & 1) << 1) | (source >> 3)
-    depth_place = (away ^ part) + ((source & 3) << 2)
+    depth_place = (away ^ part ^ (source & 2)) + ((source & 3) << 2)
     first = depth_place * (ticks * tokens) + tick * tokens
     wanted = jnp.where(token < 0, -1, first + token)
     pick = one_hot(wanted, iota((count, saved_ref.shape[0]), 1))
@@ -265,9 +265,11 @@
     depth = ranks // 2
     copies = depth // experts
     partner = [(i, i ^ 1) for i in range(ranks)]
-    far = [[x + 2 * (p + copies * e) for e in range(experts)] for p in range(copies) for x in range(2)]
+    turn = [e // 2 % 2 * 2 for e in range(experts)]
+    far = [[x + 2 * ((p ^ turn[e]) + copies * e) for e in range(experts)] for p in range(copies) for x in range(2)]
     column = [[x + 2 * z for z in range(depth)] for x in range(2)]
-    part = lax.axis_index("expert") // 2 % copies
+    depth_place = lax.axis_index("expert") // 2
+    part = (depth_place % copies) ^ (depth_place // copies // 2 % 2 * 2)
 
     def swap(slabs, groups):
         return lax.all_to_all(
@@ -280,32 +282,33 @@
     def across(value, bit):
         return lax.ppermute(value, "expert", [(i, i ^ (2 * bit)) for i in range(ranks)])
 
-    def spread_near(held, then=()):
-        near = after(jnp.concatenate([held, across(held, 2)], axis=0), *then)
+    def spread_near(held):
+        near = jnp.concatenate([held, across(held, 2)], axis=0)
         return near, across(near, 1)
 
     def add(left, right):
         return (left.astype(F32) + right.astype(F32)).astype(BF16)
 
-    def gather_near(keep, send):
-        parts = add(keep, across(send, 1))
+    def gather_near(keep, send, then=()):
+        parts = add(keep, across(after(send, *then), 1))
         count = parts.shape[0] // 2
         return add(parts[:count], across(parts[count:], 2))
 
-    def dispatch(*slabs, first=(), then=((), ())):
-        held = swap(after(jnp.concatenate(slabs, axis=1), *first), far)
-        return [spread_near(held[:, 8 * i:8 * i + 8], then[i]) for i in range(len(slabs))]
-
-    def gather_back(*slabs):
-        held = swap(jnp.concatenate([gather_near(*slab) for slab in slabs], axis=1), far)
+    def dispatch(*slabs, first=(), then=()):
+        held = after(swap(after(jnp.concatenate(slabs, axis=1), *first), far), *then)
+        return [spread_near(held[:, 8 * i:8 * i + 8]) for i in range(len(slabs))]
+
+    def gather_back(*slabs, then=((), ())):
+        held = swap(jnp.concatenate([gather_near(*slab, then[i]) for i, slab in enumerate(slabs)], axis=1), far)
         return [held[:, 8 * i:8 * i + 8] for i in range(len(slabs))]
 
     half = w_gate.shape[1] // 2
     gate_r0 = lax.ppermute(w_gate[0, :half], "expert", partner)
-    gate_r1 = lax.ppermute(after(w_gate[0, half:], gate_r0), "expert", partner)
-    up_r = lax.ppermute(after(w_up[0], gate_r0), "expert", partner)
-    down_r = lax.ppermute(after(w_down[0], gate_r1, up_r), "expert", partner)
-    gate_r = jnp.concatenate([gate_r0, gate_r1], axis=0)
+    mixed = jnp.concatenate([w_gate[0, half:], w_up[0]], axis=0)
+    mixed_r = lax.ppermute(after(mixed, gate_r0), "expert", partner)
+    down_r = lax.ppermute(after(w_down[0], mixed_r), "expert", partner)
+    gate_r = jnp.concatenate([gate_r0, mixed_r[:half]], axis=0)
+    up_r = mixed_r[half:]
 
     expert_ids = jnp.arange(experts, dtype=jnp.int32)
     fwd_places = [slot_places(fwd_routes[t, 0], experts, cap) for t in range(ticks)]
@@ -354,7 +357,7 @@
         pack_rows(normed, fwd_spreads[0], 1),
         pack_rows(cotan_in, bwd_spreads[0], 1, saved[0][1]),
         first=(gate_r0,),
-        then=((gate_r1, up_r), (saved_rows,)),
+        then=(mixed_r,),
     )
     weights = (
         jnp.concatenate([w_gate[0], gate_r], axis=1),
@@ -368,10 +371,12 @@
                 functools.partial(backward_kernel, t, tokens, ticks),
                 rows_c, (saved_rows,) + weights, width, 5, (part.reshape(1),),
             ),
+            then=((saved_rows,) if t == 0 else (), ()),
         )
         fwd_result = finish_forward(t, forward_in, normed, back_f)
         bwd_result = finish_backward(t, cotan_in, saved[t][2], back_b)
         if t + 1 < ticks:
+            fwd_result, bwd_result = lax.optimization_barrier((fwd_result, bwd_result))
             forward_in = shift(fwd_result, "pipe", 1)
             cotan_in = shift(bwd_result, "pipe", -1)
             normed = norm_rows(forward_in, gain).astype(BF16)

time: 301 us -> 282 us (0.937)
  the two profiles are of different devices: /device:TPU:18 before, /device:TPU:62 now
where the time goes in v4:
time: 282 us; the launch traced here: 281 us
  waiting for transfers between devices  105 us (37%)
  starting transfers between devices  104 us (37%)
  blocking collectives  18.6 us (7%)
  between operations  15.6 us (6%)
  other arithmetic  12.1 us (4%)
  local copies, waits for them, and re-layouts  11.3 us (4%)
  Pallas kernels  9.55 us (3%)
  matrix products  4.63 us (2%)
    ppermute x16, starting transfers between devices, across(): lax.ppermute(value, 'expert', [(i, i ^ 2 * bit) for i in range(ranks)])  63.9 us
    all_to_all x3, waiting for transfers between devices, swap(): lax.all_to_all(slabs, 'expert', split_axis=0, concat_axis=0, axis_index_g...  57.6 us
    ppermute x16, waiting for transfers between devices, across(): lax.ppermute(value, 'expert', [(i, i ^ 2 * bit) for i in range(ranks)])  33.8 us
    all_to_all x3, starting transfers between devices, swap(): lax.all_to_all(slabs, 'expert', split_axis=0, concat_axis=0, axis_index_g...  25.1 us
    all_to_all x1, blocking collectives, swap(): lax.all_to_all(slabs, 'expert', split_axis=0, concat_axis=0, axis_index_g...  18.6 us
    pallas_call x4, Pallas kernels, run_kernel(): pl.pallas_call(kernel, out_shape=[jax.ShapeDtypeStruct(near.shape, BF16)]...  9.55 us
    unnamed x88, local copies, waits for them, and re-layouts  5.98 us
  transfers between devices with their start and end apart: 25, of which 17 were waited for; matrix products, arithmetic and copies ran while one was open for 5% of the time, Pallas kernels for 3%

profile of v4, /device:TPU:62, one launch (start us, length us, event | category | flops | bytes accessed | tf_op | source)
XLA Modules:
  0.0 281.3 jit_solution(10608194455461367944)
XLA Ops:
  7.3 1.3 slice_bitcast_fusion
  8.6 3.4 %collective-permute-start = (bf16[1792,128]{1,0:T(8,128)(2,1)S(1)}, bf16[1792,128]{1,0:T(8,128)(2,1)S(1)}, u32[]{:S(2)}, u32[]{:S(2)}) collective-permute-start(bf16[1792,128]{1,0:T(8,128)(2,1)S(1)} %get-tuple-element.81), channel_id=1, source_target_pairs={{0,1},{1,0},{2,3},{3,2},{4,5},{5,4},{6,7},{7,6},{8,9},{9,8},{10,11... | collective-permute-start | bytes 1376264 | tf_op jit(solution)/shard_map/ppermute | solution.py:306
  18.9 5.5 %collective-permute-done = bf16[1792,128]{1,0:T(8,128)(2,1)S(1)} collective-permute-done((bf16[1792,128]{1,0:T(8,128)(2,1)S(1)}, bf16[1792,128]{1,0:T(8,128)(2,1)S(1)}, u32[]{:S(2)}, u32[]{:S(2)}) %collective-permute-start) | collective-permute-done | bytes 458784 | tf_op jit(solution)/shard_map/ppermute | solution.py:306
  24.4 3.3 %collective-permute-start.1 = (bf16[5376,128]{1,0:T(8,128)(2,1)}, bf16[5376,128]{1,0:T(8,128)(2,1)S(1)}, u32[]{:S(2)}, u32[]{:S(2)}) collective-permute-start(bf16[5376,128]{1,0:T(8,128)(2,1)} %pad_maximum_fusion.2), channel_id=1, source_target_pairs={{0,1},{1,0},{2,3},{3,2},{4,5},{5,4},{6,7},{7,6},{8,9},{9,8},{10,11... | collective-permute-start | bytes 4128776 | tf_op jit(solution)/shard_map/ppermute | solution.py:308
  28.4 13.3 %all-to-all-start = ((bf16[4,16,2304]{2,1,0:T(8,128)(2,1)}), bf16[4,16,2304]{2,1,0:T(8,128)(2,1)S(1)}, u32[]{:S(2)}, u32[]{:S(2)}) async-start(bf16[4,16,2304]{2,1,0:T(8,128)(2,1)} %pad_maximum_fusion.3), calls=%async_computation | async-start | bytes 589824 | tf_op jit(solution)/shard_map/all_to_all | solution.py:275
  41.7 23.1 %all-to-all-done = bf16[4,16,2304]{2,1,0:T(8,128)(2,1)S(1)} async-done(((bf16[4,16,2304]{2,1,0:T(8,128)(2,1)}), bf16[4,16,2304]{2,1,0:T(8,128)(2,1)S(1)}, u32[]{:S(2)}, u32[]{:S(2)}) %all-to-all-start) | async-done | bytes 294944 | tf_op jit(solution)/shard_map/all_to_all | solution.py:275
  64.9 2.1 collective-permute-start.2
  66.9 2.8 collective-permute-start.4
  69.7 4.8 %collective-permute-start.7 = (bf16[4,8,2304]{2,1,0:T(8,128)(2,1)S(1)}, bf16[4,8,2304]{2,1,0:T(8,128)(2,1)S(1)}, u32[]{:S(2)}, u32[]{:S(2)}) collective-permute-start(bf16[4,8,2304]{2,1,0:T(8,128)(2,1)S(1)} %get-tuple-element.95), channel_id=1, source_target_pairs={{0,4},{1,5},{2,6},{3,7},{4,0},{5,1},{6,2},{7,3},{8,12},{9,13},{10,... | collective-permute-start | bytes 442376 | tf_op jit(solution)/shard_map/ppermute | solution.py:283
  74.7 1.6 maximum_maximum_fusion
  76.3 2.6 collective-permute-done.2
  78.9 5.9 %collective-permute-start.3 = (bf16[8,8,2304]{2,1,0:T(8,128)(2,1)S(1)}, bf16[8,8,2304]{2,1,0:T(8,128)(2,1)S(1)}, u32[]{:S(2)}, u32[]{:S(2)}) collective-permute-start(bf16[8,8,2304]{2,1,0:T(8,128)(2,1)S(1)} %get-tuple-element.92), channel_id=1, source_target_pairs={{0,2},{1,3},{2,0},{3,1},{4,6},{5,7},{6,4},{7,5},{8,10},{9,11},{10,... | collective-permute-start | bytes 884744 | tf_op jit(solution)/shard_map/ppermute | solution.py:283
  85.6 2.7 collective-permute-start.8
  88.4 3.1 %collective-permute-done.4 = bf16[128,3584]{1,0:T(8,128)(2,1)S(1)} collective-permute-done((bf16[128,3584]{1,0:T(8,128)(2,1)}, bf16[128,3584]{1,0:T(8,128)(2,1)S(1)}, u32[]{:S(2)}, u32[]{:S(2)}) %collective-permute-start.4) | collective-permute-done | bytes 917536 | tf_op jit(solution)/shard_map/ppermute | solution.py:309
  91.6 2.7 collective-permute-done.3
  94.3 1.5 shard_map.113
  97.1 5.0 %all-gather.2.cloned.1.call-done.saved_ref = bf16[256,3584]{1,0:T(8,128)(2,1)} async-done(((bf16[16,3584]{1,0:T(8,128)(2,1)}), bf16[256,3584]{1,0:T(8,128)(2,1)}) %all-gather.2.cloned.1.call-update) | async-done | bytes 1835024 | tf_op jit(solution)/shard_map/all_gather | solution.py:352
  102.1 2.7 collective-permute-start.5
  104.9 1.5 copy-done.2
  106.4 1.5 copy-done.5
  107.9 1.5 copy-done.7
  109.4 3.2 %shard_map.114 = (bf16[64,2304]{1,0:T(8,128)(2,1)S(1)}, bf16[64,2304]{1,0:T(8,128)(2,1)S(1)}) custom-call(s32[1]{0:T(128)} %bitcast.29.part_ref, bf16[256,3584]{1,0:T(8,128)(2,1)S(1)} %copy-done.7, bf16[64,2304]{1,0:T(8,128)(2,1)S(1)} %get-tuple-element.97.near_ref, bf16[64,2304]{1,0:T(8,128)(2,1)S(1)} %bitcast.271, ...), custom_call_target="tpu_custom_call" | custom-call | flops 734003200 | bytes 8519680 | tf_op jit(solution)/shard_map/pallas_call | solution.py:231
  112.6 3.1 %collective-permute-start.9 = (bf16[8,8,2304]{2,1,0:T(8,128)(2,1)S(1)}, bf16[8,8,2304]{2,1,0:T(8,128)(2,1)S(1)}, u32[]{:S(2)}, u32[]{:S(2)}) collective-permute-start(bf16[8,8,2304]{2,1,0:T(8,128)(2,1)S(1)} %bitcast.278), channel_id=1, source_target_pairs={{0,2},{1,3},{2,0},{3,1},{4,6},{5,7},{6,4},{7,5},{8,10},{9,11},{10,... | collective-permute-start | bytes 884744 | tf_op jit(solution)/shard_map/ppermute | solution.py:283
  116.8 3.5 %collective-permute-start.6 = (bf16[4,8,2304]{2,1,0:T(8,128)(2,1)S(1)}, bf16[4,8,2304]{2,1,0:T(8,128)(2,1)S(1)}, u32[]{:S(2)}, u32[]{:S(2)}) collective-permute-start(bf16[4,8,2304]{2,1,0:T(8,128)(2,1)S(1)} %slice.578), channel_id=1, source_target_pairs={{0,4},{1,5},{2,6},{3,7},{4,0},{5,1},{6,2},{7,3},{8,12},{9,13},{10,... | collective-permute-start | bytes 442376 | tf_op jit(solution)/shard_map/ppermute | solution.py:283
  120.3 4.0 %collective-permute-done.9 = bf16[8,8,2304]{2,1,0:T(8,128)(2,1)S(1)} collective-permute-done((bf16[8,8,2304]{2,1,0:T(8,128)(2,1)S(1)}, bf16[8,8,2304]{2,1,0:T(8,128)(2,1)S(1)}, u32[]{:S(2)}, u32[]{:S(2)}) %collective-permute-start.9) | collective-permute-done | bytes 294944 | tf_op jit(solution)/shard_map/ppermute | solution.py:283
  124.4 1.9 collective-permute-start.10
  126.6 5.7 %collective-permute-done.10 = bf16[4,8,2304]{2,1,0:T(8,128)(2,1)S(1)} collective-permute-done((bf16[4,8,2304]{2,1,0:T(8,128)(2,1)S(1)}, bf16[4,8,2304]{2,1,0:T(8,128)(2,1)S(1)}, u32[]{:S(2)}, u32[]{:S(2)}) %collective-permute-start.10) | collective-permute-done | bytes 147488 | tf_op jit(solution)/shard_map/ppermute | solution.py:283
  133.1 6.8 %all-to-all-start.1 = ((bf16[4,16,2304]{2,1,0:T(8,128)(2,1)}), bf16[4,16,2304]{2,1,0:T(8,128)(2,1)S(1)}, u32[]{:S(2)}, u32[]{:S(2)}) async-start(bf16[4,16,2304]{2,1,0:T(8,128)(2,1)} %pad_maximum_fusion.6), calls=%async_computation.1 | async-start | bytes 589824 | tf_op jit(solution)/shard_map/all_to_all | solution.py:275
  141.2 15.3 %all-to-all-done.1 = bf16[4,16,2304]{2,1,0:T(8,128)(2,1)S(1)} async-done(((bf16[4,16,2304]{2,1,0:T(8,128)(2,1)}), bf16[4,16,2304]{2,1,0:T(8,128)(2,1)S(1)}, u32[]{:S(2)}, u32[]{:S(2)}) %all-to-all-start.1) | async-done | bytes 294944 | tf_op jit(solution)/shard_map/all_to_all | solution.py:275
  158.3 1.9 collective-permute-start.11
  160.3 3.6 %collective-permute-start.12 = (bf16[8,3584]{1,0:T(8,128)(2,1)S(1)}, bf16[8,3584]{1,0:T(8,128)(2,1)S(1)}, u32[]{:S(2)}, u32[]{:S(2)}) collective-permute-start(bf16[8,3584]{1,0:T(8,128)(2,1)S(1)} %fusion.42), channel_id=1, source_target_pairs={{32,0},{64,32},{96,64},{128,96},{160,128},{192,160},{224,192},{256... | collective-permute-start | bytes 172040 | tf_op jit(solution)/shard_map/ppermute | solution.py:16
  166.2 18.6 %all_to_all.20 = bf16[4,16,2304]{2,1,0:T(8,128)(2,1)S(1)} all-to-all(bf16[4,16,2304]{2,1,0:T(8,128)(2,1)S(1)} %pad_maximum_fusion.7), channel_id=1, replica_groups={{0,8,20,28},{1,9,21,29},{2,10,22,30},{3,11,23,31},{4,12,16,24},{5,13,17..., dimensions={0} | all-to-all | bytes 589824 | tf_op jit(solution)/shard_map/all_to_all | solution.py:275
  184.8 6.6 %collective-permute-start.13 = (bf16[4,8,2304]{2,1,0:T(8,128)(2,1)S(1)}, bf16[4,8,2304]{2,1,0:T(8,128)(2,1)S(1)}, u32[]{:S(2)}, u32[]{:S(2)}) collective-permute-start(bf16[4,8,2304]{2,1,0:T(8,128)(2,1)S(1)} %get-tuple-element.86), channel_id=1, source_target_pairs={{0,4},{1,5},{2,6},{3,7},{4,0},{5,1},{6,2},{7,3},{8,12},{9,13},{10,... | collective-permute-start | bytes 442376 | tf_op jit(solution)/shard_map/ppermute | solution.py:283
  191.4 1.9 collective-permute-start.17
  193.3 2.0 collective-permute-done.13
  195.4 10.5 %collective-permute-start.14 = (bf16[8,8,2304]{2,1,0:T(8,128)(2,1)S(1)}, bf16[8,8,2304]{2,1,0:T(8,128)(2,1)S(1)}, u32[]{:S(2)}, u32[]{:S(2)}) collective-permute-start(bf16[8,8,2304]{2,1,0:T(8,128)(2,1)S(1)} %get-tuple-element.84), channel_id=1, source_target_pairs={{0,2},{1,3},{2,0},{3,1},{4,6},{5,7},{6,4},{7,5},{8,10},{9,11},{10,... | collective-permute-start | bytes 884744 | tf_op jit(solution)/shard_map/ppermute | solution.py:283
  206.0 3.1 %collective-permute-start.18 = (bf16[8,8,2304]{2,1,0:T(8,128)(2,1)S(1)}, bf16[8,8,2304]{2,1,0:T(8,128)(2,1)S(1)}, u32[]{:S(2)}, u32[]{:S(2)}) collective-permute-start(bf16[8,8,2304]{2,1,0:T(8,128)(2,1)S(1)} %get-tuple-element.88), channel_id=1, source_target_pairs={{0,2},{1,3},{2,0},{3,1},{4,6},{5,7},{6,4},{7,5},{8,10},{9,11},{10,... | collective-permute-start | bytes 884744 | tf_op jit(solution)/shard_map/ppermute | solution.py:283
  209.1 4.1 %collective-permute-done.14 = bf16[8,8,2304]{2,1,0:T(8,128)(2,1)S(1)} collective-permute-done((bf16[8,8,2304]{2,1,0:T(8,128)(2,1)S(1)}, bf16[8,8,2304]{2,1,0:T(8,128)(2,1)S(1)}, u32[]{:S(2)}, u32[]{:S(2)}) %collective-permute-start.14) | collective-permute-done | bytes 294944 | tf_op jit(solution)/shard_map/ppermute | solution.py:283
  213.2 1.5 shard_map.115
  214.7 4.4 %collective-permute-start.15 = (bf16[8,8,2304]{2,1,0:T(8,128)(2,1)S(1)}, bf16[8,8,2304]{2,1,0:T(8,128)(2,1)S(1)}, u32[]{:S(2)}, u32[]{:S(2)}) collective-permute-start(bf16[8,8,2304]{2,1,0:T(8,128)(2,1)S(1)} %bitcast.276), channel_id=1, source_target_pairs={{0,2},{1,3},{2,0},{3,1},{4,6},{5,7},{6,4},{7,5},{8,10},{9,11},{10,... | collective-permute-start | bytes 884744 | tf_op jit(solution)/shard_map/ppermute | solution.py:283
  219.5 3.2 %shard_map.116 = (bf16[64,2304]{1,0:T(8,128)(2,1)S(1)}, bf16[64,2304]{1,0:T(8,128)(2,1)S(1)}) custom-call(s32[1]{0:T(128)} %bitcast.29.part_ref, bf16[256,3584]{1,0:T(8,128)(2,1)S(1)} %copy-done.8, bf16[64,2304]{1,0:T(8,128)(2,1)S(1)} %get-tuple-element.89.near_ref, bf16[64,2304]{1,0:T(8,128)(2,1)S(1)} %bitcast.272, ...), custom_call_target="tpu_custom_call" | custom-call | flops 734003200 | bytes 8519680 | tf_op jit(solution)/shard_map/pallas_call | solution.py:231
  222.8 4.2 %collective-permute-start.19 = (bf16[8,8,2304]{2,1,0:T(8,128)(2,1)S(1)}, bf16[8,8,2304]{2,1,0:T(8,128)(2,1)S(1)}, u32[]{:S(2)}, u32[]{:S(2)}) collective-permute-start(bf16[8,8,2304]{2,1,0:T(8,128)(2,1)S(1)} %bitcast.277), channel_id=1, source_target_pairs={{0,2},{1,3},{2,0},{3,1},{4,6},{5,7},{6,4},{7,5},{8,10},{9,11},{10,... | collective-permute-start | bytes 884744 | tf_op jit(solution)/shard_map/ppermute | solution.py:283
  227.1 1.9 collective-permute-start.16
  229.0 5.7 %collective-permute-done.19 = bf16[8,8,2304]{2,1,0:T(8,128)(2,1)S(1)} collective-permute-done((bf16[8,8,2304]{2,1,0:T(8,128)(2,1)S(1)}, bf16[8,8,2304]{2,1,0:T(8,128)(2,1)S(1)}, u32[]{:S(2)}, u32[]{:S(2)}) %collective-permute-start.19) | collective-permute-done | bytes 294944 | tf_op jit(solution)/shard_map/ppermute | solution.py:283
  234.9 4.5 %collective-permute-start.20 = (bf16[4,8,2304]{2,1,0:T(8,128)(2,1)S(1)}, bf16[4,8,2304]{2,1,0:T(8,128)(2,1)S(1)}, u32[]{:S(2)}, u32[]{:S(2)}) collective-permute-start(bf16[4,8,2304]{2,1,0:T(8,128)(2,1)S(1)} %slice.635), channel_id=1, source_target_pairs={{0,4},{1,5},{2,6},{3,7},{4,0},{5,1},{6,2},{7,3},{8,12},{9,13},{10,... | collective-permute-start | bytes 442376 | tf_op jit(solution)/shard_map/ppermute | solution.py:283
  239.5 6.4 %collective-permute-done.20 = bf16[4,8,2304]{2,1,0:T(8,128)(2,1)S(1)} collective-permute-done((bf16[4,8,2304]{2,1,0:T(8,128)(2,1)S(1)}, bf16[4,8,2304]{2,1,0:T(8,128)(2,1)S(1)}, u32[]{:S(2)}, u32[]{:S(2)}) %collective-permute-start.20) | collective-permute-done | bytes 147488 | tf_op jit(solution)/shard_map/ppermute | solution.py:283
  246.6 5.1 %all-to-all-start.3 = ((bf16[4,16,2304]{2,1,0:T(8,128)(2,1)}), bf16[4,16,2304]{2,1,0:T(8,128)(2,1)S(1)}, u32[]{:S(2)}, u32[]{:S(2)}) async-start(bf16[4,16,2304]{2,1,0:T(8,128)(2,1)} %pad_maximum_fusion.10), calls=%async_computation.3 | async-start | bytes 589824 | tf_op jit(solution)/shard_map/all_to_all | solution.py:275
  252.2 19.2 %all-to-all-done.3 = bf16[4,16,2304]{2,1,0:T(8,128)(2,1)S(1)} async-done(((bf16[4,16,2304]{2,1,0:T(8,128)(2,1)}), bf16[4,16,2304]{2,1,0:T(8,128)(2,1)S(1)}, u32[]{:S(2)}, u32[]{:S(2)}) %all-to-all-start.3) | async-done | bytes 294944 | tf_op jit(solution)/shard_map/all_to_all | solution.py:275
  (301 shorter events, 21.7 us)
Async XLA Ops:
  7.2 6.1 %copy-start = (bf16[1,3584,4]{1,2,0:T(4,128)(2,1)S(1)}, bf16[1,3584,4]{1,2,0:T(4,128)(2,1)}, u32[]{:S(2)}) copy-start(bf16[1,3584,4]{1,2,0:T(4,128)(2,1)} %param.20) | copy-start | bytes 86020
  7.2 4.9 %copy-start.11 = (bf16[2,1,8,3584]{3,2,1,0:T(8,128)(2,1)S(1)}, bf16[2,1,8,3584]{3,2,1,0:T(8,128)(2,1)}, u32[]{:S(2)}) copy-start(bf16[2,1,8,3584]{3,2,1,0:T(8,128)(2,1)} %param.15) | copy-start | bytes 344068
  7.2 5.0 %copy-start.14 = (bf16[1,8,3584]{2,1,0:T(8,128)(2,1)S(1)}, bf16[1,8,3584]{2,1,0:T(8,128)(2,1)}, u32[]{:S(2)}) copy-start(bf16[1,8,3584]{2,1,0:T(8,128)(2,1)} %param.14) | copy-start | bytes 172036
  7.2 5.2 %copy-start.17 = (f32[1,3584]{1,0:T(1,128)S(1)}, f32[1,3584]{1,0:T(1,128)}, u32[]{:S(2)}) copy-start(f32[1,3584]{1,0:T(1,128)} %param.19) | copy-start | bytes 43012
  7.2 6.5 %copy-start.18 = (s32[2,1,8,2]{2,3,1,0:T(2,128)S(1)}, s32[2,1,8,2]{2,3,1,0:T(2,128)}, u32[]{:S(2)}) copy-start(s32[2,1,8,2]{2,3,1,0:T(2,128)} %param.18) | copy-start | bytes 388
  7.2 7.4 %copy-start.19 = (s32[2,1,8,2]{2,3,1,0:T(2,128)S(1)}, s32[2,1,8,2]{2,3,1,0:T(2,128)}, u32[]{:S(2)}) copy-start(s32[2,1,8,2]{2,3,1,0:T(2,128)} %param.17) | copy-start | bytes 388
  7.2 8.0 %copy-start.13 = (bf16[1,8,3584]{2,1,0:T(8,128)(2,1)S(1)}, bf16[1,8,3584]{2,1,0:T(8,128)(2,1)}, u32[]{:S(2)}) copy-start(bf16[1,8,3584]{2,1,0:T(8,128)(2,1)} %param.16) | copy-start | bytes 172036
  7.2 94.8 %all-gather.2.cloned.1.call-start = ((), (), s32[]{:S(2)}) async-start(), calls=%async_computation.4 | async-start | bytes 1949696 | tf_op jit(solution)/shard_map/all_gather | solution.py:352
  8.6 8.7 %copy-start.10 = (bf16[1,3584,128]{2,1,0:T(8,128)(2,1)S(1)}, bf16[1,3584,128]{2,1,0:T(8,128)(2,1)}, u32[]{:S(2)}) copy-start(bf16[1,3584,128]{2,1,0:T(8,128)(2,1)} %param.22) | copy-start | bytes 2752516
  8.6 15.8 %collective-permute-start = (bf16[1792,128]{1,0:T(8,128)(2,1)S(1)}, bf16[1792,128]{1,0:T(8,128)(2,1)S(1)}, u32[]{:S(2)}, u32[]{:S(2)}) collective-permute-start(bf16[1792,128]{1,0:T(8,128)(2,1)S(1)} %get-tuple-element.81), channel_id=1, source_target_pairs={{0,1},{1,0},{2,3},{3,2},{4,5},{5,4},{6,7},{7,6},{8,9},{9,8},{10,11... | collective-permute-start | bytes 1376264 | tf_op jit(solution)/shard_map/ppermute | solution.py:306
  24.4 4.1 %copy-start.15 = (bf16[1792,128]{1,0:T(8,128)(2,1)}, bf16[1792,128]{1,0:T(8,128)(2,1)S(1)}, u32[]{:S(2)}) copy-start(bf16[1792,128]{1,0:T(8,128)(2,1)S(1)} %collective-permute-done) | copy-start | bytes 1376260
  24.4 40.5 %collective-permute-start.1 = (bf16[5376,128]{1,0:T(8,128)(2,1)}, bf16[5376,128]{1,0:T(8,128)(2,1)S(1)}, u32[]{:S(2)}, u32[]{:S(2)}) collective-permute-start(bf16[5376,128]{1,0:T(8,128)(2,1)} %pad_maximum_fusion.2), channel_id=1, source_target_pairs={{0,1},{1,0},{2,3},{3,2},{4,5},{5,4},{6,7},{7,6},{8,9},{9,8},{10,11... | collective-permute-start | bytes 4128776 | tf_op jit(solution)/shard_map/ppermute | solution.py:308
  28.4 36.4 %all-to-all-start = ((bf16[4,16,2304]{2,1,0:T(8,128)(2,1)}), bf16[4,16,2304]{2,1,0:T(8,128)(2,1)S(1)}, u32[]{:S(2)}, u32[]{:S(2)}) async-start(bf16[4,16,2304]{2,1,0:T(8,128)(2,1)} %pad_maximum_fusion.3), calls=%async_computation | async-start | bytes 589824 | tf_op jit(solution)/shard_map/all_to_all | solution.py:275
  41.7 32.9 %copy-start.9 = (bf16[1,3584,128]{2,1,0:T(8,128)(2,1)S(1)}, bf16[1,3584,128]{2,1,0:T(8,128)(2,1)}, u32[]{:S(2)}) copy-start(bf16[1,3584,128]{2,1,0:T(8,128)(2,1)} %param.21) | copy-start | bytes 2752516
  64.8 9.8 %copy-start.16 = (bf16[1792,128]{1,0:T(8,128)(2,1)S(1)}, bf16[1792,128]{1,0:T(8,128)(2,1)}, u32[]{:S(2)}) copy-start(bf16[1792,128]{1,0:T(8,128)(2,1)} %copy-done.15) | copy-start | bytes 1376260
  64.9 14.0 %collective-permute-start.2 = (bf16[4,8,2304]{2,1,0:T(8,128)(2,1)S(1)}, bf16[4,8,2304]{2,1,0:T(8,128)(2,1)S(1)}, u32[]{:S(2)}, u32[]{:S(2)}) collective-permute-start(bf16[4,8,2304]{2,1,0:T(8,128)(2,1)S(1)} %get-tuple-element.94), channel_id=1, source_target_pairs={{0,4},{1,5},{2,6},{3,7},{4,0},{5,1},{6,2},{7,3},{8,12},{9,13},{10,... | collective-permute-start | bytes 442376 | tf_op jit(solution)/shard_map/ppermute | solution.py:283
  66.9 24.5 %collective-permute-start.4 = (bf16[128,3584]{1,0:T(8,128)(2,1)}, bf16[128,3584]{1,0:T(8,128)(2,1)S(1)}, u32[]{:S(2)}, u32[]{:S(2)}) collective-permute-start(bf16[128,3584]{1,0:T(8,128)(2,1)} %bitcast.282), channel_id=1, source_target_pairs={{0,1},{1,0},{2,3},{3,2},{4,5},{5,4},{6,7},{7,6},{8,9},{9,8},{10,11... | collective-permute-start | bytes 2752520 | tf_op jit(solution)/shard_map/ppermute | solution.py:309
  69.7 15.1 %collective-permute-start.7 = (bf16[4,8,2304]{2,1,0:T(8,128)(2,1)S(1)}, bf16[4,8,2304]{2,1,0:T(8,128)(2,1)S(1)}, u32[]{:S(2)}, u32[]{:S(2)}) collective-permute-start(bf16[4,8,2304]{2,1,0:T(8,128)(2,1)S(1)} %get-tuple-element.95), channel_id=1, source_target_pairs={{0,4},{1,5},{2,6},{3,7},{4,0},{5,1},{6,2},{7,3},{8,12},{9,13},{10,... | collective-permute-start | bytes 442376 | tf_op jit(solution)/shard_map/ppermute | solution.py:283
  76.3 17.9 %copy-start.1 = (bf16[3584,256]{1,0:T(8,128)(2,1)}, bf16[3584,256]{1,0:T(8,128)(2,1)S(1)}, u32[]{:S(2)}) copy-start(bf16[3584,256]{1,0:T(8,128)(2,1)S(1)} %get-tuple-element.157.up_ref) | copy-start | bytes 5505028
  76.3 15.1 %copy-start.12 = (bf16[1,128,3584]{2,1,0:T(8,128)(2,1)S(1)}, bf16[1,128,3584]{2,1,0:T(8,128)(2,1)}, u32[]{:S(2)}) copy-start(bf16[1,128,3584]{2,1,0:T(8,128)(2,1)} %param.23) | copy-start | bytes 2752516
  78.9 15.3 %collective-permute-start.3 = (bf16[8,8,2304]{2,1,0:T(8,128)(2,1)S(1)}, bf16[8,8,2304]{2,1,0:T(8,128)(2,1)S(1)}, u32[]{:S(2)}, u32[]{:S(2)}) collective-permute-start(bf16[8,8,2304]{2,1,0:T(8,128)(2,1)S(1)} %get-tuple-element.92), channel_id=1, source_target_pairs={{0,2},{1,3},{2,0},{3,1},{4,6},{5,7},{6,4},{7,5},{8,10},{9,11},{10,... | collective-permute-start | bytes 884744 | tf_op jit(solution)/shard_map/ppermute | solution.py:283
  85.6 19.2 %collective-permute-start.8 = (bf16[8,8,2304]{2,1,0:T(8,128)(2,1)}, bf16[8,8,2304]{2,1,0:T(8,128)(2,1)S(1)}, u32[]{:S(2)}, u32[]{:S(2)}) collective-permute-start(bf16[8,8,2304]{2,1,0:T(8,128)(2,1)} %get-tuple-element.96), channel_id=1, source_target_pairs={{0,2},{1,3},{2,0},{3,1},{4,6},{5,7},{6,4},{7,5},{8,10},{9,11},{10,... | collective-permute-start | bytes 884744 | tf_op jit(solution)/shard_map/ppermute | solution.py:283
  95.8 1.3 copy-start.4
  102.1 13.7 %collective-permute-start.5 = (bf16[8,8,2304]{2,1,0:T(8,128)(2,1)S(1)}, bf16[8,8,2304]{2,1,0:T(8,128)(2,1)}, u32[]{:S(2)}, u32[]{:S(2)}) collective-permute-start(bf16[8,8,2304]{2,1,0:T(8,128)(2,1)S(1)} %bitcast.275), channel_id=1, source_target_pairs={{0,2},{1,3},{2,0},{3,1},{4,6},{5,7},{6,4},{7,5},{8,10},{9,11},{10,... | collective-permute-start | bytes 884744 | tf_op jit(solution)/shard_map/ppermute | solution.py:283
  104.9 1.5 copy-start.2
  106.4 1.5 copy-start.5
  107.9 1.5 copy-start.7
  112.6 11.7 %collective-permute-start.9 = (bf16[8,8,2304]{2,1,0:T(8,128)(2,1)S(1)}, bf16[8,8,2304]{2,1,0:T(8,128)(2,1)S(1)}, u32[]{:S(2)}, u32[]{:S(2)}) collective-permute-start(bf16[8,8,2304]{2,1,0:T(8,128)(2,1)S(1)} %bitcast.278), channel_id=1, source_target_pairs={{0,2},{1,3},{2,0},{3,1},{4,6},{5,7},{6,4},{7,5},{8,10},{9,11},{10,... | collective-permute-start | bytes 884744 | tf_op jit(solution)/shard_map/ppermute | solution.py:283
  116.8 9.7 %collective-permute-start.6 = (bf16[4,8,2304]{2,1,0:T(8,128)(2,1)S(1)}, bf16[4,8,2304]{2,1,0:T(8,128)(2,1)S(1)}, u32[]{:S(2)}, u32[]{:S(2)}) collective-permute-start(bf16[4,8,2304]{2,1,0:T(8,128)(2,1)S(1)} %slice.578), channel_id=1, source_target_pairs={{0,4},{1,5},{2,6},{3,7},{4,0},{5,1},{6,2},{7,3},{8,12},{9,13},{10,... | collective-permute-start | bytes 442376 | tf_op jit(solution)/shard_map/ppermute | solution.py:283
  124.4 7.9 %collective-permute-start.10 = (bf16[4,8,2304]{2,1,0:T(8,128)(2,1)S(1)}, bf16[4,8,2304]{2,1,0:T(8,128)(2,1)S(1)}, u32[]{:S(2)}, u32[]{:S(2)}) collective-permute-start(bf16[4,8,2304]{2,1,0:T(8,128)(2,1)S(1)} %slice.580), channel_id=1, source_target_pairs={{0,4},{1,5},{2,6},{3,7},{4,0},{5,1},{6,2},{7,3},{8,12},{9,13},{10,... | collective-permute-start | bytes 442376 | tf_op jit(solution)/shard_map/ppermute | solution.py:283
  133.1 23.3 %all-to-all-start.1 = ((bf16[4,16,2304]{2,1,0:T(8,128)(2,1)}), bf16[4,16,2304]{2,1,0:T(8,128)(2,1)S(1)}, u32[]{:S(2)}, u32[]{:S(2)}) async-start(bf16[4,16,2304]{2,1,0:T(8,128)(2,1)} %pad_maximum_fusion.6), calls=%async_computation.1 | async-start | bytes 589824 | tf_op jit(solution)/shard_map/all_to_all | solution.py:275
  158.3 5.6 %collective-permute-start.11 = (bf16[8,3584]{1,0:T(8,128)(2,1)S(1)}, bf16[8,3584]{1,0:T(8,128)(2,1)S(1)}, u32[]{:S(2)}, u32[]{:S(2)}) collective-permute-start(bf16[8,3584]{1,0:T(8,128)(2,1)S(1)} %fusion.49), channel_id=1, source_target_pairs={{480,0},{0,32},{32,64},{64,96},{96,128},{128,160},{160,192},{192,2... | collective-permute-start | bytes 172040 | tf_op jit(solution)/shard_map/ppermute | solution.py:16
  160.3 5.4 %collective-permute-start.12 = (bf16[8,3584]{1,0:T(8,128)(2,1)S(1)}, bf16[8,3584]{1,0:T(8,128)(2,1)S(1)}, u32[]{:S(2)}, u32[]{:S(2)}) collective-permute-start(bf16[8,3584]{1,0:T(8,128)(2,1)S(1)} %fusion.42), channel_id=1, source_target_pairs={{32,0},{64,32},{96,64},{128,96},{160,128},{192,160},{224,192},{256... | collective-permute-start | bytes 172040 | tf_op jit(solution)/shard_map/ppermute | solution.py:16
  166.1 47.1 %copy-start.6 = (bf16[256,3584]{1,0:T(8,128)(2,1)S(1)}, bf16[256,3584]{1,0:T(8,128)(2,1)}, u32[]{:S(2)}) copy-start(bf16[256,3584]{1,0:T(8,128)(2,1)} %copy-done.4) | copy-start | bytes 5505028
  166.1 47.1 %copy-start.3 = (bf16[3584,256]{1,0:T(8,128)(2,1)S(1)}, bf16[3584,256]{1,0:T(8,128)(2,1)}, u32[]{:S(2)}) copy-start(bf16[3584,256]{1,0:T(8,128)(2,1)} %copy-done.1) | copy-start | bytes 5505028
  184.8 10.6 %collective-permute-start.13 = (bf16[4,8,2304]{2,1,0:T(8,128)(2,1)S(1)}, bf16[4,8,2304]{2,1,0:T(8,128)(2,1)S(1)}, u32[]{:S(2)}, u32[]{:S(2)}) collective-permute-start(bf16[4,8,2304]{2,1,0:T(8,128)(2,1)S(1)} %get-tuple-element.86), channel_id=1, source_target_pairs={{0,4},{1,5},{2,6},{3,7},{4,0},{5,1},{6,2},{7,3},{8,12},{9,13},{10,... | collective-permute-start | bytes 442376 | tf_op jit(solution)/shard_map/ppermute | solution.py:283
  191.4 14.5 %collective-permute-start.17 = (bf16[4,8,2304]{2,1,0:T(8,128)(2,1)S(1)}, bf16[4,8,2304]{2,1,0:T(8,128)(2,1)S(1)}, u32[]{:S(2)}, u32[]{:S(2)}) collective-permute-start(bf16[4,8,2304]{2,1,0:T(8,128)(2,1)S(1)} %get-tuple-element.87), channel_id=1, source_target_pairs={{0,4},{1,5},{2,6},{3,7},{4,0},{5,1},{6,2},{7,3},{8,12},{9,13},{10,... | collective-permute-start | bytes 442376 | tf_op jit(solution)/shard_map/ppermute | solution.py:283
  195.4 17.8 %collective-permute-start.14 = (bf16[8,8,2304]{2,1,0:T(8,128)(2,1)S(1)}, bf16[8,8,2304]{2,1,0:T(8,128)(2,1)S(1)}, u32[]{:S(2)}, u32[]{:S(2)}) collective-permute-start(bf16[8,8,2304]{2,1,0:T(8,128)(2,1)S(1)} %get-tuple-element.84), channel_id=1, source_target_pairs={{0,2},{1,3},{2,0},{3,1},{4,6},{5,7},{6,4},{7,5},{8,10},{9,11},{10,... | collective-permute-start | bytes 884744 | tf_op jit(solution)/shard_map/ppermute | solution.py:283
  206.0 13.5 %collective-permute-start.18 = (bf16[8,8,2304]{2,1,0:T(8,128)(2,1)S(1)}, bf16[8,8,2304]{2,1,0:T(8,128)(2,1)S(1)}, u32[]{:S(2)}, u32[]{:S(2)}) collective-permute-start(bf16[8,8,2304]{2,1,0:T(8,128)(2,1)S(1)} %get-tuple-element.88), channel_id=1, source_target_pairs={{0,2},{1,3},{2,0},{3,1},{4,6},{5,7},{6,4},{7,5},{8,10},{9,11},{10,... | collective-permute-start | bytes 884744 | tf_op jit(solution)/shard_map/ppermute | solution.py:283
  213.2 6.3 %copy-start.8 = (bf16[256,3584]{1,0:T(8,128)(2,1)S(1)}, bf16[256,3584]{1,0:T(8,128)(2,1)}, u32[]{:S(2)}) copy-start(bf16[256,3584]{1,0:T(8,128)(2,1)} %all-gather.2.cloned.1.call-done.saved_ref) | copy-start | bytes 5505028
  214.7 12.3 %collective-permute-start.15 = (bf16[8,8,2304]{2,1,0:T(8,128)(2,1)S(1)}, bf16[8,8,2304]{2,1,0:T(8,128)(2,1)S(1)}, u32[]{:S(2)}, u32[]{:S(2)}) collective-permute-start(bf16[8,8,2304]{2,1,0:T(8,128)(2,1)S(1)} %bitcast.276), channel_id=1, source_target_pairs={{0,2},{1,3},{2,0},{3,1},{4,6},{5,7},{6,4},{7,5},{8,10},{9,11},{10,... | collective-permute-start | bytes 884744 | tf_op jit(solution)/shard_map/ppermute | solution.py:283
  222.8 12.0 %collective-permute-start.19 = (bf16[8,8,2304]{2,1,0:T(8,128)(2,1)S(1)}, bf16[8,8,2304]{2,1,0:T(8,128)(2,1)S(1)}, u32[]{:S(2)}, u32[]{:S(2)}) collective-permute-start(bf16[8,8,2304]{2,1,0:T(8,128)(2,1)S(1)} %bitcast.277), channel_id=1, source_target_pairs={{0,2},{1,3},{2,0},{3,1},{4,6},{5,7},{6,4},{7,5},{8,10},{9,11},{10,... | collective-permute-start | bytes 884744 | tf_op jit(solution)/shard_map/ppermute | solution.py:283
  227.1 12.3 %collective-permute-start.16 = (bf16[4,8,2304]{2,1,0:T(8,128)(2,1)S(1)}, bf16[4,8,2304]{2,1,0:T(8,128)(2,1)S(1)}, u32[]{:S(2)}, u32[]{:S(2)}) collective-permute-start(bf16[4,8,2304]{2,1,0:T(8,128)(2,1)S(1)} %slice.632), channel_id=1, source_target_pairs={{0,4},{1,5},{2,6},{3,7},{4,0},{5,1},{6,2},{7,3},{8,12},{9,13},{10,... | collective-permute-start | bytes 442376 | tf_op jit(solution)/shard_map/ppermute | solution.py:283
  234.9 11.0 %collective-permute-start.20 = (bf16[4,8,2304]{2,1,0:T(8,128)(2,1)S(1)}, bf16[4,8,2304]{2,1,0:T(8,128)(2,1)S(1)}, u32[]{:S(2)}, u32[]{:S(2)}) collective-permute-start(bf16[4,8,2304]{2,1,0:T(8,128)(2,1)S(1)} %slice.635), channel_id=1, source_target_pairs={{0,4},{1,5},{2,6},{3,7},{4,0},{5,1},{6,2},{7,3},{8,12},{9,13},{10,... | collective-permute-start | bytes 442376 | tf_op jit(solution)/shard_map/ppermute | solution.py:283
  246.6 24.7 %all-to-all-start.3 = ((bf16[4,16,2304]{2,1,0:T(8,128)(2,1)}), bf16[4,16,2304]{2,1,0:T(8,128)(2,1)S(1)}, u32[]{:S(2)}, u32[]{:S(2)}) async-start(bf16[4,16,2304]{2,1,0:T(8,128)(2,1)} %pad_maximum_fusion.10), calls=%async_computation.3 | async-start | bytes 589824 | tf_op jit(solution)/shard_map/all_to_all | solution.py:275
Sparse Core Ops, SparseCore 0:
  13.4 88.6 all-gather.1

commit v5 on v4

--- a/solution.py
+++ b/solution.py
@@ -294,9 +294,13 @@
         count = parts.shape[0] // 2
         return add(parts[:count], across(parts[count:], 2))
 
-    def dispatch(*slabs, first=(), then=()):
+    def dispatch(*slabs, first=(), then=(), turns=False):
         held = after(swap(after(jnp.concatenate(slabs, axis=1), *first), far), *then)
-        return [spread_near(held[:, 8 * i:8 * i + 8]) for i in range(len(slabs))]
+        spread = []
+        for i in range(len(slabs)):
+            ahead = [spread[-1][0]] if turns and spread else []
+            spread.append(spread_near(after(held[:, 8 * i:8 * i + 8], *ahead)))
+        return spread
 
     def gather_back(*slabs, then=((), ())):
         held = swap(jnp.concatenate([gather_near(*slab, then[i]) for i, slab in enumerate(slabs)], axis=1), far)
@@ -383,6 +387,7 @@
             rows_f, rows_c = dispatch(
                 pack_rows(normed, fwd_spreads[t + 1], 1),
                 pack_rows(cotan_in, bwd_spreads[t + 1], 1, saved[t + 1][1]),
+                turns=True,
             )
     return (fwd_result[None], bwd_result[None])
 

time: 282 us -> 283 us (level)
  the two profiles are of different devices: /device:TPU:62 before, /device:TPU:60 now
where the time goes in v5:
time: 283 us; the launch traced here: 282 us
  waiting for transfers between devices  108 us (38%)
  starting transfers between devices  97 us (34%)
  blocking collectives  23.1 us (8%)
  between operations  15.7 us (6%)
  other arithmetic  12 us (4%)
  local copies, waits for them, and re-layouts  11.3 us (4%)
  Pallas kernels  9.55 us (3%)
  matrix products  4.63 us (2%)
    ppermute x16, starting transfers between devices, across(): lax.ppermute(value, 'expert', [(i, i ^ 2 * bit) for i in range(ranks)])  57.3 us
    all_to_all x3, waiting for transfers between devices, swap(): lax.all_to_all(slabs, 'expert', split_axis=0, concat_axis=0, axis_index_g...  55.8 us
    ppermute x16, waiting for transfers between devices, across(): lax.ppermute(value, 'expert', [(i, i ^ 2 * bit) for i in range(ranks)])  38.5 us
    all_to_all x3, starting transfers between devices, swap(): lax.all_to_all(slabs, 'expert', split_axis=0, concat_axis=0, axis_index_g...  24.6 us
    all_to_all x1, blocking collectives, swap(): lax.all_to_all(slabs, 'expert', split_axis=0, concat_axis=0, axis_index_g...  23.1 us
    pallas_call x4, Pallas kernels, run_kernel(): pl.pallas_call(kernel, out_shape=[jax.ShapeDtypeStruct(near.shape, BF16)]...  9.55 us
    ppermute x1, waiting for transfers between devices, local(): gate_r0 = lax.ppermute(w_gate[0, :half], 'expert', partner)  6.36 us
    unnamed x89, local copies, waits for them, and re-layouts  5.99 us
  transfers between devices with their start and end apart: 25, of which 15 were waited for; matrix products, arithmetic and copies ran while one was open for 5% of the time, Pallas kernels for 3%

profile of v5, /device:TPU:60, one launch (start us, length us, event | category | flops | bytes accessed | tf_op | source)
XLA Modules:
  0.0 281.7 jit_solution(13781600625600399165)
XLA Ops:
  7.3 1.3 slice_bitcast_fusion
  8.6 2.5 collective-permute-start
  18.0 6.4 %collective-permute-done = bf16[1792,128]{1,0:T(8,128)(2,1)S(1)} collective-permute-done((bf16[1792,128]{1,0:T(8,128)(2,1)S(1)}, bf16[1792,128]{1,0:T(8,128)(2,1)S(1)}, u32[]{:S(2)}, u32[]{:S(2)}) %collective-permute-start) | collective-permute-done | bytes 458784 | tf_op jit(solution)/shard_map/ppermute | solution.py:310
  24.4 2.4 collective-permute-start.1
  27.5 13.3 %all-to-all-start = ((bf16[4,16,2304]{2,1,0:T(8,128)(2,1)}), bf16[4,16,2304]{2,1,0:T(8,128)(2,1)S(1)}, u32[]{:S(2)}, u32[]{:S(2)}) async-start(bf16[4,16,2304]{2,1,0:T(8,128)(2,1)} %pad_maximum_fusion.3), calls=%async_computation | async-start | bytes 589824 | tf_op jit(solution)/shard_map/all_to_all | solution.py:275
  40.8 22.1 %all-to-all-done = bf16[4,16,2304]{2,1,0:T(8,128)(2,1)S(1)} async-done(((bf16[4,16,2304]{2,1,0:T(8,128)(2,1)}), bf16[4,16,2304]{2,1,0:T(8,128)(2,1)S(1)}, u32[]{:S(2)}, u32[]{:S(2)}) %all-to-all-start) | async-done | bytes 294944 | tf_op jit(solution)/shard_map/all_to_all | solution.py:275
  62.9 2.1 collective-permute-start.2
  65.0 4.6 %collective-permute-start.4 = (bf16[128,3584]{1,0:T(8,128)(2,1)}, bf16[128,3584]{1,0:T(8,128)(2,1)S(1)}, u32[]{:S(2)}, u32[]{:S(2)}) collective-permute-start(bf16[128,3584]{1,0:T(8,128)(2,1)} %bitcast.282), channel_id=1, source_target_pairs={{0,1},{1,0},{2,3},{3,2},{4,5},{5,4},{6,7},{7,6},{8,9},{9,8},{10,11... | collective-permute-start | bytes 2752520 | tf_op jit(solution)/shard_map/ppermute | solution.py:313
  69.6 4.8 %collective-permute-start.7 = (bf16[4,8,2304]{2,1,0:T(8,128)(2,1)S(1)}, bf16[4,8,2304]{2,1,0:T(8,128)(2,1)S(1)}, u32[]{:S(2)}, u32[]{:S(2)}) collective-permute-start(bf16[4,8,2304]{2,1,0:T(8,128)(2,1)S(1)} %get-tuple-element.95), channel_id=1, source_target_pairs={{0,4},{1,5},{2,6},{3,7},{4,0},{5,1},{6,2},{7,3},{8,12},{9,13},{10,... | collective-permute-start | bytes 442376 | tf_op jit(solution)/shard_map/ppermute | solution.py:283
  74.6 1.6 maximum_maximum_fusion
  76.3 6.0 %collective-permute-start.3 = (bf16[8,8,2304]{2,1,0:T(8,128)(2,1)S(1)}, bf16[8,8,2304]{2,1,0:T(8,128)(2,1)S(1)}, u32[]{:S(2)}, u32[]{:S(2)}) collective-permute-start(bf16[8,8,2304]{2,1,0:T(8,128)(2,1)S(1)} %get-tuple-element.92), channel_id=1, source_target_pairs={{0,2},{1,3},{2,0},{3,1},{4,6},{5,7},{6,4},{7,5},{8,10},{9,11},{10,... | collective-permute-start | bytes 884744 | tf_op jit(solution)/shard_map/ppermute | solution.py:283
  83.0 4.0 %collective-permute-start.8 = (bf16[8,8,2304]{2,1,0:T(8,128)(2,1)}, bf16[8,8,2304]{2,1,0:T(8,128)(2,1)S(1)}, u32[]{:S(2)}, u32[]{:S(2)}) collective-permute-start(bf16[8,8,2304]{2,1,0:T(8,128)(2,1)} %get-tuple-element.96), channel_id=1, source_target_pairs={{0,2},{1,3},{2,0},{3,1},{4,6},{5,7},{6,4},{7,5},{8,10},{9,11},{10,... | collective-permute-start | bytes 884744 | tf_op jit(solution)/shard_map/ppermute | solution.py:283
  87.0 2.1 collective-permute-done.4
  89.3 3.0 %collective-permute-done.3 = bf16[8,8,2304]{2,1,0:T(8,128)(2,1)S(1)} collective-permute-done((bf16[8,8,2304]{2,1,0:T(8,128)(2,1)S(1)}, bf16[8,8,2304]{2,1,0:T(8,128)(2,1)S(1)}, u32[]{:S(2)}, u32[]{:S(2)}) %collective-permute-start.3) | collective-permute-done | bytes 294944 | tf_op jit(solution)/shard_map/ppermute | solution.py:283
  92.2 1.5 shard_map.113
  95.0 5.2 %all-gather.2.cloned.1.call-done.saved_ref = bf16[256,3584]{1,0:T(8,128)(2,1)} async-done(((bf16[16,3584]{1,0:T(8,128)(2,1)}), bf16[256,3584]{1,0:T(8,128)(2,1)}) %all-gather.2.cloned.1.call-update) | async-done | bytes 1835024 | tf_op jit(solution)/shard_map/all_gather | solution.py:356
  100.2 5.1 %collective-permute-start.5 = (bf16[8,8,2304]{2,1,0:T(8,128)(2,1)S(1)}, bf16[8,8,2304]{2,1,0:T(8,128)(2,1)}, u32[]{:S(2)}, u32[]{:S(2)}) collective-permute-start(bf16[8,8,2304]{2,1,0:T(8,128)(2,1)S(1)} %bitcast.275), channel_id=1, source_target_pairs={{0,2},{1,3},{2,0},{3,1},{4,6},{5,7},{6,4},{7,5},{8,10},{9,11},{10,... | collective-permute-start | bytes 884744 | tf_op jit(solution)/shard_map/ppermute | solution.py:283
  105.4 1.5 copy-done.2
  106.9 1.5 copy-done.5
  108.4 1.5 copy-done.7
  109.9 3.2 %shard_map.114 = (bf16[64,2304]{1,0:T(8,128)(2,1)S(1)}, bf16[64,2304]{1,0:T(8,128)(2,1)S(1)}) custom-call(s32[1]{0:T(128)} %bitcast.29.part_ref, bf16[256,3584]{1,0:T(8,128)(2,1)S(1)} %copy-done.7, bf16[64,2304]{1,0:T(8,128)(2,1)S(1)} %get-tuple-element.97.near_ref, bf16[64,2304]{1,0:T(8,128)(2,1)S(1)} %bitcast.271, ...), custom_call_target="tpu_custom_call" | custom-call | flops 734003200 | bytes 8519680 | tf_op jit(solution)/shard_map/pallas_call | solution.py:231
  113.2 1.9 collective-permute-start.9
  116.2 2.9 %collective-permute-start.6 = (bf16[4,8,2304]{2,1,0:T(8,128)(2,1)S(1)}, bf16[4,8,2304]{2,1,0:T(8,128)(2,1)S(1)}, u32[]{:S(2)}, u32[]{:S(2)}) collective-permute-start(bf16[4,8,2304]{2,1,0:T(8,128)(2,1)S(1)} %slice.578), channel_id=1, source_target_pairs={{0,4},{1,5},{2,6},{3,7},{4,0},{5,1},{6,2},{7,3},{8,12},{9,13},{10,... | collective-permute-start | bytes 442376 | tf_op jit(solution)/shard_map/ppermute | solution.py:283
  119.1 4.3 %collective-permute-done.9 = bf16[8,8,2304]{2,1,0:T(8,128)(2,1)S(1)} collective-permute-done((bf16[8,8,2304]{2,1,0:T(8,128)(2,1)S(1)}, bf16[8,8,2304]{2,1,0:T(8,128)(2,1)S(1)}, u32[]{:S(2)}, u32[]{:S(2)}) %collective-permute-start.9) | collective-permute-done | bytes 294944 | tf_op jit(solution)/shard_map/ppermute | solution.py:283
  123.5 4.2 %collective-permute-start.10 = (bf16[4,8,2304]{2,1,0:T(8,128)(2,1)S(1)}, bf16[4,8,2304]{2,1,0:T(8,128)(2,1)S(1)}, u32[]{:S(2)}, u32[]{:S(2)}) collective-permute-start(bf16[4,8,2304]{2,1,0:T(8,128)(2,1)S(1)} %slice.580), channel_id=1, source_target_pairs={{0,4},{1,5},{2,6},{3,7},{4,0},{5,1},{6,2},{7,3},{8,12},{9,13},{10,... | collective-permute-start | bytes 442376 | tf_op jit(solution)/shard_map/ppermute | solution.py:283
  127.8 3.7 %collective-permute-done.10 = bf16[4,8,2304]{2,1,0:T(8,128)(2,1)S(1)} collective-permute-done((bf16[4,8,2304]{2,1,0:T(8,128)(2,1)S(1)}, bf16[4,8,2304]{2,1,0:T(8,128)(2,1)S(1)}, u32[]{:S(2)}, u32[]{:S(2)}) %collective-permute-start.10) | collective-permute-done | bytes 147488 | tf_op jit(solution)/shard_map/ppermute | solution.py:283
  132.3 6.7 %all-to-all-start.1 = ((bf16[4,16,2304]{2,1,0:T(8,128)(2,1)}), bf16[4,16,2304]{2,1,0:T(8,128)(2,1)S(1)}, u32[]{:S(2)}, u32[]{:S(2)}) async-start(bf16[4,16,2304]{2,1,0:T(8,128)(2,1)} %pad_maximum_fusion.6), calls=%async_computation.1 | async-start | bytes 589824 | tf_op jit(solution)/shard_map/all_to_all | solution.py:275
  140.3 16.4 %all-to-all-done.1 = bf16[4,16,2304]{2,1,0:T(8,128)(2,1)S(1)} async-done(((bf16[4,16,2304]{2,1,0:T(8,128)(2,1)}), bf16[4,16,2304]{2,1,0:T(8,128)(2,1)S(1)}, u32[]{:S(2)}, u32[]{:S(2)}) %all-to-all-start.1) | async-done | bytes 294944 | tf_op jit(solution)/shard_map/all_to_all | solution.py:275
  158.6 1.9 collective-permute-start.11
  160.6 3.6 %collective-permute-start.12 = (bf16[8,3584]{1,0:T(8,128)(2,1)S(1)}, bf16[8,3584]{1,0:T(8,128)(2,1)S(1)}, u32[]{:S(2)}, u32[]{:S(2)}) collective-permute-start(bf16[8,3584]{1,0:T(8,128)(2,1)S(1)} %fusion.42), channel_id=1, source_target_pairs={{32,0},{64,32},{96,64},{128,96},{160,128},{192,160},{224,192},{256... | collective-permute-start | bytes 172040 | tf_op jit(solution)/shard_map/ppermute | solution.py:16
  166.4 23.1 %all_to_all.20 = bf16[4,16,2304]{2,1,0:T(8,128)(2,1)S(1)} all-to-all(bf16[4,16,2304]{2,1,0:T(8,128)(2,1)S(1)} %pad_maximum_fusion.7), channel_id=1, replica_groups={{0,8,20,28},{1,9,21,29},{2,10,22,30},{3,11,23,31},{4,12,16,24},{5,13,17..., dimensions={0} | all-to-all | bytes 589824 | tf_op jit(solution)/shard_map/all_to_all | solution.py:275
  189.6 1.9 collective-permute-start.13
  191.5 7.3 %collective-permute-done.13 = bf16[4,8,2304]{2,1,0:T(8,128)(2,1)S(1)} collective-permute-done((bf16[4,8,2304]{2,1,0:T(8,128)(2,1)S(1)}, bf16[4,8,2304]{2,1,0:T(8,128)(2,1)S(1)}, u32[]{:S(2)}, u32[]{:S(2)}) %collective-permute-start.13) | collective-permute-done | bytes 147488 | tf_op jit(solution)/shard_map/ppermute | solution.py:283
  198.8 4.4 %collective-permute-start.14 = (bf16[8,8,2304]{2,1,0:T(8,128)(2,1)S(1)}, bf16[8,8,2304]{2,1,0:T(8,128)(2,1)S(1)}, u32[]{:S(2)}, u32[]{:S(2)}) collective-permute-start(bf16[8,8,2304]{2,1,0:T(8,128)(2,1)S(1)} %get-tuple-element.87), channel_id=1, source_target_pairs={{0,2},{1,3},{2,0},{3,1},{4,6},{5,7},{6,4},{7,5},{8,10},{9,11},{10,... | collective-permute-start | bytes 884744 | tf_op jit(solution)/shard_map/ppermute | solution.py:283
  203.2 2.8 collective-permute-start.17
  206.0 8.3 %collective-permute-done.17 = bf16[4,8,2304]{2,1,0:T(8,128)(2,1)S(1)} collective-permute-done((bf16[4,8,2304]{2,1,0:T(8,128)(2,1)S(1)}, bf16[4,8,2304]{2,1,0:T(8,128)(2,1)S(1)}, u32[]{:S(2)}, u32[]{:S(2)}) %collective-permute-start.17) | collective-permute-done | bytes 147488 | tf_op jit(solution)/shard_map/ppermute | solution.py:283
  214.4 1.9 collective-permute-start.18
  216.4 1.5 shard_map.115
  217.9 4.1 %collective-permute-start.15 = (bf16[8,8,2304]{2,1,0:T(8,128)(2,1)S(1)}, bf16[8,8,2304]{2,1,0:T(8,128)(2,1)S(1)}, u32[]{:S(2)}, u32[]{:S(2)}) collective-permute-start(bf16[8,8,2304]{2,1,0:T(8,128)(2,1)S(1)} %bitcast.277), channel_id=1, source_target_pairs={{0,2},{1,3},{2,0},{3,1},{4,6},{5,7},{6,4},{7,5},{8,10},{9,11},{10,... | collective-permute-start | bytes 884744 | tf_op jit(solution)/shard_map/ppermute | solution.py:283
  222.0 4.2 %collective-permute-done.18 = bf16[8,8,2304]{2,1,0:T(8,128)(2,1)S(1)} collective-permute-done((bf16[8,8,2304]{2,1,0:T(8,128)(2,1)S(1)}, bf16[8,8,2304]{2,1,0:T(8,128)(2,1)S(1)}, u32[]{:S(2)}, u32[]{:S(2)}) %collective-permute-start.18) | collective-permute-done | bytes 294944 | tf_op jit(solution)/shard_map/ppermute | solution.py:283
  226.2 3.2 %shard_map.116 = (bf16[64,2304]{1,0:T(8,128)(2,1)S(1)}, bf16[64,2304]{1,0:T(8,128)(2,1)S(1)}) custom-call(s32[1]{0:T(128)} %bitcast.29.part_ref, bf16[256,3584]{1,0:T(8,128)(2,1)S(1)} %copy-done.8, bf16[64,2304]{1,0:T(8,128)(2,1)S(1)} %bitcast.270, bf16[64,2304]{1,0:T(8,128)(2,1)S(1)} %bitcast.274, bf16[3584,256]{1,0:T(8,128)(2,1)S(1)} %get-tuple-element.156.gate_ref, ...), custom_call_target="tpu_custom_call" | custom-call | flops 734003200 | bytes 8519680 | tf_op jit(solution)/shard_map/pallas_call | solution.py:231
  229.5 1.9 collective-permute-start.19
  231.5 4.5 %collective-permute-start.16 = (bf16[4,8,2304]{2,1,0:T(8,128)(2,1)S(1)}, bf16[4,8,2304]{2,1,0:T(8,128)(2,1)S(1)}, u32[]{:S(2)}, u32[]{:S(2)}) collective-permute-start(bf16[4,8,2304]{2,1,0:T(8,128)(2,1)S(1)} %slice.632), channel_id=1, source_target_pairs={{0,4},{1,5},{2,6},{3,7},{4,0},{5,1},{6,2},{7,3},{8,12},{9,13},{10,... | collective-permute-start | bytes 442376 | tf_op jit(solution)/shard_map/ppermute | solution.py:283
  236.0 3.7 %collective-permute-done.19 = bf16[8,8,2304]{2,1,0:T(8,128)(2,1)S(1)} collective-permute-done((bf16[8,8,2304]{2,1,0:T(8,128)(2,1)S(1)}, bf16[8,8,2304]{2,1,0:T(8,128)(2,1)S(1)}, u32[]{:S(2)}, u32[]{:S(2)}) %collective-permute-start.19) | collective-permute-done | bytes 294944 | tf_op jit(solution)/shard_map/ppermute | solution.py:283
  239.8 4.8 %collective-permute-start.20 = (bf16[4,8,2304]{2,1,0:T(8,128)(2,1)S(1)}, bf16[4,8,2304]{2,1,0:T(8,128)(2,1)S(1)}, u32[]{:S(2)}, u32[]{:S(2)}) collective-permute-start(bf16[4,8,2304]{2,1,0:T(8,128)(2,1)S(1)} %slice.635), channel_id=1, source_target_pairs={{0,4},{1,5},{2,6},{3,7},{4,0},{5,1},{6,2},{7,3},{8,12},{9,13},{10,... | collective-permute-start | bytes 442376 | tf_op jit(solution)/shard_map/ppermute | solution.py:283
  244.6 4.0 %collective-permute-done.20 = bf16[4,8,2304]{2,1,0:T(8,128)(2,1)S(1)} collective-permute-done((bf16[4,8,2304]{2,1,0:T(8,128)(2,1)S(1)}, bf16[4,8,2304]{2,1,0:T(8,128)(2,1)S(1)}, u32[]{:S(2)}, u32[]{:S(2)}) %collective-permute-start.20) | collective-permute-done | bytes 147488 | tf_op jit(solution)/shard_map/ppermute | solution.py:283
  249.4 4.6 %all-to-all-start.3 = ((bf16[4,16,2304]{2,1,0:T(8,128)(2,1)}), bf16[4,16,2304]{2,1,0:T(8,128)(2,1)S(1)}, u32[]{:S(2)}, u32[]{:S(2)}) async-start(bf16[4,16,2304]{2,1,0:T(8,128)(2,1)} %pad_maximum_fusion.9), calls=%async_computation.3 | async-start | bytes 589824 | tf_op jit(solution)/shard_map/all_to_all | solution.py:275
  254.4 17.3 %all-to-all-done.3 = bf16[4,16,2304]{2,1,0:T(8,128)(2,1)S(1)} async-done(((bf16[4,16,2304]{2,1,0:T(8,128)(2,1)}), bf16[4,16,2304]{2,1,0:T(8,128)(2,1)S(1)}, u32[]{:S(2)}, u32[]{:S(2)}) %all-to-all-start.3) | async-done | bytes 294944 | tf_op jit(solution)/shard_map/all_to_all | solution.py:275
  (302 shorter events, 21.1 us)
Async XLA Ops:
  7.2 5.2 %copy-start = (bf16[1,3584,4]{1,2,0:T(4,128)(2,1)S(1)}, bf16[1,3584,4]{1,2,0:T(4,128)(2,1)}, u32[]{:S(2)}) copy-start(bf16[1,3584,4]{1,2,0:T(4,128)(2,1)} %param.20) | copy-start | bytes 86020
  7.2 4.0 %copy-start.11 = (bf16[2,1,8,3584]{3,2,1,0:T(8,128)(2,1)S(1)}, bf16[2,1,8,3584]{3,2,1,0:T(8,128)(2,1)}, u32[]{:S(2)}) copy-start(bf16[2,1,8,3584]{3,2,1,0:T(8,128)(2,1)} %param.15) | copy-start | bytes 344068
  7.2 4.1 %copy-start.14 = (bf16[1,8,3584]{2,1,0:T(8,128)(2,1)S(1)}, bf16[1,8,3584]{2,1,0:T(8,128)(2,1)}, u32[]{:S(2)}) copy-start(bf16[1,8,3584]{2,1,0:T(8,128)(2,1)} %param.14) | copy-start | bytes 172036
  7.2 4.3 %copy-start.17 = (f32[1,3584]{1,0:T(1,128)S(1)}, f32[1,3584]{1,0:T(1,128)}, u32[]{:S(2)}) copy-start(f32[1,3584]{1,0:T(1,128)} %param.19) | copy-start | bytes 43012
  7.2 5.6 %copy-start.18 = (s32[2,1,8,2]{2,3,1,0:T(2,128)S(1)}, s32[2,1,8,2]{2,3,1,0:T(2,128)}, u32[]{:S(2)}) copy-start(s32[2,1,8,2]{2,3,1,0:T(2,128)} %param.18) | copy-start | bytes 388
  7.2 6.5 %copy-start.19 = (s32[2,1,8,2]{2,3,1,0:T(2,128)S(1)}, s32[2,1,8,2]{2,3,1,0:T(2,128)}, u32[]{:S(2)}) copy-start(s32[2,1,8,2]{2,3,1,0:T(2,128)} %param.17) | copy-start | bytes 388
  7.2 7.1 %copy-start.13 = (bf16[1,8,3584]{2,1,0:T(8,128)(2,1)S(1)}, bf16[1,8,3584]{2,1,0:T(8,128)(2,1)}, u32[]{:S(2)}) copy-start(bf16[1,8,3584]{2,1,0:T(8,128)(2,1)} %param.16) | copy-start | bytes 172036
  7.2 93.0 %all-gather.2.cloned.1.call-start = ((), (), s32[]{:S(2)}) async-start(), calls=%async_computation.4 | async-start | bytes 1949696 | tf_op jit(solution)/shard_map/all_gather | solution.py:356
  8.6 7.8 %copy-start.10 = (bf16[1,3584,128]{2,1,0:T(8,128)(2,1)S(1)}, bf16[1,3584,128]{2,1,0:T(8,128)(2,1)}, u32[]{:S(2)}) copy-start(bf16[1,3584,128]{2,1,0:T(8,128)(2,1)} %param.22) | copy-start | bytes 2752516
  8.6 15.8 %collective-permute-start = (bf16[1792,128]{1,0:T(8,128)(2,1)S(1)}, bf16[1792,128]{1,0:T(8,128)(2,1)S(1)}, u32[]{:S(2)}, u32[]{:S(2)}) collective-permute-start(bf16[1792,128]{1,0:T(8,128)(2,1)S(1)} %get-tuple-element.83), channel_id=1, source_target_pairs={{0,1},{1,0},{2,3},{3,2},{4,5},{5,4},{6,7},{7,6},{8,9},{9,8},{10,11... | collective-permute-start | bytes 1376264 | tf_op jit(solution)/shard_map/ppermute | solution.py:310
  24.4 3.2 %copy-start.15 = (bf16[1792,128]{1,0:T(8,128)(2,1)}, bf16[1792,128]{1,0:T(8,128)(2,1)S(1)}, u32[]{:S(2)}) copy-start(bf16[1792,128]{1,0:T(8,128)(2,1)S(1)} %collective-permute-done) | copy-start | bytes 1376260
  24.4 38.5 %collective-permute-start.1 = (bf16[5376,128]{1,0:T(8,128)(2,1)}, bf16[5376,128]{1,0:T(8,128)(2,1)S(1)}, u32[]{:S(2)}, u32[]{:S(2)}) collective-permute-start(bf16[5376,128]{1,0:T(8,128)(2,1)} %pad_maximum_fusion.2), channel_id=1, source_target_pairs={{0,1},{1,0},{2,3},{3,2},{4,5},{5,4},{6,7},{7,6},{8,9},{9,8},{10,11... | collective-permute-start | bytes 4128776 | tf_op jit(solution)/shard_map/ppermute | solution.py:312
  27.5 35.4 %all-to-all-start = ((bf16[4,16,2304]{2,1,0:T(8,128)(2,1)}), bf16[4,16,2304]{2,1,0:T(8,128)(2,1)S(1)}, u32[]{:S(2)}, u32[]{:S(2)}) async-start(bf16[4,16,2304]{2,1,0:T(8,128)(2,1)} %pad_maximum_fusion.3), calls=%async_computation | async-start | bytes 589824 | tf_op jit(solution)/shard_map/all_to_all | solution.py:275
  40.8 33.7 %copy-start.9 = (bf16[1,3584,128]{2,1,0:T(8,128)(2,1)S(1)}, bf16[1,3584,128]{2,1,0:T(8,128)(2,1)}, u32[]{:S(2)}) copy-start(bf16[1,3584,128]{2,1,0:T(8,128)(2,1)} %param.21) | copy-start | bytes 2752516
  62.9 11.7 %copy-start.16 = (bf16[1792,128]{1,0:T(8,128)(2,1)S(1)}, bf16[1792,128]{1,0:T(8,128)(2,1)}, u32[]{:S(2)}) copy-start(bf16[1792,128]{1,0:T(8,128)(2,1)} %copy-done.15) | copy-start | bytes 1376260
  62.9 13.3 %collective-permute-start.2 = (bf16[4,8,2304]{2,1,0:T(8,128)(2,1)S(1)}, bf16[4,8,2304]{2,1,0:T(8,128)(2,1)S(1)}, u32[]{:S(2)}, u32[]{:S(2)}) collective-permute-start(bf16[4,8,2304]{2,1,0:T(8,128)(2,1)S(1)} %get-tuple-element.94), channel_id=1, source_target_pairs={{0,4},{1,5},{2,6},{3,7},{4,0},{5,1},{6,2},{7,3},{8,12},{9,13},{10,... | collective-permute-start | bytes 442376 | tf_op jit(solution)/shard_map/ppermute | solution.py:283
  65.0 24.2 %collective-permute-start.4 = (bf16[128,3584]{1,0:T(8,128)(2,1)}, bf16[128,3584]{1,0:T(8,128)(2,1)S(1)}, u32[]{:S(2)}, u32[]{:S(2)}) collective-permute-start(bf16[128,3584]{1,0:T(8,128)(2,1)} %bitcast.282), channel_id=1, source_target_pairs={{0,1},{1,0},{2,3},{3,2},{4,5},{5,4},{6,7},{7,6},{8,9},{9,8},{10,11... | collective-permute-start | bytes 2752520 | tf_op jit(solution)/shard_map/ppermute | solution.py:313
  69.6 12.7 %collective-permute-start.7 = (bf16[4,8,2304]{2,1,0:T(8,128)(2,1)S(1)}, bf16[4,8,2304]{2,1,0:T(8,128)(2,1)S(1)}, u32[]{:S(2)}, u32[]{:S(2)}) collective-permute-start(bf16[4,8,2304]{2,1,0:T(8,128)(2,1)S(1)} %get-tuple-element.95), channel_id=1, source_target_pairs={{0,4},{1,5},{2,6},{3,7},{4,0},{5,1},{6,2},{7,3},{8,12},{9,13},{10,... | collective-permute-start | bytes 442376 | tf_op jit(solution)/shard_map/ppermute | solution.py:283
  76.2 16.1 %copy-start.1 = (bf16[3584,256]{1,0:T(8,128)(2,1)}, bf16[3584,256]{1,0:T(8,128)(2,1)S(1)}, u32[]{:S(2)}) copy-start(bf16[3584,256]{1,0:T(8,128)(2,1)S(1)} %get-tuple-element.157.up_ref) | copy-start | bytes 5505028
  76.2 13.0 %copy-start.12 = (bf16[1,128,3584]{2,1,0:T(8,128)(2,1)S(1)}, bf16[1,128,3584]{2,1,0:T(8,128)(2,1)}, u32[]{:S(2)}) copy-start(bf16[1,128,3584]{2,1,0:T(8,128)(2,1)} %param.23) | copy-start | bytes 2752516
  76.3 16.0 %collective-permute-start.3 = (bf16[8,8,2304]{2,1,0:T(8,128)(2,1)S(1)}, bf16[8,8,2304]{2,1,0:T(8,128)(2,1)S(1)}, u32[]{:S(2)}, u32[]{:S(2)}) collective-permute-start(bf16[8,8,2304]{2,1,0:T(8,128)(2,1)S(1)} %get-tuple-element.92), channel_id=1, source_target_pairs={{0,2},{1,3},{2,0},{3,1},{4,6},{5,7},{6,4},{7,5},{8,10},{9,11},{10,... | collective-permute-start | bytes 884744 | tf_op jit(solution)/shard_map/ppermute | solution.py:283
  83.0 22.4 %collective-permute-start.8 = (bf16[8,8,2304]{2,1,0:T(8,128)(2,1)}, bf16[8,8,2304]{2,1,0:T(8,128)(2,1)S(1)}, u32[]{:S(2)}, u32[]{:S(2)}) collective-permute-start(bf16[8,8,2304]{2,1,0:T(8,128)(2,1)} %get-tuple-element.96), channel_id=1, source_target_pairs={{0,2},{1,3},{2,0},{3,1},{4,6},{5,7},{6,4},{7,5},{8,10},{9,11},{10,... | collective-permute-start | bytes 884744 | tf_op jit(solution)/shard_map/ppermute | solution.py:283
  93.8 1.3 copy-start.4
  100.2 14.9 %collective-permute-start.5 = (bf16[8,8,2304]{2,1,0:T(8,128)(2,1)S(1)}, bf16[8,8,2304]{2,1,0:T(8,128)(2,1)}, u32[]{:S(2)}, u32[]{:S(2)}) collective-permute-start(bf16[8,8,2304]{2,1,0:T(8,128)(2,1)S(1)} %bitcast.275), channel_id=1, source_target_pairs={{0,2},{1,3},{2,0},{3,1},{4,6},{5,7},{6,4},{7,5},{8,10},{9,11},{10,... | collective-permute-start | bytes 884744 | tf_op jit(solution)/shard_map/ppermute | solution.py:283
  105.4 1.5 copy-start.2
  106.9 1.5 copy-start.5
  108.4 1.5 copy-start.7
  113.2 10.2 %collective-permute-start.9 = (bf16[8,8,2304]{2,1,0:T(8,128)(2,1)S(1)}, bf16[8,8,2304]{2,1,0:T(8,128)(2,1)S(1)}, u32[]{:S(2)}, u32[]{:S(2)}) collective-permute-start(bf16[8,8,2304]{2,1,0:T(8,128)(2,1)S(1)} %bitcast.278), channel_id=1, source_target_pairs={{0,2},{1,3},{2,0},{3,1},{4,6},{5,7},{6,4},{7,5},{8,10},{9,11},{10,... | collective-permute-start | bytes 884744 | tf_op jit(solution)/shard_map/ppermute | solution.py:283
  116.2 11.5 %collective-permute-start.6 = (bf16[4,8,2304]{2,1,0:T(8,128)(2,1)S(1)}, bf16[4,8,2304]{2,1,0:T(8,128)(2,1)S(1)}, u32[]{:S(2)}, u32[]{:S(2)}) collective-permute-start(bf16[4,8,2304]{2,1,0:T(8,128)(2,1)S(1)} %slice.578), channel_id=1, source_target_pairs={{0,4},{1,5},{2,6},{3,7},{4,0},{5,1},{6,2},{7,3},{8,12},{9,13},{10,... | collective-permute-start | bytes 442376 | tf_op jit(solution)/shard_map/ppermute | solution.py:283
  123.5 8.0 %collective-permute-start.10 = (bf16[4,8,2304]{2,1,0:T(8,128)(2,1)S(1)}, bf16[4,8,2304]{2,1,0:T(8,128)(2,1)S(1)}, u32[]{:S(2)}, u32[]{:S(2)}) collective-permute-start(bf16[4,8,2304]{2,1,0:T(8,128)(2,1)S(1)} %slice.580), channel_id=1, source_target_pairs={{0,4},{1,5},{2,6},{3,7},{4,0},{5,1},{6,2},{7,3},{8,12},{9,13},{10,... | collective-permute-start | bytes 442376 | tf_op jit(solution)/shard_map/ppermute | solution.py:283
  132.3 24.4 %all-to-all-start.1 = ((bf16[4,16,2304]{2,1,0:T(8,128)(2,1)}), bf16[4,16,2304]{2,1,0:T(8,128)(2,1)S(1)}, u32[]{:S(2)}, u32[]{:S(2)}) async-start(bf16[4,16,2304]{2,1,0:T(8,128)(2,1)} %pad_maximum_fusion.6), calls=%async_computation.1 | async-start | bytes 589824 | tf_op jit(solution)/shard_map/all_to_all | solution.py:275
  158.6 5.6 %collective-permute-start.11 = (bf16[8,3584]{1,0:T(8,128)(2,1)S(1)}, bf16[8,3584]{1,0:T(8,128)(2,1)S(1)}, u32[]{:S(2)}, u32[]{:S(2)}) collective-permute-start(bf16[8,3584]{1,0:T(8,128)(2,1)S(1)} %fusion.49), channel_id=1, source_target_pairs={{480,0},{0,32},{32,64},{64,96},{96,128},{128,160},{160,192},{192,2... | collective-permute-start | bytes 172040 | tf_op jit(solution)/shard_map/ppermute | solution.py:16
  160.6 5.4 %collective-permute-start.12 = (bf16[8,3584]{1,0:T(8,128)(2,1)S(1)}, bf16[8,3584]{1,0:T(8,128)(2,1)S(1)}, u32[]{:S(2)}, u32[]{:S(2)}) collective-permute-start(bf16[8,3584]{1,0:T(8,128)(2,1)S(1)} %fusion.42), channel_id=1, source_target_pairs={{32,0},{64,32},{96,64},{128,96},{160,128},{192,160},{224,192},{256... | collective-permute-start | bytes 172040 | tf_op jit(solution)/shard_map/ppermute | solution.py:16
  166.2 50.1 %copy-start.6 = (bf16[256,3584]{1,0:T(8,128)(2,1)S(1)}, bf16[256,3584]{1,0:T(8,128)(2,1)}, u32[]{:S(2)}) copy-start(bf16[256,3584]{1,0:T(8,128)(2,1)} %copy-done.4) | copy-start | bytes 5505028
  166.2 50.1 %copy-start.3 = (bf16[3584,256]{1,0:T(8,128)(2,1)S(1)}, bf16[3584,256]{1,0:T(8,128)(2,1)}, u32[]{:S(2)}) copy-start(bf16[3584,256]{1,0:T(8,128)(2,1)} %copy-done.1) | copy-start | bytes 5505028
  189.6 9.2 %collective-permute-start.13 = (bf16[4,8,2304]{2,1,0:T(8,128)(2,1)S(1)}, bf16[4,8,2304]{2,1,0:T(8,128)(2,1)S(1)}, u32[]{:S(2)}, u32[]{:S(2)}) collective-permute-start(bf16[4,8,2304]{2,1,0:T(8,128)(2,1)S(1)} %get-tuple-element.88), channel_id=1, source_target_pairs={{0,4},{1,5},{2,6},{3,7},{4,0},{5,1},{6,2},{7,3},{8,12},{9,13},{10,... | collective-permute-start | bytes 442376 | tf_op jit(solution)/shard_map/ppermute | solution.py:283
  198.8 17.5 %collective-permute-start.14 = (bf16[8,8,2304]{2,1,0:T(8,128)(2,1)S(1)}, bf16[8,8,2304]{2,1,0:T(8,128)(2,1)S(1)}, u32[]{:S(2)}, u32[]{:S(2)}) collective-permute-start(bf16[8,8,2304]{2,1,0:T(8,128)(2,1)S(1)} %get-tuple-element.87), channel_id=1, source_target_pairs={{0,2},{1,3},{2,0},{3,1},{4,6},{5,7},{6,4},{7,5},{8,10},{9,11},{10,... | collective-permute-start | bytes 884744 | tf_op jit(solution)/shard_map/ppermute | solution.py:283
  203.2 11.1 %collective-permute-start.17 = (bf16[4,8,2304]{2,1,0:T(8,128)(2,1)S(1)}, bf16[4,8,2304]{2,1,0:T(8,128)(2,1)S(1)}, u32[]{:S(2)}, u32[]{:S(2)}) collective-permute-start(bf16[4,8,2304]{2,1,0:T(8,128)(2,1)S(1)} %get-tuple-element.55), channel_id=1, source_target_pairs={{0,4},{1,5},{2,6},{3,7},{4,0},{5,1},{6,2},{7,3},{8,12},{9,13},{10,... | collective-permute-start | bytes 442376 | tf_op jit(solution)/shard_map/ppermute | solution.py:283
  214.4 11.8 %collective-permute-start.18 = (bf16[8,8,2304]{2,1,0:T(8,128)(2,1)S(1)}, bf16[8,8,2304]{2,1,0:T(8,128)(2,1)S(1)}, u32[]{:S(2)}, u32[]{:S(2)}) collective-permute-start(bf16[8,8,2304]{2,1,0:T(8,128)(2,1)S(1)} %constant_dynamic-update-slice_fusion.42), channel_id=1, source_target_pairs={{0,2},{1,3},{2,0},{3,1},{4,6},{5,7},{6,4},{7,5},{8,10},{9,11},{10,... | collective-permute-start | bytes 884744 | tf_op jit(solution)/shard_map/ppermute | solution.py:283
  216.4 9.9 %copy-start.8 = (bf16[256,3584]{1,0:T(8,128)(2,1)S(1)}, bf16[256,3584]{1,0:T(8,128)(2,1)}, u32[]{:S(2)}) copy-start(bf16[256,3584]{1,0:T(8,128)(2,1)} %all-gather.2.cloned.1.call-done.saved_ref) | copy-start | bytes 5505028
  217.9 13.5 %collective-permute-start.15 = (bf16[8,8,2304]{2,1,0:T(8,128)(2,1)S(1)}, bf16[8,8,2304]{2,1,0:T(8,128)(2,1)S(1)}, u32[]{:S(2)}, u32[]{:S(2)}) collective-permute-start(bf16[8,8,2304]{2,1,0:T(8,128)(2,1)S(1)} %bitcast.277), channel_id=1, source_target_pairs={{0,2},{1,3},{2,0},{3,1},{4,6},{5,7},{6,4},{7,5},{8,10},{9,11},{10,... | collective-permute-start | bytes 884744 | tf_op jit(solution)/shard_map/ppermute | solution.py:283
  229.5 10.2 %collective-permute-start.19 = (bf16[8,8,2304]{2,1,0:T(8,128)(2,1)S(1)}, bf16[8,8,2304]{2,1,0:T(8,128)(2,1)S(1)}, u32[]{:S(2)}, u32[]{:S(2)}) collective-permute-start(bf16[8,8,2304]{2,1,0:T(8,128)(2,1)S(1)} %bitcast.276), channel_id=1, source_target_pairs={{0,2},{1,3},{2,0},{3,1},{4,6},{5,7},{6,4},{7,5},{8,10},{9,11},{10,... | collective-permute-start | bytes 884744 | tf_op jit(solution)/shard_map/ppermute | solution.py:283
  231.5 13.1 %collective-permute-start.16 = (bf16[4,8,2304]{2,1,0:T(8,128)(2,1)S(1)}, bf16[4,8,2304]{2,1,0:T(8,128)(2,1)S(1)}, u32[]{:S(2)}, u32[]{:S(2)}) collective-permute-start(bf16[4,8,2304]{2,1,0:T(8,128)(2,1)S(1)} %slice.632), channel_id=1, source_target_pairs={{0,4},{1,5},{2,6},{3,7},{4,0},{5,1},{6,2},{7,3},{8,12},{9,13},{10,... | collective-permute-start | bytes 442376 | tf_op jit(solution)/shard_map/ppermute | solution.py:283
  239.8 8.8 %collective-permute-start.20 = (bf16[4,8,2304]{2,1,0:T(8,128)(2,1)S(1)}, bf16[4,8,2304]{2,1,0:T(8,128)(2,1)S(1)}, u32[]{:S(2)}, u32[]{:S(2)}) collective-permute-start(bf16[4,8,2304]{2,1,0:T(8,128)(2,1)S(1)} %slice.635), channel_id=1, source_target_pairs={{0,4},{1,5},{2,6},{3,7},{4,0},{5,1},{6,2},{7,3},{8,12},{9,13},{10,... | collective-permute-start | bytes 442376 | tf_op jit(solution)/shard_map/ppermute | solution.py:283
  249.4 22.4 %all-to-all-start.3 = ((bf16[4,16,2304]{2,1,0:T(8,128)(2,1)}), bf16[4,16,2304]{2,1,0:T(8,128)(2,1)S(1)}, u32[]{:S(2)}, u32[]{:S(2)}) async-start(bf16[4,16,2304]{2,1,0:T(8,128)(2,1)} %pad_maximum_fusion.9), calls=%async_computation.3 | async-start | bytes 589824 | tf_op jit(solution)/shard_map/all_to_all | solution.py:275
Sparse Core Ops, SparseCore 0:
  12.5 87.6 all-gather.1
